TPU v7x, 256 devices: a whole 4x4x8 slice. The times are simulated.
256 devices in a mesh: row: 32 (over z, x_hi, core), col: 8 (over y, x_lo).
Axes of the slice: x: 4 (x_hi: 2, x_lo: 2; x = x_hi * 2 + x_lo), y: 4, z: 8, core: 2. Of those that a mesh axis runs over, the one named last changes fastest.
Arguments:
- queries: bfloat16 [32768, 256], P(('row', 'col')), may hold values from -128 to 128
- key_states: bfloat16 [32768, 128], P(('col', 'row')), may hold values from -8 to 8
- value_states: bfloat16 [32768, 128], P(('col', 'row')), may hold values from -6 to 6
- grad_output: bfloat16 [32768, 256], P(('row', 'col')), may hold values from -6 to 6
- block_ids: int32 [16384], replicated, may hold values from 0 to 31, never falling along the last dimension, each value on 1 to 1024 neighbouring positions
Outputs:
- grad_queries: bfloat16 [32768, 256], P(('row', 'col'))
- grad_keys: bfloat16 [32768, 128], P(('col', 'row'))
- grad_values: bfloat16 [32768, 128], P(('col', 'row'))
Inputs may be any that keep to these rules, and one draw needn't show every extreme that they name: `block_ids`: block numbers never fall along the clean sequence; every block from 0 to 31 holds 1 to 1024 tokens and some block holds exactly 1024. The noisy copy's token 16384 + i has the block of clean token i.
All inputs are finite; a program needn't handle non-finite values.
Results may differ from a plain program's by a relative error of at most 0.0051.
Values may be sent and summed in bfloat16 or wider, within the bound.
No kernel may reach another device: no remote copies, remote signals or barrier semaphores. Data moves between devices by JAX's collectives and lax.ppermute only.
A program may use at most 64 MiB of HBM per device.

v0:
```python
import math

import jax
import jax.numpy as jnp
from jax import lax
from jax.sharding import PartitionSpec as P

masked_score = -1e30
large_block = 1 << 30
score_entries = 1 << 19


def allowed(query_block, query_noisy, key_block, key_noisy):
    clean_key = jnp.logical_not(key_noisy)
    earlier = key_block < query_block
    same_block = key_block == query_block
    from_clean = clean_key & (earlier | same_block & jnp.logical_not(query_noisy))
    from_noisy = key_noisy & query_noisy & same_block
    return from_clean | from_noisy


def live_pair(query_block, query_noisy, key_block, key_noisy):
    clean_query_top = jnp.max(jnp.where(query_noisy, -1, query_block))
    noisy_query_top = jnp.max(jnp.where(query_noisy, query_block, -1))
    noisy_query_low = jnp.min(jnp.where(query_noisy, query_block, large_block))
    clean_key_low = jnp.min(jnp.where(key_noisy, large_block, key_block))
    noisy_key_low = jnp.min(jnp.where(key_noisy, key_block, large_block))
    noisy_key_top = jnp.max(jnp.where(key_noisy, key_block, -1))
    return (
        (clean_key_low <= clean_query_top)
        | (clean_key_low < noisy_query_top)
        | (noisy_key_low <= noisy_query_top) & (noisy_query_low <= noisy_key_top)
    )


def piece_length(set_width, query_heads):
    rows_heads = query_heads.shape[0] * query_heads.shape[1]
    return math.gcd(set_width, max(8, score_entries // rows_heads))


def key_piece_of(key_set, step_index, step_len):
    pair_keys, key_block, key_noisy = key_set
    offset = step_index * step_len
    key_piece = lax.dynamic_slice_in_dim(pair_keys, offset, step_len, 1)
    piece_block = lax.dynamic_slice_in_dim(key_block, offset, step_len, 0)
    piece_noisy = lax.dynamic_slice_in_dim(key_noisy, offset, step_len, 0)
    return (offset, key_piece, piece_block, piece_noisy)


def stats_pass(query_heads, grad_heads, query_block, query_noisy, key_set, score_scale, running):
    set_width = key_set[0].shape[1]
    step_len = piece_length(set_width, query_heads)

    def stats_visit(step_index, state):
        offset, key_piece, piece_block, piece_noisy = key_piece_of(key_set, step_index, step_len)

        def stats_compute(state_in):
            run_max, run_sum, run_dot = state_in
            scores = (
                jnp.einsum(
                    "ihd,jd->ihj", query_heads, key_piece[0], preferred_element_type=jnp.float32
                )
                * score_scale
            )
            visible = allowed(
                query_block[:, None, None],
                query_noisy[:, None, None],
                piece_block[None, None, :],
                piece_noisy[None, None, :],
            )
            scores = jnp.where(visible, scores, masked_score)
            new_max = jnp.maximum(run_max, jnp.max(scores, axis=2))
            weights = jnp.where(visible, jnp.exp(scores - new_max[:, :, None]), 0.0)
            grad_probs = jnp.einsum(
                "ihd,jd->ihj", grad_heads, key_piece[1], preferred_element_type=jnp.float32
            )
            factor = jnp.exp(run_max - new_max)
            return (
                new_max,
                run_sum * factor + jnp.sum(weights, axis=2),
                run_dot * factor + jnp.sum(weights * grad_probs, axis=2),
            )

        def stats_unchanged(state_in):
            return state_in

        return lax.cond(
            live_pair(query_block, query_noisy, piece_block, piece_noisy),
            stats_compute,
            stats_unchanged,
            state,
        )

    return lax.fori_loop(0, set_width // step_len, stats_visit, running)


def grad_pass(
    query_heads,
    grad_heads,
    query_block,
    query_noisy,
    key_set,
    score_scale,
    row_max,
    row_sum,
    row_delta,
    grad_rows,
):
    set_width = key_set[0].shape[1]
    head_dim = key_set[0].shape[2]
    step_len = piece_length(set_width, query_heads)
    grad_pair = jnp.zeros((2, set_width, head_dim), jnp.float32)

    def grad_visit(step_index, state):
        offset, key_piece, piece_block, piece_noisy = key_piece_of(key_set, step_index, step_len)

        def grad_compute(state_in):
            rows_in, pair_in = state_in
            scores = (
                jnp.einsum(
                    "ihd,jd->ihj", query_heads, key_piece[0], preferred_element_type=jnp.float32
                )
                * score_scale
            )
            visible = allowed(
                query_block[:, None, None],
                query_noisy[:, None, None],
                piece_block[None, None, :],
                piece_noisy[None, None, :],
            )
            attn_probs = jnp.where(
                visible, jnp.exp(scores - row_max[:, :, None]) / row_sum[:, :, None], 0.0
            )
            grad_probs = jnp.einsum(
                "ihd,jd->ihj", grad_heads, key_piece[1], preferred_element_type=jnp.float32
            )
            grad_scores = attn_probs * (grad_probs - row_delta[:, :, None])
            probs_low = attn_probs.astype(jnp.bfloat16)
            scaled_low = (grad_scores * score_scale).astype(jnp.bfloat16)
            value_part = jnp.einsum(
                "ihj,ihd->jd", probs_low, grad_heads, preferred_element_type=jnp.float32
            )
            key_part = jnp.einsum(
                "ihj,ihd->jd", scaled_low, query_heads, preferred_element_type=jnp.float32
            )
            rows_out = rows_in + jnp.einsum(
                "ihj,jd->ihd", scaled_low, key_piece[0], preferred_element_type=jnp.float32
            )
            pair_out = lax.dynamic_update_slice_in_dim(
                pair_in, jnp.stack([key_part, value_part]), offset, 1
            )
            return (rows_out, pair_out)

        def grad_unchanged(state_in):
            return state_in

        return lax.cond(
            live_pair(query_block, query_noisy, piece_block, piece_noisy),
            grad_compute,
            grad_unchanged,
            state,
        )

    return lax.fori_loop(0, set_width // step_len, grad_visit, (grad_rows, grad_pair))


def per_device(queries, key_states, value_states, grad_output, block_ids):
    col_count = lax.axis_size("col")
    row_count = lax.axis_size("row")
    shard_len = key_states.shape[0]
    head_dim = key_states.shape[1]
    head_count = queries.shape[1] // head_dim
    half_len = block_ids.shape[0]
    score_scale = 1.0 / math.sqrt(head_dim)
    block_twice = jnp.concatenate([block_ids, block_ids])
    pair_local = jnp.stack([key_states, value_states])
    col_index = lax.axis_index("col")
    row_index = lax.axis_index("row")
    query_all, grad_all = (
        lax.all_gather(queries, "col", axis=0, tiled=True),
        lax.all_gather(grad_output, "col", axis=0, tiled=True),
    )
    query_len = shard_len * col_count
    query_start = row_index * query_len
    query_pos = query_start + jnp.arange(query_len, dtype=jnp.int32)
    query_block = lax.dynamic_slice_in_dim(block_twice, query_start, query_len, 0)
    pair_all = lax.all_gather(pair_local, "row", axis=1, tiled=True)
    key_len = shard_len * row_count
    key_start = col_index * key_len
    key_pos = key_start + jnp.arange(key_len, dtype=jnp.int32)
    key_sets = (
        pair_all,
        lax.dynamic_slice_in_dim(block_twice, key_start, key_len, 0),
        key_pos >= half_len,
    )
    query_noisy = query_pos >= half_len
    query_heads = query_all.reshape(query_len, head_count, head_dim)
    grad_heads = grad_all.reshape(query_len, head_count, head_dim)
    stat_shape = (query_len, head_count)
    running = (
        jnp.full(stat_shape, masked_score, jnp.float32),
        jnp.zeros(stat_shape, jnp.float32),
        jnp.zeros(stat_shape, jnp.float32),
    )
    running = stats_pass(
        query_heads, grad_heads, query_block, query_noisy, key_sets, score_scale, running
    )
    run_max, run_sum, run_dot = running
    row_max = lax.pmax(run_max, "col")
    factor = jnp.exp(run_max - row_max)
    row_sum, row_dot = lax.psum((run_sum * factor, run_dot * factor), "col")
    row_delta = row_dot / row_sum
    grad_rows = jnp.zeros((query_len, head_count, head_dim), jnp.float32)
    grad_rows, grad_pair = grad_pass(
        query_heads,
        grad_heads,
        query_block,
        query_noisy,
        key_sets,
        score_scale,
        row_max,
        row_sum,
        row_delta,
        grad_rows,
    )
    grad_flat = grad_rows.reshape(query_len, head_count * head_dim)
    grad_query = lax.psum_scatter(grad_flat, "col", scatter_dimension=0, tiled=True).astype(
        jnp.bfloat16
    )
    final_pair = lax.psum_scatter(grad_pair, "row", scatter_dimension=1, tiled=True).astype(
        jnp.bfloat16
    )
    return (grad_query, final_pair[0], final_pair[1])


def solution(mesh):
    return jax.shard_map(
        per_device,
        mesh=mesh,
        in_specs=(
            P(("row", "col"), None),
            P(("col", "row"), None),
            P(("col", "row"), None),
            P(("row", "col"), None),
            P(),
        ),
        out_specs=(P(("row", "col"), None), P(("col", "row"), None), P(("col", "row"), None)),
        check_vma=False,
    )
```

profile of v0, /device:TPU:8, one launch (start us, length us, event | category | flops | bytes accessed | tf_op | source)
XLA Modules:
  0.0 709.4 jit_solution(2843051180290244146)
XLA Ops:
  7.2 1.4 pad_maximum_fusion
  8.7 1.0 copy.11
  9.7 1.0 copy.12
  10.6 0.9 constant_dynamic-update-slice_fusion.1
  11.5 0.8 constant_dynamic-update-slice_fusion
  12.3 28.1 %all_gather.11 = bf16[1024,256]{0,1:T(8,128)(2,1)S(1)} all-gather(bf16[128,256]{0,1:T(8,128)(2,1)S(1)} %copy.12), channel_id=1, replica_groups=mesh['row'=32,'col'=8] {'col'}, dimensions={0}, use_global_device_ids=true | all-gather | bytes 589824 | tf_op jit(solution)/shard_map/all_gather | solution.py:181
  40.7 27.4 %all_gather.10 = bf16[1024,256]{0,1:T(8,128)(2,1)S(1)} all-gather(bf16[128,256]{0,1:T(8,128)(2,1)S(1)} %copy.11), channel_id=1, replica_groups=mesh['row'=32,'col'=8] {'col'}, dimensions={0}, use_global_device_ids=true | all-gather | bytes 589824 | tf_op jit(solution)/shard_map/all_gather | solution.py:180
  68.4 26.7 %all-gather.2.cloned.1.call-done = bf16[2,4096,128]{2,1,0:T(8,128)(2,1)} async-done(((bf16[2,128,128]{2,1,0:T(8,128)(2,1)}), bf16[2,4096,128]{2,1,0:T(8,128)(2,1)}) %all-gather.2.cloned.1.call-update) | async-done | bytes 2097168 | tf_op jit(solution)/shard_map/all_gather | solution.py:187
  95.1 105.9 %while.34 = (s32[]{:T(128)}, f32[1024,2]{0,1:T(2,128)S(1)}, f32[1024,2]{0,1:T(2,128)S(1)}, f32[1024,2]{0,1:T(2,128)S(1)}, pred[4096]{0:T(1024)(128)(4,1)S(1)}, /...) while((s32[]{:T(128)}, f32[1024,2]{0,1:T(2,128)S(1)}, ...), condition=%wide.region_12.13_spmd.clone, body=%wide.region_0.12_spmd.clone.sunk | while | flops 277891840 | bytes 8686513 | solution.py:94
  95.8 0.8 select_reduce_fusion.16
  102.5 0.8 select_reduce_fusion.16
  109.1 0.8 select_reduce_fusion.16
  115.7 0.8 select_reduce_fusion.16
  122.3 0.8 select_reduce_fusion.16
  128.9 0.8 select_reduce_fusion.16
  135.5 0.8 select_reduce_fusion.16
  142.2 0.8 select_reduce_fusion.16
  148.8 0.8 select_reduce_fusion.16
  155.4 0.8 select_reduce_fusion.16
  162.0 0.8 select_reduce_fusion.16
  168.6 0.8 select_reduce_fusion.16
  175.2 0.8 select_reduce_fusion.16
  181.9 0.8 select_reduce_fusion.16
  188.5 0.8 select_reduce_fusion.16
  195.1 0.8 select_reduce_fusion.16
  201.0 44.8 %pmax.7 = f32[1024,2]{0,1:T(2,128)S(1)} all-reduce(f32[1024,2]{0,1:T(2,128)S(1)} %get-tuple-element.558), channel_id=1, replica_groups=mesh['row'=32,'col'=8] {'col'}, use_global_device_ids=true, to_apply=%region_13.14 | all-reduce | flops 2048 | bytes 16384 | tf_op jit(solution)/shard_map/pmax | solution.py:209
  245.8 32.7 %all-reduce = (f32[1024,2]{0,1:T(2,128)S(1)}, f32[1024,2]{0,1:T(2,128)S(1)}) all-reduce(f32[1024,2]{0,1:T(2,128)S(1)} %get-tuple-element.719, f32[1024,2]{0,1:T(2,128)S(1)} %get-tuple-element.718), channel_id=1, replica_groups=mesh['row'=32,'col'=8] {'col'}, use_global_device_ids=true, to_apply=%region_14.15 | all-reduce | flops 4096 | bytes 32768 | tf_op jit(solution)/shard_map/psum | solution.py:211
  278.6 2.2 broadcast_in_dim.117
  280.8 106.0 %while.35 = (s32[]{:T(128)}, f32[1024,2,128]{2,0,1:T(8,128)S(1)}, f32[2,4096,128]{2,1,0:T(8,128)}, pred[4096]{0:T(1024)(128)(4,1)S(1)}, s32[4096]{0:T(1024)S(1)}...) while((s32[]{:T(128)}, f32[1024,2,128]{2,0,1:T(8,128)S(1)}, ...), condition=%wide.region_25.26_spmd.clone, body=%wide.region_16.25_spmd.clone.sunk | while | flops 678245120 | bytes 15183343 | solution.py:164
  281.5 0.8 select_reduce_fusion.18
  287.4 0.7 select_reduce_fusion.19
  288.2 0.8 select_reduce_fusion.18
  294.1 0.7 select_reduce_fusion.19
  294.8 0.8 select_reduce_fusion.18
  300.7 0.7 select_reduce_fusion.19
  301.4 0.8 select_reduce_fusion.18
  307.3 0.7 select_reduce_fusion.19
  308.1 0.8 select_reduce_fusion.18
  314.0 0.7 select_reduce_fusion.19
  314.7 0.8 select_reduce_fusion.18
  320.6 0.7 select_reduce_fusion.19
  321.3 0.8 select_reduce_fusion.18
  327.2 0.7 select_reduce_fusion.19
  327.9 0.8 select_reduce_fusion.18
  333.8 0.7 select_reduce_fusion.19
  334.6 0.8 select_reduce_fusion.18
  340.5 0.7 select_reduce_fusion.19
  341.2 0.8 select_reduce_fusion.18
  347.1 0.7 select_reduce_fusion.19
  347.8 0.8 select_reduce_fusion.18
  353.7 0.7 select_reduce_fusion.19
  354.5 0.8 select_reduce_fusion.18
  360.3 0.7 select_reduce_fusion.19
  361.1 0.8 select_reduce_fusion.18
  367.0 0.7 select_reduce_fusion.19
  367.7 0.8 select_reduce_fusion.18
  373.6 0.7 select_reduce_fusion.19
  374.3 0.8 select_reduce_fusion.18
  381.0 0.8 select_reduce_fusion.18
  386.8 1.1 copy_bitcast_fusion
  388.7 179.6 %reduce-scatter.3.cloned.1.call-done = f32[128,256]{1,0:T(8,128)} async-done(((f32[1024,256]{1,0:T(8,128)}), f32[128,256]{1,0:T(8,128)}) %reduce-scatter.3.cloned.1.call-update) | async-done | bytes 131088 | tf_op jit(solution)/shard_map/reduce_scatter | solution.py:227
  568.2 1.5 convert_element_type.28
  569.8 131.5 %reduce-scatter.5.cloned.1.call-done = f32[2,128,128]{2,1,0:T(8,128)} async-done(((f32[2,4096,128]{2,1,0:T(8,128)}), f32[2,128,128]{2,1,0:T(8,128)}) %reduce-scatter.5.cloned.1.call-update) | async-done | bytes 131088 | tf_op jit(solution)/shard_map/reduce_scatter | solution.py:230
  701.3 0.9 convert_element_type.29
  (100 shorter events, 15.7 us)
Async XLA Ops:
  7.2 87.9 %all-gather.2.cloned.1.call-start = ((), (), s32[]{:S(2)}) async-start(), calls=%async_computation.2 | async-start | bytes 2162688 | tf_op jit(solution)/shard_map/all_gather | solution.py:187
  8.6 559.6 %reduce-scatter.3.cloned.1.call-start = ((), (), s32[]{:S(2)}) async-start(), calls=%async_computation.3 | async-start | bytes 1179648 | tf_op jit(solution)/shard_map/reduce_scatter | solution.py:227
  387.9 313.4 %reduce-scatter.5.cloned.1.call-start = ((), (), s32[]{:S(2)}) async-start(), calls=%async_computation.4 | async-start | bytes 4325376 | tf_op jit(solution)/shard_map/reduce_scatter | solution.py:230
Sparse Core Ops, SparseCore 0:
  11.4 83.6 all-gather.1
  388.0 180.1 reduce-scatter.2
  572.5 128.7 reduce-scatter.4
where the time goes:
time: 716 us; the launch traced here: 709 us
  waiting for transfers between devices  338 us (47%)
  loops' own time  164 us (23%)
  blocking collectives  133 us (19%)
  other arithmetic  52.2 us (7%)
  between operations  13.8 us (2%)
  local copies, waits for them, and re-layouts  8.12 us (1%)
    reduce_scatter x1, waiting for transfers between devices, per_device(): lax.psum_scatter(grad_flat, 'col', scatter_dimension=0, tiled=True)  180 us
    reduce_scatter x1, waiting for transfers between devices, per_device(): lax.psum_scatter(grad_pair, 'row', scatter_dimension=1, tiled=True)  132 us
    another operation x1, loops' own time, stats_pass(): return lax.fori_loop(0, set_width // step_len, stats_visit, running)  81.8 us
    another operation x1, loops' own time, grad_pass(): lax.fori_loop(0, set_width // step_len, grad_visit, (grad_rows, grad_pair))  81.5 us
    pmax x1, blocking collectives, per_device(): row_max = lax.pmax(run_max, 'col')  44.8 us
    psum x1, blocking collectives, per_device(): row_sum, row_dot = lax.psum((run_sum * factor, run_dot * factor), 'col')  32.7 us
    all_gather x1, blocking collectives, per_device(): lax.all_gather(grad_output, 'col', axis=0, tiled=True)  28.1 us
    all_gather x1, blocking collectives, per_device(): lax.all_gather(queries, 'col', axis=0, tiled=True)  27.4 us
  transfers between devices with their start and end apart: 3, of which 3 were waited for; matrix products, arithmetic and copies ran while one was open for 1% of the time, Pallas kernels for 0%

commit v1 on v0

v1 whole, which is shorter than its diff:
```python
import functools
import math

import jax
import jax.numpy as jnp
from jax import lax
from jax.experimental import pallas as pl
from jax.experimental.pallas import tpu as pltpu
from jax.sharding import Mesh
from jax.sharding import PartitionSpec as P

bf16 = jnp.bfloat16
f32 = jnp.float32
i32 = jnp.int32
NZ, NXH, NCORE, NY, NXL = 8, 2, 2, 4, 2
NX = NXH * NXL
CH = 128
HD = 128
RUN = NXH * NCORE * CH
NRUN = NY * NXL
HALF = NRUN // 2
LOW = -1e30
SCALE = 1.0 / math.sqrt(HD)
LOG2E = math.log2(math.e)
ROWS = ("z", "xh", "core")
COLS = ("y", "xl")
XAX = ("xh", "xl")


def shift(x, axis, size, by):
    return lax.ppermute(x, axis, [(i, (i + by) % size) for i in range(size)])


def nt(a, b):
    return lax.dot_general(a, b, (((1,), (1,)), ((), ())), preferred_element_type=f32)


def nn(a, b):
    return lax.dot_general(a, b, (((1,), (0,)), ((), ())), preferred_element_type=f32)


def load_all(ids, q_pieces, k_own, k_other, qs, kvs, sem):
    z, y, xh, xl, core = ids[0], ids[1], ids[2], ids[3], ids[4]
    copies = []
    for r, by in enumerate(Q_SHIFTS):
        copies.append((q_pieces[r], qs.at[(z - by) % NZ]))
    x = xh * NXL + xl
    for s in range(NY):
        for k in range(NX):
            px = (x - k) % NX
            py = (y - s) % NY
            slot = py * NXL + px % NXL
            for refs, pc in ((k_own, core), (k_other, 1 - core)):
                at = pl.multiple_of((px // NXL) * (NCORE * CH) + pc * CH, CH)
                copies.append((refs[s].at[k], kvs.at[slot, pl.ds(at, CH)]))
    copies = [pltpu.make_async_copy(a, b, sem.at[n]) for n, (a, b) in enumerate(copies)]
    for c in copies:
        c.start()
    for c in copies:
        c.wait()


Q_SHIFTS = (0, 1, -1, 2, -2, 3, -3, 4)
N_COPIES = NZ + NCORE * NY * NX


def key_columns(kid_ref, kcol):
    for b in range(HALF):
        row = kid_ref[b : b + 1, :]
        kcol[b] = jnp.broadcast_to(row, (CH, RUN)).T


def both_heads(qo, base):
    return jnp.concatenate([qo[:, base : base + HD], qo[:, base + HD : base + 2 * HD]], axis=0)


def mask_of(kcol_b, qrow, noisy_q, noisy_k):
    if noisy_k:
        seen = kcol_b == qrow
    else:
        seen = kcol_b <= jnp.where(noisy_q, qrow - 1, qrow)
    return jnp.concatenate([seen, seen], axis=1)


def for_live(mm, body):
    def clean(n, carry):
        j = n // HALF
        b = n % HALF
        a = j % HALF
        less = jnp.where(j >= HALF, 1, 0)
        live = mm[2, b] <= mm[1, a] - less
        full = mm[3, b] <= mm[0, a] - less

        @pl.when(live & full)
        def _():
            body(j, b, b, a, False, False)

        @pl.when(live & jnp.logical_not(full))
        def _():
            body(j, b, b, a, True, False)

        return carry

    def noisy(n, carry):
        a = n // HALF
        b = n % HALF
        live = (mm[2, b] <= mm[1, a]) & (mm[3, b] >= mm[0, a])

        @pl.when(live)
        def _():
            body(a + HALF, b + HALF, b, a, True, True)

        return carry

    lax.fori_loop(0, NZ * HALF, clean, 0)
    lax.fori_loop(0, HALF * HALF, noisy, 0)


def stats_kernel(ids, mm, qid_ref, kid_ref, *refs):
    q_pieces, k_own, k_other = refs[:NZ], refs[NZ : NZ + NY], refs[NZ + NY : NZ + 2 * NY]
    out_ref = refs[NZ + 2 * NY]
    qs, kvs, kcol, top, total, dot, sem = refs[NZ + 2 * NY + 1 :]
    load_all(ids, q_pieces, k_own, k_other, qs, kvs, sem)
    key_columns(kid_ref, kcol)
    top[...] = jnp.full(top.shape, LOW, f32)
    total[...] = jnp.zeros(total.shape, f32)
    dot[...] = jnp.zeros(dot.shape, f32)
    c = SCALE * LOG2E

    def body(j, slot, b, a, masked, noisy_k):
        qo = qs[j]
        kv = kvs[slot]
        s = nt(kv[:, :HD], both_heads(qo, 0)) * c
        dp = nt(kv[:, HD:], both_heads(qo, 2 * HD))
        if masked:
            seen = mask_of(kcol[b], qid_ref[pl.ds(a, 1)][0], j >= HALF, noisy_k)
            s = jnp.where(seen, s, LOW)
        old = top[j]
        new = jnp.maximum(old, jnp.max(s, axis=0, keepdims=True))
        p = jnp.exp2(s - new)
        if masked:
            p = jnp.where(seen, p, 0.0)
        f = jnp.exp2(old - new)
        top[j] = new
        total[j] = total[j] * f + jnp.sum(p, axis=0, keepdims=True)
        dot[j] = dot[j] * f + jnp.sum(p * dp, axis=0, keepdims=True)

    for_live(mm, body)
    t = total[...]
    some = t > 0.0
    safe = jnp.where(some, t, 1.0)
    out_ref[:, 0:1, :] = jnp.where(some, top[...] + jnp.log2(safe), LOW)
    out_ref[:, 1:2, :] = jnp.where(some, dot[...] / safe, 0.0)


def grad_kernel(ids, mm, qid_ref, kid_ref, st_ref, *refs):
    q_pieces, k_own, k_other = refs[:NZ], refs[NZ : NZ + NY], refs[NZ + NY : NZ + 2 * NY]
    dq_ref, own_ref, other_ref = refs[NZ + 2 * NY : NZ + 2 * NY + 3]
    qs, kvs, kcol, kts, lse, delta, dq_acc, dkv_acc, sem = refs[NZ + 2 * NY + 3 :]
    load_all(ids, q_pieces, k_own, k_other, qs, kvs, sem)
    key_columns(kid_ref, kcol)
    for b in range(NRUN):
        kts[b] = kvs[b][:, :HD].T
    parts = st_ref[:, :, 0:1, :]
    high = jnp.max(parts, axis=0)
    shares = jnp.exp2(parts - high[None])
    sums = jnp.sum(shares, axis=0)
    lse[...] = high + jnp.log2(sums)
    delta[...] = jnp.sum(shares * st_ref[:, :, 1:2, :], axis=0) / sums
    dq_acc[...] = jnp.zeros(dq_acc.shape, f32)
    dkv_acc[...] = jnp.zeros(dkv_acc.shape, f32)
    c = SCALE * LOG2E

    def body(j, slot, b, a, masked, noisy_k):
        qo = qs[j]
        kv = kvs[slot]
        q2 = both_heads(qo, 0)
        o2 = both_heads(qo, 2 * HD)
        s = nt(kv[:, :HD], q2) * c
        dp = nt(kv[:, HD:], o2)
        p = jnp.exp2(s - lse[j])
        if masked:
            seen = mask_of(kcol[b], qid_ref[pl.ds(a, 1)][0], j >= HALF, noisy_k)
            p = jnp.where(seen, p, 0.0)
        ds = (p * (dp - delta[j]) * SCALE).astype(bf16)
        dkv_acc[slot, :, :HD] += nn(ds, q2)
        dkv_acc[slot, :, HD:] += nn(p.astype(bf16), o2)
        dq_acc[j] += nn(kts[slot], ds)

    for_live(mm, body)
    for j in range(NZ):
        t = dq_acc[j]
        dq_ref[j] = jnp.concatenate([t[:, :CH].T, t[:, CH:].T], axis=1).astype(bf16)
    core = ids[4]
    for slot in range(NRUN):
        for xh in range(NXH):
            y, x = slot // NXL, xh * NXL + slot % NXL
            at = xh * NCORE * CH
            own_at = pl.multiple_of(at + core * CH, CH)
            other_at = pl.multiple_of(at + (1 - core) * CH, CH)
            own_ref[y * NX + x] = dkv_acc[slot, pl.ds(own_at, CH), :].astype(bf16)
            other_ref[y * NX + x] = dkv_acc[slot, pl.ds(other_at, CH), :].astype(bf16)


SMEM = pl.BlockSpec(memory_space=pltpu.SMEM)
VMEM = pl.BlockSpec(memory_space=pltpu.VMEM)
ANY = pl.BlockSpec(memory_space=pl.ANY)
BIG = 48 << 20
LOADS = [
    pltpu.VMEM((NZ, CH, 4 * HD), bf16),
    pltpu.VMEM((NRUN, RUN, 2 * HD), bf16),
    pltpu.VMEM((HALF, RUN, CH), i32),
]
ROW = pltpu.VMEM((NZ, 1, 2 * CH), f32)
SEMS = pltpu.SemaphoreType.DMA((N_COPIES,))


def per_device(queries, key_states, value_states, grad_output, block_ids):
    z, xh, core = (lax.axis_index(n) for n in ROWS)
    y, xl = (lax.axis_index(n) for n in COLS)
    qo = jnp.concatenate([queries, grad_output], axis=1)
    kv = jnp.concatenate([key_states, value_states], axis=1)

    def swap(t):
        return lax.ppermute(t, "core", [(0, 1), (1, 0)])

    xs = jnp.stack([kv] + [shift(kv, XAX, NX, k) for k in range(1, NX)])
    k_own = [xs] + [shift(xs, "y", NY, s) for s in range(1, NY)]
    k_other = [swap(t) for t in k_own]
    pieces = {0: qo}
    for s in range(1, NZ // 2 + 1):
        pieces[s] = shift(pieces[s - 1], "z", NZ, 1)
        if s < NZ // 2:
            pieces[-s] = shift(pieces[1 - s], "z", NZ, -1)
    q_pieces = [pieces[s] for s in Q_SHIFTS]

    qid = block_ids.reshape(HALF, NXH * NCORE * NY * NXL, CH)
    place = ((xh * NCORE + core) * NY + y) * NXL + xl
    qid = lax.dynamic_slice_in_dim(qid, place, 1, 1)
    kid = block_ids.reshape(HALF, NZ, RUN)
    kid = lax.dynamic_slice_in_dim(kid, z, 1, 1).reshape(HALF, RUN)
    mm = jnp.stack([qid[:, 0, 0], qid[:, 0, CH - 1], kid[:, 0], kid[:, RUN - 1]])
    ids = jnp.stack([z, y, xh, xl, core]).astype(i32)
    data = (*q_pieces, *k_own, *k_other)

    stats = pl.pallas_call(
        stats_kernel,
        out_shape=jax.ShapeDtypeStruct((NZ, 2, 2 * CH), f32),
        in_specs=[SMEM, SMEM, VMEM, VMEM] + [ANY] * len(data),
        out_specs=VMEM,
        scratch_shapes=LOADS + [ROW, ROW, ROW, SEMS],
        compiler_params=pltpu.CompilerParams(vmem_limit_bytes=BIG),
    )(ids, mm, qid, kid, *data)
    stats = jnp.broadcast_to(stats[None], (NZ,) + stats.shape)
    stats = lax.all_to_all(stats, "z", 0, 0)
    dq, own, other = pl.pallas_call(
        grad_kernel,
        out_shape=(
            jax.ShapeDtypeStruct((NZ, CH, 2 * HD), bf16),
            jax.ShapeDtypeStruct((NY * NX, CH, 2 * HD), bf16),
            jax.ShapeDtypeStruct((NY * NX, CH, 2 * HD), bf16),
        ),
        in_specs=[SMEM, SMEM, VMEM, VMEM, VMEM] + [ANY] * len(data),
        out_specs=(VMEM, VMEM, VMEM),
        scratch_shapes=LOADS
        + [
            pltpu.VMEM((NRUN, HD, RUN), bf16),
            ROW,
            ROW,
            pltpu.VMEM((NZ, HD, 2 * CH), f32),
            pltpu.VMEM((NRUN, RUN, 2 * HD), f32),
            SEMS,
        ],
        compiler_params=pltpu.CompilerParams(vmem_limit_bytes=BIG),
    )(ids, mm, qid, kid, stats, *data)
    pair = (own.astype(f32) + swap(other).astype(f32)).astype(bf16)
    pair = lax.all_to_all(pair, ("y", "xh", "xl"), 0, 0)
    dq = lax.all_to_all(dq, "z", 0, 0)
    pair = jnp.sum(pair.astype(f32), axis=0).astype(bf16)
    dq = jnp.sum(dq.astype(f32), axis=0).astype(bf16)
    return dq, pair[:, :HD], pair[:, HD:]


def solution(mesh):
    fine = Mesh(mesh.devices.reshape(NZ, NXH, NCORE, NY, NXL), ROWS + COLS)
    by_row = P(ROWS + COLS, None)
    by_col = P(COLS + ROWS, None)
    return jax.shard_map(
        per_device,
        mesh=fine,
        in_specs=(by_row, by_col, by_col, by_row, P()),
        out_specs=(by_row, by_col, by_col),
        check_vma=False,
    )
```

time: 716 us -> 144 us (0.20)
  waiting for transfers between devices: 338 us -> 46.7 us
  loops' own time: 164 us -> 0 us
  blocking collectives: 133 us -> 11.5 us
  other arithmetic: 52.2 us -> 2.19 us
  Pallas kernels: 0 us -> 39.7 us
  starting transfers between devices: 0.12 us -> 27.8 us
  between operations: 13.8 us -> 0.85 us
    reduce_scatter x2 -> x0, waiting for transfers between devices: 311 us -> none  [the longest x1 180 us: per_device(): lax.psum_scatter(grad_flat, 'col', scatter_dimension=0, tiled=True)]
    another operation x34 -> x0, loops' own time: 164 us -> none  [the longest x1 81.8 us: stats_pass(): return lax.fori_loop(0, set_width // step_len, stats_visit, running)]
    all_gather x2 -> x0, blocking collectives: 55.5 us -> none  [the longest x1 28.1 us: per_device(): lax.all_gather(grad_output, 'col', axis=0, tiled=True)]
    pmax x1 -> x0, blocking collectives: 44.8 us -> none  [per_device(): row_max = lax.pmax(run_max, 'col')]
    pallas_call x0 -> x2, Pallas kernels: none -> 39.7 us  [the longest x1 21.8 us: per_device(): pl.pallas_call(grad_kernel, out_shape=(jax.ShapeDtypeStruct((NZ, CH, 2 *...]
    psum x1 -> x0, blocking collectives: 32.7 us -> none  [per_device(): row_sum, row_dot = lax.psum((run_sum * factor, run_dot * factor), 'col')]
    all_to_all x0 -> x2, waiting for transfers between devices: none -> 31.2 us  [the longest x1 17.1 us: per_device(): dq = lax.all_to_all(dq, 'z', 0, 0)]
    all_gather x1 -> x0, waiting for transfers between devices: 26.7 us -> none  [per_device(): pair_all = lax.all_gather(pair_local, 'row', axis=1, tiled=True)]
  transfers between devices with their start and end apart: 3 -> 20, of which waited for: 3 -> 10; matrix products, arithmetic and copies ran while one was open for 1% -> 5% of each run, Pallas kernels for 0% -> 0%
where the time goes in v1:
time: 144 us; the launch traced here: 141 us
  waiting for transfers between devices  46.7 us (32%)
  Pallas kernels  39.7 us (28%)
  starting transfers between devices  27.8 us (19%)
  local copies, waits for them, and re-layouts  12.1 us (8%)
  blocking collectives  11.5 us (8%)
  other arithmetic  2.19 us (2%)
    pallas_call x1, Pallas kernels, per_device(): pl.pallas_call(grad_kernel, out_shape=(jax.ShapeDtypeStruct((NZ, CH, 2 *...  21.8 us
    ppermute x13, starting transfers between devices, shift(): return lax.ppermute(x, axis, [(i, (i + by) % size) for i in range(size)])  20 us
    pallas_call x1, Pallas kernels, per_device(): pl.pallas_call(stats_kernel, out_shape=jax.ShapeDtypeStruct((NZ, 2, 2 * C...  17.9 us
    all_to_all x1, waiting for transfers between devices, per_device(): dq = lax.all_to_all(dq, 'z', 0, 0)  17.1 us
    ppermute x13, waiting for transfers between devices, shift(): return lax.ppermute(x, axis, [(i, (i + by) % size) for i in range(size)])  15.5 us
    all_to_all x1, waiting for transfers between devices, per_device(): pair = lax.all_to_all(pair, ('y', 'xh', 'xl'), 0, 0)  14.1 us
    all_to_all x1, blocking collectives, per_device(): stats = lax.all_to_all(stats, 'z', 0, 0)  11.5 us
    unnamed x25, local copies, waits for them, and re-layouts  6.96 us
  transfers between devices with their start and end apart: 20, of which 10 were waited for; matrix products, arithmetic and copies ran while one was open for 5% of the time, Pallas kernels for 0%

profile of v1, /device:TPU:8, one launch (start us, length us, event | category | flops | bytes accessed | tf_op | source)
XLA Modules:
  0.0 140.8 jit_solution(4701052903861750467)
XLA Ops:
  0.6 0.8 constant_dynamic-update-slice_fusion.1
  1.5 0.8 constant_dynamic-update-slice_fusion.refs_0_
  2.3 5.9 %collective-permute-start.1 = (bf16[128,512]{1,0:T(8,128)(2,1)S(1)}, bf16[128,512]{1,0:T(8,128)(2,1)S(1)}, u32[]{:S(2)}, u32[]{:S(2)}) collective-permute-start(bf16[128,512]{1,0:T(8,128)(2,1)S(1)} %constant_dynamic-update-slice_fusion.refs_0_), channel_id=1, source_target_pairs={{0,224},{32,0},{64,32},{96,64},{128,96},{160,128},{192,160},{224,1... | collective-permute-start | bytes 393224 | tf_op jit(solution)/shard_map/ppermute | solution.py:31
  8.2 0.8 constant_dynamic-update-slice_fusion.3
  8.9 0.8 constant_dynamic-update-slice_fusion.2
  9.7 2.8 %collective-permute-start.9 = (bf16[128,256]{1,0:T(8,128)(2,1)S(1)}, bf16[128,256]{1,0:T(8,128)(2,1)S(1)}, u32[]{:S(2)}, u32[]{:S(2)}) collective-permute-start(bf16[128,256]{1,0:T(8,128)(2,1)S(1)} %constant_dynamic-update-slice_fusion.2), channel_id=1, source_target_pairs={{0,17},{1,0},{16,1},{17,16},{2,19},{3,2},{18,3},{19,18},{4,21},{5,... | collective-permute-start | bytes 196616 | tf_op jit(solution)/shard_map/ppermute | solution.py:31
  12.5 0.8 collective-permute-start.8
  13.3 0.9 collective-permute-start.7
  14.2 0.0 collective-permute-start
  14.2 0.0 collective-permute-done.1.refs_2_
  14.2 3.2 %collective-permute-start.3 = (bf16[128,512]{1,0:T(8,128)(2,1)S(1)}, bf16[128,512]{1,0:T(8,128)(2,1)S(1)}, u32[]{:S(2)}, u32[]{:S(2)}) collective-permute-start(bf16[128,512]{1,0:T(8,128)(2,1)S(1)} %collective-permute-done.1.refs_2_), channel_id=1, source_target_pairs={{0,224},{32,0},{64,32},{96,64},{128,96},{160,128},{192,160},{224,1... | collective-permute-start | bytes 393224 | tf_op jit(solution)/shard_map/ppermute | solution.py:31
  17.5 0.0 collective-permute-done.9
  17.5 0.9 collective-permute-done.8
  18.3 0.7 collective-permute-done.7
  19.0 0.5 collective-permute-start.12
  19.6 2.6 %collective-permute-start.11 = (bf16[4,128,256]{2,1,0:T(8,128)(2,1)S(1)}, bf16[4,128,256]{2,1,0:T(8,128)(2,1)S(1)}, u32[]{:S(2)}, u32[]{:S(2)}) collective-permute-start(bf16[4,128,256]{2,1,0:T(8,128)(2,1)S(1)} %pad_maximum_fusion.refs_8_), channel_id=1, source_target_pairs={{0,4},{2,6},{4,0},{6,2},{1,5},{3,7},{5,1},{7,3},{8,12},{10,14},{12... | collective-permute-start | bytes 786440 | tf_op jit(solution)/shard_map/ppermute | solution.py:31
  22.2 1.9 %collective-permute-start.10 = (bf16[4,128,256]{2,1,0:T(8,128)(2,1)S(1)}, bf16[4,128,256]{2,1,0:T(8,128)(2,1)S(1)}, u32[]{:S(2)}, u32[]{:S(2)}) collective-permute-start(bf16[4,128,256]{2,1,0:T(8,128)(2,1)S(1)} %pad_maximum_fusion.refs_8_), channel_id=1, source_target_pairs={{0,2},{2,4},{4,6},{6,0},{1,3},{3,5},{5,7},{7,1},{8,10},{10,12},{12... | collective-permute-start | bytes 786440 | tf_op jit(solution)/shard_map/ppermute | solution.py:31
  24.1 0.0 collective-permute-done.refs_1_
  24.1 0.0 collective-permute-start.2
  24.1 0.0 collective-permute-done.3.refs_4_
  24.1 0.0 copy-start.1
  24.1 0.1 collective-permute-start.13
  24.2 0.9 reshape.17
  25.0 5.2 %collective-permute-done.2.refs_3_ = bf16[128,512]{1,0:T(8,128)(2,1)S(1)} collective-permute-done((bf16[128,512]{1,0:T(8,128)(2,1)S(1)}, bf16[128,512]{1,0:T(8,128)(2,1)S(1)}, u32[]{:S(2)}, u32[]{:S(2)}) %collective-permute-start.2) | collective-permute-done | bytes 131104 | tf_op jit(solution)/shard_map/ppermute | solution.py:31
  30.3 0.0 collective-permute-start.4
  30.3 0.0 collective-permute-done.12.refs_11_
  30.3 0.1 collective-permute-start.16
  30.4 1.7 %collective-permute-done.11.refs_10_ = bf16[4,128,256]{2,1,0:T(8,128)(2,1)S(1)} collective-permute-done((bf16[4,128,256]{2,1,0:T(8,128)(2,1)S(1)}, bf16[4,128,256]{2,1,0:T(8,128)(2,1)S(1)}, u32[]{:S(2)}, u32[]{:S(2)}) %collective-permute-start.11) | collective-permute-done | bytes 262176 | tf_op jit(solution)/shard_map/ppermute | solution.py:31
  32.1 0.0 collective-permute-start.15
  32.1 0.8 collective-permute-done.10.refs_9_
  32.9 0.0 collective-permute-start.14
  32.9 0.2 slice_reduce_fusion.1
  33.1 0.0 collective-permute-done.13.refs_12_
  33.1 1.4 %collective-permute-start.5 = (bf16[128,512]{1,0:T(8,128)(2,1)S(1)}, bf16[128,512]{1,0:T(8,128)(2,1)S(1)}, u32[]{:S(2)}, u32[]{:S(2)}) collective-permute-start(bf16[128,512]{1,0:T(8,128)(2,1)S(1)} %collective-permute-done.3.refs_4_), channel_id=1, source_target_pairs={{0,224},{32,0},{64,32},{96,64},{128,96},{160,128},{192,160},{224,1... | collective-permute-start | bytes 393224 | tf_op jit(solution)/shard_map/ppermute | solution.py:31
  34.5 1.9 %collective-permute-done.4.refs_5_ = bf16[128,512]{1,0:T(8,128)(2,1)S(1)} collective-permute-done((bf16[128,512]{1,0:T(8,128)(2,1)S(1)}, bf16[128,512]{1,0:T(8,128)(2,1)S(1)}, u32[]{:S(2)}, u32[]{:S(2)}) %collective-permute-start.4) | collective-permute-done | bytes 131104 | tf_op jit(solution)/shard_map/ppermute | solution.py:31
  36.4 0.0 collective-permute-start.6
  36.4 0.7 constant_dynamic-slice_fusion.1.qid_ref
  37.2 0.1 stack.41.ids
  37.3 1.0 dynamic-slice_reduce_fusion.1
  38.3 0.8 collective-permute-done.5.refs_6_
  39.1 3.5 %collective-permute-done.6.refs_7_ = bf16[128,512]{1,0:T(8,128)(2,1)S(1)} collective-permute-done((bf16[128,512]{1,0:T(8,128)(2,1)S(1)}, bf16[128,512]{1,0:T(8,128)(2,1)S(1)}, u32[]{:S(2)}, u32[]{:S(2)}) %collective-permute-start.6) | collective-permute-done | bytes 131104 | tf_op jit(solution)/shard_map/ppermute | solution.py:31
  42.6 0.0 collective-permute-done.16.refs_15_
  42.6 0.0 collective-permute-done.15.refs_14_
  42.6 0.0 collective-permute-done.14.refs_13_
  42.6 17.9 %shard_map.76 = f32[8,2,256]{2,1,0:T(2,128)S(1)} custom-call(s32[5]{0:T(128)S(1)} %stack.41.ids, s32[4,4]{1,0:T(4,128)S(1)} %pad_add_fusion.mm, s32[4,1,128]{2,1,0:T(1,128)S(1)} %constant_dynamic-slice_fusion.1.qid_ref, s32[4,512]{1,0:T(4,128)S(1)} %bitcast.18, bf16[128,512]{1,0:T(8,128)(2,1)S(1)} %constant_dynamic-update-slice_fusion.refs_0_, ...), custom_call_target="tpu_custom_call" | custom-call | tf_op jit(solution)/shard_map/pallas_call | solution.py:246
  60.6 0.0 copy-done.1
  60.6 11.5 %all_to_all.15.st_ref = f32[8,8,2,256]{3,2,1,0:T(2,128)S(1)} all-to-all(f32[8,8,2,256]{3,2,1,0:T(2,128)S(1)} %broadcast_in_dim.2), channel_id=1, replica_groups=mesh['z'=8,'xh'=2,'core'=2,'y'=4,'xl'=2] {'z'}, dimensions={0} | all-to-all | bytes 262144 | tf_op jit(solution)/shard_map/all_to_all | solution.py:255
  72.1 0.9 copy-done.2
  73.0 0.9 copy-done.4
  73.9 0.9 copy-done.6
  74.8 0.9 copy-done.8
  75.7 0.9 copy-done.10
  76.6 21.8 %shard_map.77 = (bf16[8,128,256]{2,1,0:T(8,128)(2,1)S(1)}, bf16[16,128,256]{2,1,0:T(8,128)(2,1)S(1)}, bf16[16,128,256]{2,1,0:T(8,128)(2,1)}) custom-call(s32[5]{0:T(128)S(1)} %stack.41.ids, s32[4,4]{1,0:T(4,128)S(1)} %pad_add_fusion.mm, s32[4,1,128]{2,1,0:T(1,128)S(1)} %constant_dynamic-slice_fusion.1.qid_ref, s32[4,512]{1,0:T(4,128)S(1)} %bitcast.19, ...), custom_call_target="tpu_custom_call" | custom-call | tf_op jit(solution)/shard_map/pallas_call | solution.py:256
  98.4 0.8 copy-done
  99.2 0.0 collective-permute-start.17
  99.2 3.5 %all-to-all-start.1 = ((bf16[8,128,256]{2,1,0:T(8,128)(2,1)}), bf16[8,128,256]{2,1,0:T(8,128)(2,1)S(1)}, u32[]{:S(2)}, u32[]{:S(2)}) async-start(bf16[8,128,256]{2,1,0:T(8,128)(2,1)} %copy-done), calls=%async_computation.1 | async-start | bytes 1048576 | tf_op jit(solution)/shard_map/all_to_all | solution.py:278
  102.7 0.0 collective-permute-done.17
  102.7 1.3 add_convert_fusion
  104.0 17.1 %all-to-all-done.1 = bf16[8,128,256]{2,1,0:T(8,128)(2,1)S(1)} async-done(((bf16[8,128,256]{2,1,0:T(8,128)(2,1)}), bf16[8,128,256]{2,1,0:T(8,128)(2,1)S(1)}, u32[]{:S(2)}, u32[]{:S(2)}) %all-to-all-start.1) | async-done | bytes 524320 | tf_op jit(solution)/shard_map/all_to_all | solution.py:278
  121.1 4.1 %all-to-all-start.2 = ((bf16[16,128,256]{2,1,0:T(8,128)(2,1)}), bf16[16,128,256]{2,1,0:T(8,128)(2,1)S(1)}, u32[]{:S(2)}, u32[]{:S(2)}) async-start(bf16[16,128,256]{2,1,0:T(8,128)(2,1)} %add_convert_fusion), calls=%async_computation.2 | async-start | bytes 2097152 | tf_op jit(solution)/shard_map/all_to_all | solution.py:277
  125.3 0.7 reduce_sum.24
  126.0 14.1 %all-to-all-done.2 = bf16[16,128,256]{2,1,0:T(8,128)(2,1)S(1)} async-done(((bf16[16,128,256]{2,1,0:T(8,128)(2,1)}), bf16[16,128,256]{2,1,0:T(8,128)(2,1)S(1)}, u32[]{:S(2)}, u32[]{:S(2)}) %all-to-all-start.2) | async-done | bytes 1048608 | tf_op jit(solution)/shard_map/all_to_all | solution.py:277
  140.1 0.1 reduce_sum.25
  140.2 0.6 fusion
  (19 shorter events, 0.1 us)
Async XLA Ops:
  2.3 11.9 %collective-permute-start.1 = (bf16[128,512]{1,0:T(8,128)(2,1)S(1)}, bf16[128,512]{1,0:T(8,128)(2,1)S(1)}, u32[]{:S(2)}, u32[]{:S(2)}) collective-permute-start(bf16[128,512]{1,0:T(8,128)(2,1)S(1)} %constant_dynamic-update-slice_fusion.refs_0_), channel_id=1, source_target_pairs={{0,224},{32,0},{64,32},{96,64},{128,96},{160,128},{192,160},{224,1... | collective-permute-start | bytes 393224 | tf_op jit(solution)/shard_map/ppermute | solution.py:31
  9.7 7.8 %collective-permute-start.9 = (bf16[128,256]{1,0:T(8,128)(2,1)S(1)}, bf16[128,256]{1,0:T(8,128)(2,1)S(1)}, u32[]{:S(2)}, u32[]{:S(2)}) collective-permute-start(bf16[128,256]{1,0:T(8,128)(2,1)S(1)} %constant_dynamic-update-slice_fusion.2), channel_id=1, source_target_pairs={{0,17},{1,0},{16,1},{17,16},{2,19},{3,2},{18,3},{19,18},{4,21},{5,... | collective-permute-start | bytes 196616 | tf_op jit(solution)/shard_map/ppermute | solution.py:31
  12.5 5.8 %collective-permute-start.8 = (bf16[128,256]{1,0:T(8,128)(2,1)S(1)}, bf16[128,256]{1,0:T(8,128)(2,1)S(1)}, u32[]{:S(2)}, u32[]{:S(2)}) collective-permute-start(bf16[128,256]{1,0:T(8,128)(2,1)S(1)} %constant_dynamic-update-slice_fusion.2), channel_id=1, source_target_pairs={{0,16},{1,17},{16,0},{17,1},{2,18},{3,19},{18,2},{19,3},{4,20},{5,... | collective-permute-start | bytes 196616 | tf_op jit(solution)/shard_map/ppermute | solution.py:31
  13.3 5.7 %collective-permute-start.7 = (bf16[128,256]{1,0:T(8,128)(2,1)S(1)}, bf16[128,256]{1,0:T(8,128)(2,1)S(1)}, u32[]{:S(2)}, u32[]{:S(2)}) collective-permute-start(bf16[128,256]{1,0:T(8,128)(2,1)S(1)} %constant_dynamic-update-slice_fusion.2), channel_id=1, source_target_pairs={{0,1},{1,16},{16,17},{17,0},{2,3},{3,18},{18,19},{19,2},{4,5},{5,2... | collective-permute-start | bytes 196616 | tf_op jit(solution)/shard_map/ppermute | solution.py:31
  14.2 9.8 %collective-permute-start = (bf16[128,512]{1,0:T(8,128)(2,1)S(1)}, bf16[128,512]{1,0:T(8,128)(2,1)S(1)}, u32[]{:S(2)}, u32[]{:S(2)}) collective-permute-start(bf16[128,512]{1,0:T(8,128)(2,1)S(1)} %constant_dynamic-update-slice_fusion.refs_0_), channel_id=1, source_target_pairs={{0,32},{32,64},{64,96},{96,128},{128,160},{160,192},{192,224},{224... | collective-permute-start | bytes 393224 | tf_op jit(solution)/shard_map/ppermute | solution.py:31
  14.2 9.8 %collective-permute-start.3 = (bf16[128,512]{1,0:T(8,128)(2,1)S(1)}, bf16[128,512]{1,0:T(8,128)(2,1)S(1)}, u32[]{:S(2)}, u32[]{:S(2)}) collective-permute-start(bf16[128,512]{1,0:T(8,128)(2,1)S(1)} %collective-permute-done.1.refs_2_), channel_id=1, source_target_pairs={{0,224},{32,0},{64,32},{96,64},{128,96},{160,128},{192,160},{224,1... | collective-permute-start | bytes 393224 | tf_op jit(solution)/shard_map/ppermute | solution.py:31
  19.0 11.2 %collective-permute-start.12 = (bf16[4,128,256]{2,1,0:T(8,128)(2,1)S(1)}, bf16[4,128,256]{2,1,0:T(8,128)(2,1)S(1)}, u32[]{:S(2)}, u32[]{:S(2)}) collective-permute-start(bf16[4,128,256]{2,1,0:T(8,128)(2,1)S(1)} %pad_maximum_fusion.refs_8_), channel_id=1, source_target_pairs={{0,6},{2,0},{4,2},{6,4},{1,7},{3,1},{5,3},{7,5},{8,14},{10,8},{12,... | collective-permute-start | bytes 786440 | tf_op jit(solution)/shard_map/ppermute | solution.py:31
  19.6 12.5 %collective-permute-start.11 = (bf16[4,128,256]{2,1,0:T(8,128)(2,1)S(1)}, bf16[4,128,256]{2,1,0:T(8,128)(2,1)S(1)}, u32[]{:S(2)}, u32[]{:S(2)}) collective-permute-start(bf16[4,128,256]{2,1,0:T(8,128)(2,1)S(1)} %pad_maximum_fusion.refs_8_), channel_id=1, source_target_pairs={{0,4},{2,6},{4,0},{6,2},{1,5},{3,7},{5,1},{7,3},{8,12},{10,14},{12... | collective-permute-start | bytes 786440 | tf_op jit(solution)/shard_map/ppermute | solution.py:31
  22.2 10.7 %collective-permute-start.10 = (bf16[4,128,256]{2,1,0:T(8,128)(2,1)S(1)}, bf16[4,128,256]{2,1,0:T(8,128)(2,1)S(1)}, u32[]{:S(2)}, u32[]{:S(2)}) collective-permute-start(bf16[4,128,256]{2,1,0:T(8,128)(2,1)S(1)} %pad_maximum_fusion.refs_8_), channel_id=1, source_target_pairs={{0,2},{2,4},{4,6},{6,0},{1,3},{3,5},{5,7},{7,1},{8,10},{10,12},{12... | collective-permute-start | bytes 786440 | tf_op jit(solution)/shard_map/ppermute | solution.py:31
  24.1 6.2 %collective-permute-start.2 = (bf16[128,512]{1,0:T(8,128)(2,1)S(1)}, bf16[128,512]{1,0:T(8,128)(2,1)S(1)}, u32[]{:S(2)}, u32[]{:S(2)}) collective-permute-start(bf16[128,512]{1,0:T(8,128)(2,1)S(1)} %collective-permute-done.refs_1_), channel_id=1, source_target_pairs={{0,32},{32,64},{64,96},{96,128},{128,160},{160,192},{192,224},{224... | collective-permute-start | bytes 393224 | tf_op jit(solution)/shard_map/ppermute | solution.py:31
  24.1 36.5 %copy-start.1 = (bf16[128,512]{1,0:T(8,128)(2,1)}, bf16[128,512]{1,0:T(8,128)(2,1)S(1)}, u32[]{:S(2)}) copy-start(bf16[128,512]{1,0:T(8,128)(2,1)S(1)} %collective-permute-done.3.refs_4_) | copy-start | bytes 393220
  24.1 9.0 %collective-permute-start.13 = (bf16[4,128,256]{2,1,0:T(8,128)(2,1)S(1)}, bf16[4,128,256]{2,1,0:T(8,128)(2,1)S(1)}, u32[]{:S(2)}, u32[]{:S(2)}) collective-permute-start(bf16[4,128,256]{2,1,0:T(8,128)(2,1)S(1)} %pad_maximum_fusion.refs_8_), channel_id=1, source_target_pairs={{0,8},{8,0},{1,9},{9,1},{2,10},{10,2},{3,11},{11,3},{4,12},{12,4},... | collective-permute-start | bytes 786440 | tf_op jit(solution)/shard_map/ppermute | solution.py:225
  30.2 30.3 %copy-start.3 = (bf16[128,512]{1,0:T(8,128)(2,1)}, bf16[128,512]{1,0:T(8,128)(2,1)S(1)}, u32[]{:S(2)}) copy-start(bf16[128,512]{1,0:T(8,128)(2,1)S(1)} %collective-permute-done.2.refs_3_) | copy-start | bytes 393220
  30.3 6.2 %collective-permute-start.4 = (bf16[128,512]{1,0:T(8,128)(2,1)S(1)}, bf16[128,512]{1,0:T(8,128)(2,1)S(1)}, u32[]{:S(2)}, u32[]{:S(2)}) collective-permute-start(bf16[128,512]{1,0:T(8,128)(2,1)S(1)} %collective-permute-done.2.refs_3_), channel_id=1, source_target_pairs={{0,32},{32,64},{64,96},{96,128},{128,160},{160,192},{192,224},{224... | collective-permute-start | bytes 393224 | tf_op jit(solution)/shard_map/ppermute | solution.py:31
  30.3 12.3 %collective-permute-start.16 = (bf16[4,128,256]{2,1,0:T(8,128)(2,1)S(1)}, bf16[4,128,256]{2,1,0:T(8,128)(2,1)S(1)}, u32[]{:S(2)}, u32[]{:S(2)}) collective-permute-start(bf16[4,128,256]{2,1,0:T(8,128)(2,1)S(1)} %collective-permute-done.12.refs_11_), channel_id=1, source_target_pairs={{0,8},{8,0},{1,9},{9,1},{2,10},{10,2},{3,11},{11,3},{4,12},{12,4},... | collective-permute-start | bytes 786440 | tf_op jit(solution)/shard_map/ppermute | solution.py:225
  32.1 10.5 %collective-permute-start.15 = (bf16[4,128,256]{2,1,0:T(8,128)(2,1)S(1)}, bf16[4,128,256]{2,1,0:T(8,128)(2,1)S(1)}, u32[]{:S(2)}, u32[]{:S(2)}) collective-permute-start(bf16[4,128,256]{2,1,0:T(8,128)(2,1)S(1)} %collective-permute-done.11.refs_10_), channel_id=1, source_target_pairs={{0,8},{8,0},{1,9},{9,1},{2,10},{10,2},{3,11},{11,3},{4,12},{12,4},... | collective-permute-start | bytes 786440 | tf_op jit(solution)/shard_map/ppermute | solution.py:225
  32.9 9.7 %collective-permute-start.14 = (bf16[4,128,256]{2,1,0:T(8,128)(2,1)S(1)}, bf16[4,128,256]{2,1,0:T(8,128)(2,1)S(1)}, u32[]{:S(2)}, u32[]{:S(2)}) collective-permute-start(bf16[4,128,256]{2,1,0:T(8,128)(2,1)S(1)} %collective-permute-done.10.refs_9_), channel_id=1, source_target_pairs={{0,8},{8,0},{1,9},{9,1},{2,10},{10,2},{3,11},{11,3},{4,12},{12,4},... | collective-permute-start | bytes 786440 | tf_op jit(solution)/shard_map/ppermute | solution.py:225
  33.1 6.0 %collective-permute-start.5 = (bf16[128,512]{1,0:T(8,128)(2,1)S(1)}, bf16[128,512]{1,0:T(8,128)(2,1)S(1)}, u32[]{:S(2)}, u32[]{:S(2)}) collective-permute-start(bf16[128,512]{1,0:T(8,128)(2,1)S(1)} %collective-permute-done.3.refs_4_), channel_id=1, source_target_pairs={{0,224},{32,0},{64,32},{96,64},{128,96},{160,128},{192,160},{224,1... | collective-permute-start | bytes 393224 | tf_op jit(solution)/shard_map/ppermute | solution.py:31
  36.4 24.1 %copy-start.5 = (bf16[128,512]{1,0:T(8,128)(2,1)}, bf16[128,512]{1,0:T(8,128)(2,1)S(1)}, u32[]{:S(2)}) copy-start(bf16[128,512]{1,0:T(8,128)(2,1)S(1)} %collective-permute-done.4.refs_5_) | copy-start | bytes 393220
  36.4 6.2 %collective-permute-start.6 = (bf16[128,512]{1,0:T(8,128)(2,1)S(1)}, bf16[128,512]{1,0:T(8,128)(2,1)S(1)}, u32[]{:S(2)}, u32[]{:S(2)}) collective-permute-start(bf16[128,512]{1,0:T(8,128)(2,1)S(1)} %collective-permute-done.4.refs_5_), channel_id=1, source_target_pairs={{0,32},{32,64},{64,96},{96,128},{128,160},{160,192},{192,224},{224... | collective-permute-start | bytes 393224 | tf_op jit(solution)/shard_map/ppermute | solution.py:31
  39.1 21.5 %copy-start.7 = (bf16[128,512]{1,0:T(8,128)(2,1)}, bf16[128,512]{1,0:T(8,128)(2,1)S(1)}, u32[]{:S(2)}) copy-start(bf16[128,512]{1,0:T(8,128)(2,1)S(1)} %collective-permute-done.5.refs_6_) | copy-start | bytes 393220
  42.6 18.0 %copy-start.9 = (bf16[128,512]{1,0:T(8,128)(2,1)}, bf16[128,512]{1,0:T(8,128)(2,1)S(1)}, u32[]{:S(2)}) copy-start(bf16[128,512]{1,0:T(8,128)(2,1)S(1)} %collective-permute-done.6.refs_7_) | copy-start | bytes 393220
  72.1 0.9 copy-start.2
  73.0 0.9 copy-start.4
  73.9 0.9 copy-start.6
  74.8 0.9 copy-start.8
  75.7 0.9 copy-start.10
  98.4 0.8 copy-start
  99.2 3.5 %collective-permute-start.17 = (bf16[16,128,256]{2,1,0:T(8,128)(2,1)}, bf16[16,128,256]{2,1,0:T(8,128)(2,1)S(1)}, u32[]{:S(2)}, u32[]{:S(2)}) collective-permute-start(bf16[16,128,256]{2,1,0:T(8,128)(2,1)} %get-tuple-element.8), channel_id=1, source_target_pairs={{0,8},{8,0},{1,9},{9,1},{2,10},{10,2},{3,11},{11,3},{4,12},{12,4},... | collective-permute-start | bytes 3145736 | tf_op jit(solution)/shard_map/ppermute | solution.py:225
  99.2 21.9 %all-to-all-start.1 = ((bf16[8,128,256]{2,1,0:T(8,128)(2,1)}), bf16[8,128,256]{2,1,0:T(8,128)(2,1)S(1)}, u32[]{:S(2)}, u32[]{:S(2)}) async-start(bf16[8,128,256]{2,1,0:T(8,128)(2,1)} %copy-done), calls=%async_computation.1 | async-start | bytes 1048576 | tf_op jit(solution)/shard_map/all_to_all | solution.py:278
  121.1 18.9 %all-to-all-start.2 = ((bf16[16,128,256]{2,1,0:T(8,128)(2,1)}), bf16[16,128,256]{2,1,0:T(8,128)(2,1)S(1)}, u32[]{:S(2)}, u32[]{:S(2)}) async-start(bf16[16,128,256]{2,1,0:T(8,128)(2,1)} %add_convert_fusion), calls=%async_computation.2 | async-start | bytes 2097152 | tf_op jit(solution)/shard_map/all_to_all | solution.py:277

commit v2 on v1

v2 whole, which is shorter than its diff:
```python
import functools
import math

import jax
import jax.numpy as jnp
from jax import lax
from jax.experimental import pallas as pl
from jax.experimental.pallas import tpu as pltpu
from jax.sharding import Mesh
from jax.sharding import PartitionSpec as P

bf16 = jnp.bfloat16
f32 = jnp.float32
i32 = jnp.int32
NZ, NXH, NCORE, NY, NXL = 8, 2, 2, 4, 2
NX = NXH * NXL
CH = 128
HD = 128
RUN = NXH * NCORE * CH
NRUN = NY * NXL
HALF = NRUN // 2
NBLK = 32
LOW = -1e30
SCALE = 1.0 / math.sqrt(HD)
FACTOR = SCALE * math.log2(math.e)
ROWS = ("z", "xh", "core")
COLS = ("y", "xl")
XAX = ("xh", "xl")


def shift(x, axis, size, by):
    return lax.ppermute(x, axis, [(i, (i + by) % size) for i in range(size)])


def nt(a, b):
    return lax.dot_general(a, b, (((1,), (1,)), ((), ())), preferred_element_type=f32)


def nn(a, b):
    return lax.dot_general(a, b, (((1,), (0,)), ((), ())), preferred_element_type=f32)


def load_all(ids, q_pieces, k_own, k_other, qs, kvs, sem):
    z, y, xh, xl, core = ids[0], ids[1], ids[2], ids[3], ids[4]
    copies = []
    for r, by in enumerate(Q_SHIFTS):
        copies.append((q_pieces[r], qs.at[(z - by) % NZ]))
    x = xh * NXL + xl
    for s in range(NY):
        for k in range(NX):
            px = (x - k) % NX
            py = (y - s) % NY
            slot = py * NXL + px % NXL
            for refs, pc in ((k_own, core), (k_other, 1 - core)):
                at = pl.multiple_of((px // NXL) * (NCORE * CH) + pc * CH, CH)
                copies.append((refs[s].at[k], kvs.at[slot, pl.ds(at, CH)]))
    copies = [pltpu.make_async_copy(a, b, sem.at[n]) for n, (a, b) in enumerate(copies)]
    for c in copies:
        c.start()
    return copies


Q_SHIFTS = (0, 1, -1, 2, -2, 3, -3, 4)
N_COPIES = NZ + NCORE * NY * NX


def masks(qid_ref, kid_ref, hot, bias):
    lane = lax.broadcasted_iota(i32, (RUN, CH), 1)
    for b in range(HALF):
        col = jnp.broadcast_to(kid_ref[b : b + 1, :], (CH, RUN)).T
        hot[b] = jnp.where(lane == col, 1.0, 0.0).astype(bf16)
        hot[b + HALF] = jnp.where(lane == col + NBLK, 1.0, 0.0).astype(bf16)
    lane = lax.broadcasted_iota(i32, (CH, CH), 1)
    for a in range(HALF):
        col = jnp.broadcast_to(qid_ref[a], (CH, CH)).T
        bias[a] = jnp.where(lane <= col, 0.0, LOW).astype(bf16)
        seen = (lane < col) | (lane == col + NBLK)
        bias[a + HALF] = jnp.where(seen, 0.0, LOW).astype(bf16)


def both_heads(qo, base):
    return jnp.concatenate([qo[:, base : base + HD], qo[:, base + HD : base + 2 * HD]], axis=0)


def scores(k, q2, hot, bias):
    return nt(
        jnp.concatenate([k, hot], axis=1),
        jnp.concatenate([q2, jnp.concatenate([bias, bias], axis=0)], axis=1),
    )


def for_live(mm, body):
    def visit(n, carry):
        a = n // HALF
        b = n % HALF

        @pl.when(mm[2, b] <= mm[1, a])
        def _():
            body((a, a + HALF), b)

        @pl.when((mm[2, b] <= mm[1, a]) & (mm[3, b] >= mm[0, a]))
        def _():
            body((a + HALF,), b + HALF)

        return carry

    lax.fori_loop(0, HALF * HALF, visit, 0)


def stats_kernel(ids, mm, qid_ref, kid_ref, *refs):
    q_pieces, k_own, k_other = refs[:NZ], refs[NZ : NZ + NY], refs[NZ + NY : NZ + 2 * NY]
    out_ref = refs[NZ + 2 * NY]
    qs, kvs, hot, bias, top, total, dot, sem = refs[NZ + 2 * NY + 1 :]
    copies = load_all(ids, q_pieces, k_own, k_other, qs, kvs, sem)
    masks(qid_ref, kid_ref, hot, bias)
    for c in copies:
        c.wait()
    top[...] = jnp.full(top.shape, LOW, f32)
    total[...] = jnp.zeros(total.shape, f32)
    dot[...] = jnp.zeros(dot.shape, f32)

    def body(chunks, slot):
        ss = [scores(kvs[slot, :, :HD], both_heads(qs[j], 0), hot[slot], bias[j]) for j in chunks]
        dps = [nt(kvs[slot, :, HD:], both_heads(qs[j], 2 * HD)) for j in chunks]
        for j, s, dp in zip(chunks, ss, dps):
            old = top[j]
            new = jnp.maximum(old, jnp.max(s, axis=0, keepdims=True))
            p = jnp.exp2((s - new) * FACTOR)
            f = jnp.exp2((old - new) * FACTOR)
            top[j] = new
            total[j] = total[j] * f + jnp.sum(p, axis=0, keepdims=True)
            dot[j] = dot[j] * f + jnp.sum(p * dp, axis=0, keepdims=True)

    for_live(mm, body)
    t = total[...]
    some = t > 0.0
    safe = jnp.where(some, t, 1.0)
    out_ref[:, 0:1, :] = jnp.where(some, top[...] * FACTOR + jnp.log2(safe), LOW)
    out_ref[:, 1:2, :] = dot[...] / safe


def grad_kernel(ids, mm, qid_ref, kid_ref, st_ref, *refs):
    q_pieces, k_own, k_other = refs[:NZ], refs[NZ : NZ + NY], refs[NZ + NY : NZ + 2 * NY]
    dq_ref, own_ref, other_ref = refs[NZ + 2 * NY : NZ + 2 * NY + 3]
    qs, kvs, hot, bias, kts, lse, delta, dq_acc, dkv_acc, sem = refs[NZ + 2 * NY + 3 :]
    copies = load_all(ids, q_pieces, k_own, k_other, qs, kvs, sem)
    masks(qid_ref, kid_ref, hot, bias)
    parts = st_ref[:, :, 0:1, :]
    high = jnp.max(parts, axis=0)
    shares = jnp.exp2(parts - high[None])
    sums = jnp.sum(shares, axis=0)
    lse[...] = high + jnp.log2(sums)
    delta[...] = jnp.sum(shares * st_ref[:, :, 1:2, :], axis=0) / sums
    dq_acc[...] = jnp.zeros(dq_acc.shape, f32)
    dkv_acc[...] = jnp.zeros(dkv_acc.shape, f32)
    for c in copies:
        c.wait()

    def body(chunks, slot):
        q2s, o2s, dss, ps = [], [], [], []
        for j in chunks:
            qo = qs[j]
            q2 = both_heads(qo, 0)
            o2 = both_heads(qo, 2 * HD)
            s = scores(kvs[slot, :, :HD], q2, hot[slot], bias[j])
            dp = nt(kvs[slot, :, HD:], o2)
            p = jnp.exp2(s * FACTOR - lse[j])
            ds = (p * (dp - delta[j]) * SCALE).astype(bf16)
            q2s.append(q2)
            o2s.append(o2)
            dss.append(ds)
            ps.append(p.astype(bf16))
        q2, o2 = jnp.concatenate(q2s, axis=0), jnp.concatenate(o2s, axis=0)
        ds, p = jnp.concatenate(dss, axis=1), jnp.concatenate(ps, axis=1)
        dq = lax.dot_general(ds, kvs[slot, :, :HD], (((0,), (0,)), ((), ())), preferred_element_type=f32)
        for i, j in enumerate(chunks):
            dq_acc[j] += dq[2 * CH * i : 2 * CH * (i + 1)]
        dkv_acc[slot, :, :HD] += nn(ds, q2)
        dkv_acc[slot, :, HD:] += nn(p, o2)

    for_live(mm, body)
    for j in range(NZ):
        t = dq_acc[j]
        dq_ref[j] = jnp.concatenate([t[:CH], t[CH:]], axis=1).astype(bf16)
    core = ids[4]
    for slot in range(NRUN):
        for xh in range(NXH):
            y, x = slot // NXL, xh * NXL + slot % NXL
            at = xh * NCORE * CH
            own_at = pl.multiple_of(at + core * CH, CH)
            other_at = pl.multiple_of(at + (1 - core) * CH, CH)
            own_ref[y, x] = dkv_acc[slot, pl.ds(own_at, CH), :].astype(bf16)
            other_ref[y, x] = dkv_acc[slot, pl.ds(other_at, CH), :].astype(bf16)


SMEM = pl.BlockSpec(memory_space=pltpu.SMEM)
VMEM = pl.BlockSpec(memory_space=pltpu.VMEM)
ANY = pl.BlockSpec(memory_space=pl.ANY)
BIG = 60 << 20
LOADS = [
    pltpu.VMEM((NZ, CH, 4 * HD), bf16),
    pltpu.VMEM((NRUN, RUN, 2 * HD), bf16),
    pltpu.VMEM((NRUN, RUN, CH), bf16),
    pltpu.VMEM((NZ, CH, CH), bf16),
]
ROW = pltpu.VMEM((NZ, 1, 2 * CH), f32)
SEMS = pltpu.SemaphoreType.DMA((N_COPIES,))


def per_device(queries, key_states, value_states, grad_output, block_ids):
    z, xh, core = (lax.axis_index(n) for n in ROWS)
    y, xl = (lax.axis_index(n) for n in COLS)
    qo = jnp.concatenate([queries, grad_output], axis=1)
    kv = jnp.concatenate([key_states, value_states], axis=1)

    def swap(t):
        return lax.ppermute(t, "core", [(0, 1), (1, 0)])

    xs = jnp.stack([kv] + [shift(kv, XAX, NX, k) for k in range(1, NX)])
    k_own = [xs] + [shift(xs, "y", NY, s) for s in range(1, NY)]
    k_other = [swap(t) for t in k_own]
    pieces = {0: qo}
    for s in range(1, NZ // 2 + 1):
        pieces[s] = shift(pieces[s - 1], "z", NZ, 1)
        if s < NZ // 2:
            pieces[-s] = shift(pieces[1 - s], "z", NZ, -1)
    q_pieces = [pieces[s] for s in Q_SHIFTS]

    qid = block_ids.reshape(HALF, NXH * NCORE * NY * NXL, CH)
    place = ((xh * NCORE + core) * NY + y) * NXL + xl
    qid = lax.dynamic_slice_in_dim(qid, place, 1, 1)
    kid = block_ids.reshape(HALF, NZ, RUN)
    kid = lax.dynamic_slice_in_dim(kid, z, 1, 1).reshape(HALF, RUN)
    mm = jnp.stack([qid[:, 0, 0], qid[:, 0, CH - 1], kid[:, 0], kid[:, RUN - 1]])
    ids = jnp.stack([z, y, xh, xl, core]).astype(i32)
    data = (*q_pieces, *k_own, *k_other)

    stats = stats_call(ids, mm, qid, kid, data)
    stats = jnp.broadcast_to(stats[None], (NZ,) + stats.shape)
    stats = lax.all_to_all(stats, "z", 0, 0)
    dq, own, other = grad_call(ids, mm, qid, kid, stats, data)

    dq = lax.all_to_all(dq, "z", 0, 0)
    pair = (own.astype(f32) + swap(other).astype(f32)).astype(bf16)
    pair = scatter(pair, y, "y", NY)
    pair = scatter(pair, xh * NXL + xl, XAX, NX)
    dq = jnp.sum(dq.astype(f32), axis=0).astype(bf16)
    return dq, pair[:, :HD], pair[:, HD:]


def scatter(t, me, axis, size):
    def part(k):
        return lax.dynamic_index_in_dim(t, (me + k) % size, 0, keepdims=False)

    got = [part(0)] + [shift(part(k), axis, size, k) for k in range(1, size)]
    return sum(g.astype(f32) for g in got).astype(bf16)


def stats_call(ids, mm, qid, kid, data):
    return pl.pallas_call(
        stats_kernel,
        out_shape=jax.ShapeDtypeStruct((NZ, 2, 2 * CH), f32),
        in_specs=[SMEM, SMEM, VMEM, VMEM] + [ANY] * len(data),
        out_specs=VMEM,
        scratch_shapes=LOADS + [ROW, ROW, ROW, SEMS],
        compiler_params=pltpu.CompilerParams(vmem_limit_bytes=BIG),
    )(ids, mm, qid, kid, *data)


def grad_call(ids, mm, qid, kid, stats, data):
    return pl.pallas_call(
        grad_kernel,
        out_shape=(
            jax.ShapeDtypeStruct((NZ, CH, 2 * HD), bf16),
            jax.ShapeDtypeStruct((NY, NX, CH, 2 * HD), bf16),
            jax.ShapeDtypeStruct((NY, NX, CH, 2 * HD), bf16),
        ),
        in_specs=[SMEM, SMEM, VMEM, VMEM, VMEM] + [ANY] * len(data),
        out_specs=(VMEM, VMEM, VMEM),
        scratch_shapes=LOADS
        + [
            pltpu.VMEM((NRUN, HD, RUN), bf16),
            ROW,
            ROW,
            pltpu.VMEM((NZ, 2 * CH, HD), f32),
            pltpu.VMEM((NRUN, RUN, 2 * HD), f32),
            SEMS,
        ],
        compiler_params=pltpu.CompilerParams(vmem_limit_bytes=BIG),
    )(ids, mm, qid, kid, stats, *data)


def solution(mesh):
    fine = Mesh(mesh.devices.reshape(NZ, NXH, NCORE, NY, NXL), ROWS + COLS)
    by_row = P(ROWS + COLS, None)
    by_col = P(COLS + ROWS, None)
    return jax.shard_map(
        per_device,
        mesh=fine,
        in_specs=(by_row, by_col, by_col, by_row, P()),
        out_specs=(by_row, by_col, by_col),
        check_vma=False,
    )
```

time: 144 us -> 117 us (0.81); the launches traced: 141 us -> 116 us
  waiting for transfers between devices: 46.7 us -> 24.8 us
  Pallas kernels: 39.7 us -> 29.1 us
  starting transfers between devices: 27.8 us -> 34.5 us
    all_to_all x1, waiting for transfers between devices: 17.1 us -> 0.01 us  [per_device(): dq = lax.all_to_all(dq, 'z', 0, 0)]
    all_to_all x1 -> x0, waiting for transfers between devices: 14.1 us -> none  [per_device(): pair = lax.all_to_all(pair, ('y', 'xh', 'xl'), 0, 0)]
    ppermute x13 -> x19, starting transfers between devices: 20 us -> 30.6 us  [shift(): return lax.ppermute(x, axis, [(i, (i + by) % size) for i in range(size)])]
    pallas_call x2, Pallas kernels: 39.7 us -> 29.1 us  [the longest x1 17.5 us: grad_call(): pl.pallas_call(grad_kernel, out_shape=(jax.ShapeDtypeStruct((NZ, CH, 2 *...]
    ppermute x13 -> x19, waiting for transfers between devices: 15.5 us -> 24.8 us  [shift(): return lax.ppermute(x, axis, [(i, (i + by) % size) for i in range(size)])]
    all_to_all x1 -> x0, starting transfers between devices: 4.12 us -> none  [per_device(): pair = lax.all_to_all(pair, ('y', 'xh', 'xl'), 0, 0)]
    unnamed x25 -> x41, local copies, waits for them, and re-layouts: 6.96 us -> 4.04 us
  transfers between devices with their start and end apart: 20 -> 25, of which waited for: 10 -> 10; matrix products, arithmetic and copies ran while one was open for 5% -> 8% of each run, Pallas kernels for 0% -> 0%
where the time goes in v2:
time: 117 us; the launch traced here: 116 us
  starting transfers between devices  34.5 us (29%)
  Pallas kernels  29.1 us (25%)
  waiting for transfers between devices  24.8 us (21%)
  blocking collectives  12.1 us (10%)
  local copies, waits for them, and re-layouts  11.2 us (10%)
  other arithmetic  3.04 us (3%)
    ppermute x19, starting transfers between devices, shift(): return lax.ppermute(x, axis, [(i, (i + by) % size) for i in range(size)])  30.6 us
    ppermute x19, waiting for transfers between devices, shift(): return lax.ppermute(x, axis, [(i, (i + by) % size) for i in range(size)])  24.8 us
    pallas_call x1, Pallas kernels, grad_call(): pl.pallas_call(grad_kernel, out_shape=(jax.ShapeDtypeStruct((NZ, CH, 2 *...  17.5 us
    all_to_all x1, blocking collectives, per_device(): stats = lax.all_to_all(stats, 'z', 0, 0)  12.1 us
    pallas_call x1, Pallas kernels, stats_call(): pl.pallas_call(stats_kernel, out_shape=jax.ShapeDtypeStruct((NZ, 2, 2 * C...  11.5 us
    unnamed x41, local copies, waits for them, and re-layouts  4.04 us
    all_to_all x1, starting transfers between devices, per_device(): dq = lax.all_to_all(dq, 'z', 0, 0)  3.64 us
  transfers between devices with their start and end apart: 25, of which 10 were waited for; matrix products, arithmetic and copies ran while one was open for 8% of the time, Pallas kernels for 0%

profile of v2, /device:TPU:8, one launch (start us, length us, event | category | flops | bytes accessed | tf_op | source)
XLA Modules:
  0.0 115.8 jit_solution(11771476527272151934)
XLA Ops:
  0.6 0.8 constant_dynamic-update-slice_fusion.1
  1.5 0.8 constant_dynamic-update-slice_fusion.refs_0_
  2.3 1.9 %collective-permute-start = (bf16[128,512]{1,0:T(8,128)(2,1)S(1)}, bf16[128,512]{1,0:T(8,128)(2,1)S(1)}, u32[]{:S(2)}, u32[]{:S(2)}) collective-permute-start(bf16[128,512]{1,0:T(8,128)(2,1)S(1)} %constant_dynamic-update-slice_fusion.refs_0_), channel_id=1, source_target_pairs={{0,32},{32,64},{64,96},{96,128},{128,160},{160,192},{192,224},{224... | collective-permute-start | bytes 393224 | tf_op jit(solution)/shard_map/ppermute | solution.py:32
  4.2 0.8 constant_dynamic-update-slice_fusion.3
  5.0 0.8 constant_dynamic-update-slice_fusion.2
  5.8 1.6 %collective-permute-start.7 = (bf16[128,256]{1,0:T(8,128)(2,1)S(1)}, bf16[128,256]{1,0:T(8,128)(2,1)S(1)}, u32[]{:S(2)}, u32[]{:S(2)}) collective-permute-start(bf16[128,256]{1,0:T(8,128)(2,1)S(1)} %constant_dynamic-update-slice_fusion.2), channel_id=1, source_target_pairs={{0,1},{1,16},{16,17},{17,0},{2,3},{3,18},{18,19},{19,2},{4,5},{5,2... | collective-permute-start | bytes 196616 | tf_op jit(solution)/shard_map/ppermute | solution.py:32
  7.3 2.7 %collective-permute-start.8 = (bf16[128,256]{1,0:T(8,128)(2,1)S(1)}, bf16[128,256]{1,0:T(8,128)(2,1)S(1)}, u32[]{:S(2)}, u32[]{:S(2)}) collective-permute-start(bf16[128,256]{1,0:T(8,128)(2,1)S(1)} %constant_dynamic-update-slice_fusion.2), channel_id=1, source_target_pairs={{0,16},{1,17},{16,0},{17,1},{2,18},{3,19},{18,2},{19,3},{4,20},{5,... | collective-permute-start | bytes 196616 | tf_op jit(solution)/shard_map/ppermute | solution.py:32
  10.1 1.4 %collective-permute-start.9 = (bf16[128,256]{1,0:T(8,128)(2,1)S(1)}, bf16[128,256]{1,0:T(8,128)(2,1)S(1)}, u32[]{:S(2)}, u32[]{:S(2)}) collective-permute-start(bf16[128,256]{1,0:T(8,128)(2,1)S(1)} %constant_dynamic-update-slice_fusion.2), channel_id=1, source_target_pairs={{0,17},{1,0},{16,1},{17,16},{2,19},{3,2},{18,3},{19,18},{4,21},{5,... | collective-permute-start | bytes 196616 | tf_op jit(solution)/shard_map/ppermute | solution.py:32
  11.5 4.0 %collective-permute-start.1 = (bf16[128,512]{1,0:T(8,128)(2,1)S(1)}, bf16[128,512]{1,0:T(8,128)(2,1)S(1)}, u32[]{:S(2)}, u32[]{:S(2)}) collective-permute-start(bf16[128,512]{1,0:T(8,128)(2,1)S(1)} %constant_dynamic-update-slice_fusion.refs_0_), channel_id=1, source_target_pairs={{0,224},{32,0},{64,32},{96,64},{128,96},{160,128},{192,160},{224,1... | collective-permute-start | bytes 393224 | tf_op jit(solution)/shard_map/ppermute | solution.py:32
  15.5 0.0 collective-permute-done.refs_1_
  15.5 0.0 collective-permute-start.2
  15.5 0.0 collective-permute-done.8
  15.5 0.0 collective-permute-done.9
  15.6 1.7 %collective-permute-start.10 = (bf16[4,128,256]{2,1,0:T(8,128)(2,1)S(1)}, bf16[4,128,256]{2,1,0:T(8,128)(2,1)S(1)}, u32[]{:S(2)}, u32[]{:S(2)}) collective-permute-start(bf16[4,128,256]{2,1,0:T(8,128)(2,1)S(1)} %pad_maximum_fusion.refs_8_), channel_id=1, source_target_pairs={{0,2},{2,4},{4,6},{6,0},{1,3},{3,5},{5,7},{7,1},{8,10},{10,12},{12... | collective-permute-start | bytes 786440 | tf_op jit(solution)/shard_map/ppermute | solution.py:32
  17.2 0.9 collective-permute-start.11
  18.2 2.4 %collective-permute-start.12 = (bf16[4,128,256]{2,1,0:T(8,128)(2,1)S(1)}, bf16[4,128,256]{2,1,0:T(8,128)(2,1)S(1)}, u32[]{:S(2)}, u32[]{:S(2)}) collective-permute-start(bf16[4,128,256]{2,1,0:T(8,128)(2,1)S(1)} %pad_maximum_fusion.refs_8_), channel_id=1, source_target_pairs={{0,6},{2,0},{4,2},{6,4},{1,7},{3,1},{5,3},{7,5},{8,14},{10,8},{12,... | collective-permute-start | bytes 786440 | tf_op jit(solution)/shard_map/ppermute | solution.py:32
  20.6 0.0 collective-permute-done.1.refs_2_
  20.6 3.2 %collective-permute-start.3 = (bf16[128,512]{1,0:T(8,128)(2,1)S(1)}, bf16[128,512]{1,0:T(8,128)(2,1)S(1)}, u32[]{:S(2)}, u32[]{:S(2)}) collective-permute-start(bf16[128,512]{1,0:T(8,128)(2,1)S(1)} %collective-permute-done.1.refs_2_), channel_id=1, source_target_pairs={{0,224},{32,0},{64,32},{96,64},{128,96},{160,128},{192,160},{224,1... | collective-permute-start | bytes 393224 | tf_op jit(solution)/shard_map/ppermute | solution.py:32
  23.8 0.0 collective-permute-start.13
  23.8 0.9 reshape.21
  24.7 1.6 %collective-permute-done.3.refs_4_ = bf16[128,512]{1,0:T(8,128)(2,1)S(1)} collective-permute-done((bf16[128,512]{1,0:T(8,128)(2,1)S(1)}, bf16[128,512]{1,0:T(8,128)(2,1)S(1)}, u32[]{:S(2)}, u32[]{:S(2)}) %collective-permute-start.3) | collective-permute-done | bytes 131104 | tf_op jit(solution)/shard_map/ppermute | solution.py:32
  26.3 0.3 collective-permute-start.4
  26.6 0.0 copy-start.18
  26.6 0.0 collective-permute-done.10.refs_9_
  26.6 0.1 collective-permute-start.14
  26.7 1.2 %collective-permute-done.11.refs_10_ = bf16[4,128,256]{2,1,0:T(8,128)(2,1)S(1)} collective-permute-done((bf16[4,128,256]{2,1,0:T(8,128)(2,1)S(1)}, bf16[4,128,256]{2,1,0:T(8,128)(2,1)S(1)}, u32[]{:S(2)}, u32[]{:S(2)}) %collective-permute-start.11) | collective-permute-done | bytes 262176 | tf_op jit(solution)/shard_map/ppermute | solution.py:32
  28.0 0.0 collective-permute-start.15
  28.0 2.3 %collective-permute-done.12.refs_11_ = bf16[4,128,256]{2,1,0:T(8,128)(2,1)S(1)} collective-permute-done((bf16[4,128,256]{2,1,0:T(8,128)(2,1)S(1)}, bf16[4,128,256]{2,1,0:T(8,128)(2,1)S(1)}, u32[]{:S(2)}, u32[]{:S(2)}) %collective-permute-start.12) | collective-permute-done | bytes 262176 | tf_op jit(solution)/shard_map/ppermute | solution.py:32
  30.3 0.0 collective-permute-start.16
  30.3 0.2 slice_reduce_fusion.1
  30.5 3.0 %collective-permute-start.5 = (bf16[128,512]{1,0:T(8,128)(2,1)S(1)}, bf16[128,512]{1,0:T(8,128)(2,1)S(1)}, u32[]{:S(2)}, u32[]{:S(2)}) collective-permute-start(bf16[128,512]{1,0:T(8,128)(2,1)S(1)} %collective-permute-done.3.refs_4_), channel_id=1, source_target_pairs={{0,224},{32,0},{64,32},{96,64},{128,96},{160,128},{192,160},{224,1... | collective-permute-start | bytes 393224 | tf_op jit(solution)/shard_map/ppermute | solution.py:32
  33.5 0.0 collective-permute-start.6
  33.5 1.4 %constant_dynamic-slice_fusion.3.qid_ref = s32[4,1,128]{2,1,0:T(1,128)} fusion(s32[4,32,128]{2,1,0:T(8,128)} %bitcast.39, s32[]{:T(128)S(6)} %select_n.67), kind=kLoop, calls=%fused_computation.24 | loop fusion | bytes 4100 | tf_op jit(solution)/shard_map/dynamic_slice | solution.py:231
  34.9 0.6 stack.41.ids
  35.5 1.0 fusion.6
  36.6 0.6 pad_add_fusion.mm
  37.2 3.2 %collective-permute-done.6.refs_7_ = bf16[128,512]{1,0:T(8,128)(2,1)S(1)} collective-permute-done((bf16[128,512]{1,0:T(8,128)(2,1)S(1)}, bf16[128,512]{1,0:T(8,128)(2,1)S(1)}, u32[]{:S(2)}, u32[]{:S(2)}) %collective-permute-start.6) | collective-permute-done | bytes 131104 | tf_op jit(solution)/shard_map/ppermute | solution.py:32
  40.5 0.5 copy-done.17
  41.0 0.1 copy-done.7
  41.2 0.1 copy-done.8
  41.2 0.7 copy-done.9
  42.0 11.5 %shard_map.76 = f32[8,2,256]{2,1,0:T(2,128)} custom-call(s32[5]{0:T(128)} %stack.41.ids, s32[4,4]{1,0:T(4,128)} %pad_add_fusion.mm, s32[4,1,128]{2,1,0:T(1,128)} %constant_dynamic-slice_fusion.3.qid_ref, s32[4,512]{1,0:T(4,128)} %bitcast.37, bf16[128,512]{1,0:T(8,128)(2,1)} %copy-done.10, bf16[128,512]{1,0:T(8,128)(2,1)} %copy-done.11, ...), custom_call_target="tpu_custom_call" | custom-call | tf_op jit(solution)/shard_map/pallas_call | solution.py:260
  53.5 0.8 broadcast_in_dim.2
  54.3 12.1 %all_to_all.10.st_ref = f32[8,8,2,256]{3,2,1,0:T(2,128)} all-to-all(f32[8,8,2,256]{3,2,1,0:T(2,128)S(1)} %broadcast_in_dim.2), channel_id=1, replica_groups=mesh['z'=8,'xh'=2,'core'=2,'y'=4,'xl'=2] {'z'}, dimensions={0} | all-to-all | bytes 262144 | tf_op jit(solution)/shard_map/all_to_all | solution.py:240
  66.4 17.5 %shard_map.77 = (bf16[8,128,256]{2,1,0:T(8,128)(2,1)}, bf16[4,4,128,256]{3,2,1,0:T(8,128)(2,1)}, bf16[4,4,128,256]{3,2,1,0:T(8,128)(2,1)}) custom-call(s32[5]{0:T(128)} %stack.41.ids, s32[4,4]{1,0:T(4,128)} %pad_add_fusion.mm, s32[4,1,128]{2,1,0:T(1,128)} %constant_dynamic-slice_fusion.3.qid_ref, s32[4,512]{1,0:T(4,128)} %bitcast.38, ...), custom_call_target="tpu_custom_call" | custom-call | tf_op jit(solution)/shard_map/pallas_call | solution.py:271
  84.0 0.1 collective-permute-start.17
  84.1 3.6 %all-to-all-start.1 = ((bf16[8,128,256]{2,1,0:T(8,128)(2,1)}), bf16[8,128,256]{2,1,0:T(8,128)(2,1)S(1)}, u32[]{:S(2)}, u32[]{:S(2)}) async-start(bf16[8,128,256]{2,1,0:T(8,128)(2,1)} %get-tuple-element.6), calls=%async_computation.1 | async-start | bytes 1048576 | tf_op jit(solution)/shard_map/all_to_all | solution.py:243
  87.8 0.9 copy-done.2
  88.7 1.5 %add_convert_fusion = bf16[4,4,128,256]{3,2,1,0:T(8,128)(2,1)S(1)} fusion(bf16[4,4,128,256]{3,2,1,0:T(8,128)(2,1)} %copy-done.2, bf16[4,4,128,256]{3,2,1,0:T(8,128)(2,1)S(1)} %copy-done.1), kind=kLoop, calls=%fused_computation | loop fusion | flops 2097152 | bytes 3145728 | tf_op jit(solution)/shard_map/convert_element_type | solution.py:244
  90.3 0.1 dynamic-slice_bitcast_fusion.2
  90.3 1.4 %collective-permute-start.18 = (bf16[4,128,256]{2,1,0:T(8,128)(2,1)S(1)}, bf16[4,128,256]{2,1,0:T(8,128)(2,1)S(1)}, u32[]{:S(2)}, u32[]{:S(2)}) collective-permute-start(bf16[4,128,256]{2,1,0:T(8,128)(2,1)S(1)} %get-tuple-element.13), channel_id=1, source_target_pairs={{0,2},{2,4},{4,6},{6,0},{1,3},{3,5},{5,7},{7,1},{8,10},{10,12},{12... | collective-permute-start | bytes 786440 | tf_op jit(solution)/shard_map/ppermute | solution.py:32
  91.7 1.7 %collective-permute-start.19 = (bf16[4,128,256]{2,1,0:T(8,128)(2,1)S(1)}, bf16[4,128,256]{2,1,0:T(8,128)(2,1)S(1)}, u32[]{:S(2)}, u32[]{:S(2)}) collective-permute-start(bf16[4,128,256]{2,1,0:T(8,128)(2,1)S(1)} %get-tuple-element.15), channel_id=1, source_target_pairs={{0,4},{2,6},{4,0},{6,2},{1,5},{3,7},{5,1},{7,3},{8,12},{10,14},{12... | collective-permute-start | bytes 786440 | tf_op jit(solution)/shard_map/ppermute | solution.py:32
  93.4 0.8 collective-permute-start.20
  94.1 5.4 %collective-permute-done.18 = bf16[4,128,256]{2,1,0:T(8,128)(2,1)S(1)} collective-permute-done((bf16[4,128,256]{2,1,0:T(8,128)(2,1)S(1)}, bf16[4,128,256]{2,1,0:T(8,128)(2,1)S(1)}, u32[]{:S(2)}, u32[]{:S(2)}) %collective-permute-start.18) | collective-permute-done | bytes 262176 | tf_op jit(solution)/shard_map/ppermute | solution.py:32
  99.5 2.9 %collective-permute-done.19 = bf16[4,128,256]{2,1,0:T(8,128)(2,1)S(1)} collective-permute-done((bf16[4,128,256]{2,1,0:T(8,128)(2,1)S(1)}, bf16[4,128,256]{2,1,0:T(8,128)(2,1)S(1)}, u32[]{:S(2)}, u32[]{:S(2)}) %collective-permute-start.19) | collective-permute-done | bytes 262176 | tf_op jit(solution)/shard_map/ppermute | solution.py:32
  102.4 4.5 %collective-permute-done.20 = bf16[4,128,256]{2,1,0:T(8,128)(2,1)S(1)} collective-permute-done((bf16[4,128,256]{2,1,0:T(8,128)(2,1)S(1)}, bf16[4,128,256]{2,1,0:T(8,128)(2,1)S(1)}, u32[]{:S(2)}, u32[]{:S(2)}) %collective-permute-start.20) | collective-permute-done | bytes 262176 | tf_op jit(solution)/shard_map/ppermute | solution.py:32
  106.9 0.1 fusion.2
  107.1 0.1 collective-permute-start.21
  107.2 3.7 %collective-permute-start.22 = (bf16[128,256]{1,0:T(8,128)(2,1)S(1)}, bf16[128,256]{1,0:T(8,128)(2,1)S(1)}, u32[]{:S(2)}, u32[]{:S(2)}) collective-permute-start(bf16[128,256]{1,0:T(8,128)(2,1)S(1)} %get-tuple-element.18), channel_id=1, source_target_pairs={{0,16},{1,17},{16,0},{17,1},{2,18},{3,19},{18,2},{19,3},{4,20},{5,... | collective-permute-start | bytes 196616 | tf_op jit(solution)/shard_map/ppermute | solution.py:32
  110.9 0.7 reduce_sum.12
  111.6 1.8 %collective-permute-done.21 = bf16[128,256]{1,0:T(8,128)(2,1)S(1)} collective-permute-done((bf16[128,256]{1,0:T(8,128)(2,1)S(1)}, bf16[128,256]{1,0:T(8,128)(2,1)S(1)}, u32[]{:S(2)}, u32[]{:S(2)}) %collective-permute-start.21) | collective-permute-done | bytes 65568 | tf_op jit(solution)/shard_map/ppermute | solution.py:32
  113.4 0.9 collective-permute-done.22
  114.3 0.9 collective-permute-done.23
  115.2 0.6 fusion.8
  (48 shorter events, 0.2 us)
Async XLA Ops:
  2.3 38.1 %copy-start.10 = (bf16[128,512]{1,0:T(8,128)(2,1)}, bf16[128,512]{1,0:T(8,128)(2,1)S(1)}, u32[]{:S(2)}) copy-start(bf16[128,512]{1,0:T(8,128)(2,1)S(1)} %constant_dynamic-update-slice_fusion.refs_0_) | copy-start | bytes 393220
  2.3 13.2 %collective-permute-start = (bf16[128,512]{1,0:T(8,128)(2,1)S(1)}, bf16[128,512]{1,0:T(8,128)(2,1)S(1)}, u32[]{:S(2)}, u32[]{:S(2)}) collective-permute-start(bf16[128,512]{1,0:T(8,128)(2,1)S(1)} %constant_dynamic-update-slice_fusion.refs_0_), channel_id=1, source_target_pairs={{0,32},{32,64},{64,96},{96,128},{128,160},{160,192},{192,224},{224... | collective-permute-start | bytes 393224 | tf_op jit(solution)/shard_map/ppermute | solution.py:32
  5.8 9.7 %collective-permute-start.7 = (bf16[128,256]{1,0:T(8,128)(2,1)S(1)}, bf16[128,256]{1,0:T(8,128)(2,1)S(1)}, u32[]{:S(2)}, u32[]{:S(2)}) collective-permute-start(bf16[128,256]{1,0:T(8,128)(2,1)S(1)} %constant_dynamic-update-slice_fusion.2), channel_id=1, source_target_pairs={{0,1},{1,16},{16,17},{17,0},{2,3},{3,18},{18,19},{19,2},{4,5},{5,2... | collective-permute-start | bytes 196616 | tf_op jit(solution)/shard_map/ppermute | solution.py:32
  7.3 8.2 %collective-permute-start.8 = (bf16[128,256]{1,0:T(8,128)(2,1)S(1)}, bf16[128,256]{1,0:T(8,128)(2,1)S(1)}, u32[]{:S(2)}, u32[]{:S(2)}) collective-permute-start(bf16[128,256]{1,0:T(8,128)(2,1)S(1)} %constant_dynamic-update-slice_fusion.2), channel_id=1, source_target_pairs={{0,16},{1,17},{16,0},{17,1},{2,18},{3,19},{18,2},{19,3},{4,20},{5,... | collective-permute-start | bytes 196616 | tf_op jit(solution)/shard_map/ppermute | solution.py:32
  10.1 5.4 %collective-permute-start.9 = (bf16[128,256]{1,0:T(8,128)(2,1)S(1)}, bf16[128,256]{1,0:T(8,128)(2,1)S(1)}, u32[]{:S(2)}, u32[]{:S(2)}) collective-permute-start(bf16[128,256]{1,0:T(8,128)(2,1)S(1)} %constant_dynamic-update-slice_fusion.2), channel_id=1, source_target_pairs={{0,17},{1,0},{16,1},{17,16},{2,19},{3,2},{18,3},{19,18},{4,21},{5,... | collective-permute-start | bytes 196616 | tf_op jit(solution)/shard_map/ppermute | solution.py:32
  11.5 9.1 %collective-permute-start.1 = (bf16[128,512]{1,0:T(8,128)(2,1)S(1)}, bf16[128,512]{1,0:T(8,128)(2,1)S(1)}, u32[]{:S(2)}, u32[]{:S(2)}) collective-permute-start(bf16[128,512]{1,0:T(8,128)(2,1)S(1)} %constant_dynamic-update-slice_fusion.refs_0_), channel_id=1, source_target_pairs={{0,224},{32,0},{64,32},{96,64},{128,96},{160,128},{192,160},{224,1... | collective-permute-start | bytes 393224 | tf_op jit(solution)/shard_map/ppermute | solution.py:32
  15.5 24.9 %copy-start.11 = (bf16[128,512]{1,0:T(8,128)(2,1)}, bf16[128,512]{1,0:T(8,128)(2,1)S(1)}, u32[]{:S(2)}) copy-start(bf16[128,512]{1,0:T(8,128)(2,1)S(1)} %collective-permute-done.refs_1_) | copy-start | bytes 393220
  15.5 8.3 %collective-permute-start.2 = (bf16[128,512]{1,0:T(8,128)(2,1)S(1)}, bf16[128,512]{1,0:T(8,128)(2,1)S(1)}, u32[]{:S(2)}, u32[]{:S(2)}) collective-permute-start(bf16[128,512]{1,0:T(8,128)(2,1)S(1)} %collective-permute-done.refs_1_), channel_id=1, source_target_pairs={{0,32},{32,64},{64,96},{96,128},{128,160},{160,192},{192,224},{224... | collective-permute-start | bytes 393224 | tf_op jit(solution)/shard_map/ppermute | solution.py:32
  15.6 24.9 %copy-start = (bf16[4,128,256]{2,1,0:T(8,128)(2,1)}, bf16[4,128,256]{2,1,0:T(8,128)(2,1)S(1)}, u32[]{:S(2)}) copy-start(bf16[4,128,256]{2,1,0:T(8,128)(2,1)S(1)} %pad_maximum_fusion.refs_8_) | copy-start | bytes 786436
  15.6 11.0 %collective-permute-start.10 = (bf16[4,128,256]{2,1,0:T(8,128)(2,1)S(1)}, bf16[4,128,256]{2,1,0:T(8,128)(2,1)S(1)}, u32[]{:S(2)}, u32[]{:S(2)}) collective-permute-start(bf16[4,128,256]{2,1,0:T(8,128)(2,1)S(1)} %pad_maximum_fusion.refs_8_), channel_id=1, source_target_pairs={{0,2},{2,4},{4,6},{6,0},{1,3},{3,5},{5,7},{7,1},{8,10},{10,12},{12... | collective-permute-start | bytes 786440 | tf_op jit(solution)/shard_map/ppermute | solution.py:32
  17.2 10.8 %collective-permute-start.11 = (bf16[4,128,256]{2,1,0:T(8,128)(2,1)S(1)}, bf16[4,128,256]{2,1,0:T(8,128)(2,1)S(1)}, u32[]{:S(2)}, u32[]{:S(2)}) collective-permute-start(bf16[4,128,256]{2,1,0:T(8,128)(2,1)S(1)} %pad_maximum_fusion.refs_8_), channel_id=1, source_target_pairs={{0,4},{2,6},{4,0},{6,2},{1,5},{3,7},{5,1},{7,3},{8,12},{10,14},{12... | collective-permute-start | bytes 786440 | tf_op jit(solution)/shard_map/ppermute | solution.py:32
  18.2 12.1 %collective-permute-start.12 = (bf16[4,128,256]{2,1,0:T(8,128)(2,1)S(1)}, bf16[4,128,256]{2,1,0:T(8,128)(2,1)S(1)}, u32[]{:S(2)}, u32[]{:S(2)}) collective-permute-start(bf16[4,128,256]{2,1,0:T(8,128)(2,1)S(1)} %pad_maximum_fusion.refs_8_), channel_id=1, source_target_pairs={{0,6},{2,0},{4,2},{6,4},{1,7},{3,1},{5,3},{7,5},{8,14},{10,8},{12,... | collective-permute-start | bytes 786440 | tf_op jit(solution)/shard_map/ppermute | solution.py:32
  20.6 19.9 %copy-start.12 = (bf16[128,512]{1,0:T(8,128)(2,1)}, bf16[128,512]{1,0:T(8,128)(2,1)S(1)}, u32[]{:S(2)}) copy-start(bf16[128,512]{1,0:T(8,128)(2,1)S(1)} %collective-permute-done.1.refs_2_) | copy-start | bytes 393220
  20.6 5.7 %collective-permute-start.3 = (bf16[128,512]{1,0:T(8,128)(2,1)S(1)}, bf16[128,512]{1,0:T(8,128)(2,1)S(1)}, u32[]{:S(2)}, u32[]{:S(2)}) collective-permute-start(bf16[128,512]{1,0:T(8,128)(2,1)S(1)} %collective-permute-done.1.refs_2_), channel_id=1, source_target_pairs={{0,224},{32,0},{64,32},{96,64},{128,96},{160,128},{192,160},{224,1... | collective-permute-start | bytes 393224 | tf_op jit(solution)/shard_map/ppermute | solution.py:32
  23.8 16.7 %copy-start.13 = (bf16[128,512]{1,0:T(8,128)(2,1)}, bf16[128,512]{1,0:T(8,128)(2,1)S(1)}, u32[]{:S(2)}) copy-start(bf16[128,512]{1,0:T(8,128)(2,1)S(1)} %collective-permute-done.2.refs_3_) | copy-start | bytes 393220
  23.8 6.7 %collective-permute-start.13 = (bf16[4,128,256]{2,1,0:T(8,128)(2,1)S(1)}, bf16[4,128,256]{2,1,0:T(8,128)(2,1)S(1)}, u32[]{:S(2)}, u32[]{:S(2)}) collective-permute-start(bf16[4,128,256]{2,1,0:T(8,128)(2,1)S(1)} %pad_maximum_fusion.refs_8_), channel_id=1, source_target_pairs={{0,8},{8,0},{1,9},{9,1},{2,10},{10,2},{3,11},{11,3},{4,12},{12,4},... | collective-permute-start | bytes 786440 | tf_op jit(solution)/shard_map/ppermute | solution.py:217
  26.3 14.1 %copy-start.14 = (bf16[128,512]{1,0:T(8,128)(2,1)}, bf16[128,512]{1,0:T(8,128)(2,1)S(1)}, u32[]{:S(2)}) copy-start(bf16[128,512]{1,0:T(8,128)(2,1)S(1)} %collective-permute-done.3.refs_4_) | copy-start | bytes 393220
  26.3 7.2 %collective-permute-start.4 = (bf16[128,512]{1,0:T(8,128)(2,1)S(1)}, bf16[128,512]{1,0:T(8,128)(2,1)S(1)}, u32[]{:S(2)}, u32[]{:S(2)}) collective-permute-start(bf16[128,512]{1,0:T(8,128)(2,1)S(1)} %collective-permute-done.2.refs_3_), channel_id=1, source_target_pairs={{0,32},{32,64},{64,96},{96,128},{128,160},{160,192},{192,224},{224... | collective-permute-start | bytes 393224 | tf_op jit(solution)/shard_map/ppermute | solution.py:32
  26.6 13.9 %copy-start.18 = (s32[4,1,512]{2,0,1:T(4,128)}, s32[4,1,512]{2,0,1:T(4,128)S(1)}, u32[]{:S(2)}) copy-start(s32[4,1,512]{2,0,1:T(4,128)S(1)} %copy.10) | copy-start | bytes 24580
  26.6 13.9 %copy-start.3 = (bf16[4,128,256]{2,1,0:T(8,128)(2,1)}, bf16[4,128,256]{2,1,0:T(8,128)(2,1)S(1)}, u32[]{:S(2)}) copy-start(bf16[4,128,256]{2,1,0:T(8,128)(2,1)S(1)} %collective-permute-done.10.refs_9_) | copy-start | bytes 786436
  26.6 13.7 %collective-permute-start.14 = (bf16[4,128,256]{2,1,0:T(8,128)(2,1)S(1)}, bf16[4,128,256]{2,1,0:T(8,128)(2,1)S(1)}, u32[]{:S(2)}, u32[]{:S(2)}) collective-permute-start(bf16[4,128,256]{2,1,0:T(8,128)(2,1)S(1)} %collective-permute-done.10.refs_9_), channel_id=1, source_target_pairs={{0,8},{8,0},{1,9},{9,1},{2,10},{10,2},{3,11},{11,3},{4,12},{12,4},... | collective-permute-start | bytes 786440 | tf_op jit(solution)/shard_map/ppermute | solution.py:217
  28.0 12.5 %copy-start.4 = (bf16[4,128,256]{2,1,0:T(8,128)(2,1)}, bf16[4,128,256]{2,1,0:T(8,128)(2,1)S(1)}, u32[]{:S(2)}) copy-start(bf16[4,128,256]{2,1,0:T(8,128)(2,1)S(1)} %collective-permute-done.11.refs_10_) | copy-start | bytes 786436
  28.0 12.4 %collective-permute-start.15 = (bf16[4,128,256]{2,1,0:T(8,128)(2,1)S(1)}, bf16[4,128,256]{2,1,0:T(8,128)(2,1)S(1)}, u32[]{:S(2)}, u32[]{:S(2)}) collective-permute-start(bf16[4,128,256]{2,1,0:T(8,128)(2,1)S(1)} %collective-permute-done.11.refs_10_), channel_id=1, source_target_pairs={{0,8},{8,0},{1,9},{9,1},{2,10},{10,2},{3,11},{11,3},{4,12},{12,4},... | collective-permute-start | bytes 786440 | tf_op jit(solution)/shard_map/ppermute | solution.py:217
  30.3 10.2 %copy-start.5 = (bf16[4,128,256]{2,1,0:T(8,128)(2,1)}, bf16[4,128,256]{2,1,0:T(8,128)(2,1)S(1)}, u32[]{:S(2)}) copy-start(bf16[4,128,256]{2,1,0:T(8,128)(2,1)S(1)} %collective-permute-done.12.refs_11_) | copy-start | bytes 786436
  30.3 10.1 %collective-permute-start.16 = (bf16[4,128,256]{2,1,0:T(8,128)(2,1)S(1)}, bf16[4,128,256]{2,1,0:T(8,128)(2,1)S(1)}, u32[]{:S(2)}, u32[]{:S(2)}) collective-permute-start(bf16[4,128,256]{2,1,0:T(8,128)(2,1)S(1)} %collective-permute-done.12.refs_11_), channel_id=1, source_target_pairs={{0,8},{8,0},{1,9},{9,1},{2,10},{10,2},{3,11},{11,3},{4,12},{12,4},... | collective-permute-start | bytes 786440 | tf_op jit(solution)/shard_map/ppermute | solution.py:217
  30.5 10.0 %copy-start.6 = (bf16[4,128,256]{2,1,0:T(8,128)(2,1)}, bf16[4,128,256]{2,1,0:T(8,128)(2,1)S(1)}, u32[]{:S(2)}) copy-start(bf16[4,128,256]{2,1,0:T(8,128)(2,1)S(1)} %collective-permute-done.13.refs_12_) | copy-start | bytes 786436
  30.5 6.6 %collective-permute-start.5 = (bf16[128,512]{1,0:T(8,128)(2,1)S(1)}, bf16[128,512]{1,0:T(8,128)(2,1)S(1)}, u32[]{:S(2)}, u32[]{:S(2)}) collective-permute-start(bf16[128,512]{1,0:T(8,128)(2,1)S(1)} %collective-permute-done.3.refs_4_), channel_id=1, source_target_pairs={{0,224},{32,0},{64,32},{96,64},{128,96},{160,128},{192,160},{224,1... | collective-permute-start | bytes 393224 | tf_op jit(solution)/shard_map/ppermute | solution.py:32
  33.5 7.0 %copy-start.15 = (bf16[128,512]{1,0:T(8,128)(2,1)}, bf16[128,512]{1,0:T(8,128)(2,1)S(1)}, u32[]{:S(2)}) copy-start(bf16[128,512]{1,0:T(8,128)(2,1)S(1)} %collective-permute-done.4.refs_5_) | copy-start | bytes 393220
  33.5 6.8 %collective-permute-start.6 = (bf16[128,512]{1,0:T(8,128)(2,1)S(1)}, bf16[128,512]{1,0:T(8,128)(2,1)S(1)}, u32[]{:S(2)}, u32[]{:S(2)}) collective-permute-start(bf16[128,512]{1,0:T(8,128)(2,1)S(1)} %collective-permute-done.4.refs_5_), channel_id=1, source_target_pairs={{0,32},{32,64},{64,96},{96,128},{128,160},{160,192},{192,224},{224... | collective-permute-start | bytes 393224 | tf_op jit(solution)/shard_map/ppermute | solution.py:32
  37.2 3.4 %copy-start.16 = (bf16[128,512]{1,0:T(8,128)(2,1)}, bf16[128,512]{1,0:T(8,128)(2,1)S(1)}, u32[]{:S(2)}) copy-start(bf16[128,512]{1,0:T(8,128)(2,1)S(1)} %collective-permute-done.5.refs_6_) | copy-start | bytes 393220
  40.4 0.7 copy-start.17
  40.4 0.8 copy-start.7
  40.4 0.8 copy-start.8
  41.2 0.7 copy-start.9
  84.0 4.8 %copy-start.1 = (bf16[4,4,128,256]{3,2,1,0:T(8,128)(2,1)S(1)}, bf16[4,4,128,256]{3,2,1,0:T(8,128)(2,1)}, u32[]{:S(2)}) copy-start(bf16[4,4,128,256]{3,2,1,0:T(8,128)(2,1)} %get-tuple-element.7) | copy-start | bytes 3145732
  84.0 3.8 %collective-permute-start.17 = (bf16[4,4,128,256]{3,2,1,0:T(8,128)(2,1)}, bf16[4,4,128,256]{3,2,1,0:T(8,128)(2,1)S(1)}, u32[]{:S(2)}, u32[]{:S(2)}) collective-permute-start(bf16[4,4,128,256]{3,2,1,0:T(8,128)(2,1)} %get-tuple-element.8), channel_id=1, source_target_pairs={{0,8},{8,0},{1,9},{9,1},{2,10},{10,2},{3,11},{11,3},{4,12},{12,4},... | collective-permute-start | bytes 3145736 | tf_op jit(solution)/shard_map/ppermute | solution.py:217
  84.1 26.8 %all-to-all-start.1 = ((bf16[8,128,256]{2,1,0:T(8,128)(2,1)}), bf16[8,128,256]{2,1,0:T(8,128)(2,1)S(1)}, u32[]{:S(2)}, u32[]{:S(2)}) async-start(bf16[8,128,256]{2,1,0:T(8,128)(2,1)} %get-tuple-element.6), calls=%async_computation.1 | async-start | bytes 1048576 | tf_op jit(solution)/shard_map/all_to_all | solution.py:243
  87.8 1.0 copy-start.2
  90.3 9.2 %collective-permute-start.18 = (bf16[4,128,256]{2,1,0:T(8,128)(2,1)S(1)}, bf16[4,128,256]{2,1,0:T(8,128)(2,1)S(1)}, u32[]{:S(2)}, u32[]{:S(2)}) collective-permute-start(bf16[4,128,256]{2,1,0:T(8,128)(2,1)S(1)} %get-tuple-element.13), channel_id=1, source_target_pairs={{0,2},{2,4},{4,6},{6,0},{1,3},{3,5},{5,7},{7,1},{8,10},{10,12},{12... | collective-permute-start | bytes 786440 | tf_op jit(solution)/shard_map/ppermute | solution.py:32
  91.7 10.7 %collective-permute-start.19 = (bf16[4,128,256]{2,1,0:T(8,128)(2,1)S(1)}, bf16[4,128,256]{2,1,0:T(8,128)(2,1)S(1)}, u32[]{:S(2)}, u32[]{:S(2)}) collective-permute-start(bf16[4,128,256]{2,1,0:T(8,128)(2,1)S(1)} %get-tuple-element.15), channel_id=1, source_target_pairs={{0,4},{2,6},{4,0},{6,2},{1,5},{3,7},{5,1},{7,3},{8,12},{10,14},{12... | collective-permute-start | bytes 786440 | tf_op jit(solution)/shard_map/ppermute | solution.py:32
  93.4 13.6 %collective-permute-start.20 = (bf16[4,128,256]{2,1,0:T(8,128)(2,1)S(1)}, bf16[4,128,256]{2,1,0:T(8,128)(2,1)S(1)}, u32[]{:S(2)}, u32[]{:S(2)}) collective-permute-start(bf16[4,128,256]{2,1,0:T(8,128)(2,1)S(1)} %get-tuple-element.14), channel_id=1, source_target_pairs={{0,6},{2,0},{4,2},{6,4},{1,7},{3,1},{5,3},{7,5},{8,14},{10,8},{12,... | collective-permute-start | bytes 786440 | tf_op jit(solution)/shard_map/ppermute | solution.py:32
  107.1 6.3 %collective-permute-start.21 = (bf16[128,256]{1,0:T(8,128)(2,1)S(1)}, bf16[128,256]{1,0:T(8,128)(2,1)S(1)}, u32[]{:S(2)}, u32[]{:S(2)}) collective-permute-start(bf16[128,256]{1,0:T(8,128)(2,1)S(1)} %get-tuple-element.16), channel_id=1, source_target_pairs={{0,1},{1,16},{16,17},{17,0},{2,3},{3,18},{18,19},{19,2},{4,5},{5,2... | collective-permute-start | bytes 196616 | tf_op jit(solution)/shard_map/ppermute | solution.py:32
  107.2 7.1 %collective-permute-start.22 = (bf16[128,256]{1,0:T(8,128)(2,1)S(1)}, bf16[128,256]{1,0:T(8,128)(2,1)S(1)}, u32[]{:S(2)}, u32[]{:S(2)}) collective-permute-start(bf16[128,256]{1,0:T(8,128)(2,1)S(1)} %get-tuple-element.18), channel_id=1, source_target_pairs={{0,16},{1,17},{16,0},{17,1},{2,18},{3,19},{18,2},{19,3},{4,20},{5,... | collective-permute-start | bytes 196616 | tf_op jit(solution)/shard_map/ppermute | solution.py:32
  110.9 4.3 %collective-permute-start.23 = (bf16[128,256]{1,0:T(8,128)(2,1)S(1)}, bf16[128,256]{1,0:T(8,128)(2,1)S(1)}, u32[]{:S(2)}, u32[]{:S(2)}) collective-permute-start(bf16[128,256]{1,0:T(8,128)(2,1)S(1)} %get-tuple-element.17), channel_id=1, source_target_pairs={{0,17},{1,0},{16,1},{17,16},{2,19},{3,2},{18,3},{19,18},{4,21},{5,... | collective-permute-start | bytes 196616 | tf_op jit(solution)/shard_map/ppermute | solution.py:32

commit v3 on v2

v3 whole, which is shorter than its diff:
```python
import functools
import math

import jax
import jax.numpy as jnp
from jax import lax
from jax.experimental import pallas as pl
from jax.experimental.pallas import tpu as pltpu
from jax.sharding import Mesh
from jax.sharding import PartitionSpec as P

bf16 = jnp.bfloat16
f32 = jnp.float32
i32 = jnp.int32
NZ, NXH, NCORE, NY, NXL = 8, 2, 2, 4, 2
NX = NXH * NXL
CH = 128
HD = 128
RUN = NXH * NCORE * CH
NRUN = NY * NXL
HALF = NRUN // 2
NBLK = 32
LOW = -1e30
SCALE = 1.0 / math.sqrt(HD)
FACTOR = SCALE * math.log2(math.e)
ROWS = ("z", "xh", "core")
COLS = ("y", "xl")
XAX = ("xh", "xl")


def shift(x, axis, size, by):
    return lax.ppermute(x, axis, [(i, (i + by) % size) for i in range(size)])


def nt(a, b):
    return lax.dot_general(a, b, (((1,), (1,)), ((), ())), preferred_element_type=f32)


def nn(a, b):
    return lax.dot_general(a, b, (((1,), (0,)), ((), ())), preferred_element_type=f32)


def load_all(ids, q_pieces, k_own, k_other, qs, kvs, sem):
    z, core = ids[0], ids[4]
    copies = []
    for r, by in enumerate(Q_SHIFTS):
        copies.append((q_pieces[r], qs.at[(z - by) % NZ]))
    for y in range(NY):
        for xh in range(NXH):
            for ref, pc in ((k_own, core), (k_other, 1 - core)):
                at = pl.multiple_of(xh * (NCORE * CH) + pc * CH, CH)
                copies.append(
                    (
                        ref.at[pl.ds(y * NX + xh * NXL, NXL)],
                        kvs.at[pl.ds(y * NXL, NXL), pl.ds(at, CH)],
                    )
                )
    copies = [pltpu.make_async_copy(a, b, sem.at[n]) for n, (a, b) in enumerate(copies)]
    for c in copies:
        c.start()
    return copies


Q_SHIFTS = (0, 1, -1, 2, -2, 3, -3, 4)
N_COPIES = NZ + NCORE * NY * NXH


def pack_kernel(q_ref, o_ref, k_ref, v_ref, qo_ref, kv_ref):
    qo_ref[:, : 2 * HD] = q_ref[...]
    qo_ref[:, 2 * HD :] = o_ref[...]
    for i in range(NY * NX):
        kv_ref[i, :, :HD] = k_ref[...]
        kv_ref[i, :, HD:] = v_ref[...]


def masks(qid_ref, kid_ref, hot, bias):
    lane = lax.broadcasted_iota(i32, (RUN, CH), 1)
    for b in range(HALF):
        col = jnp.broadcast_to(kid_ref[b : b + 1, :], (CH, RUN)).T
        hot[b] = jnp.where(lane == col, 1.0, 0.0).astype(bf16)
        hot[b + HALF] = jnp.where(lane == col + NBLK, 1.0, 0.0).astype(bf16)
    lane = lax.broadcasted_iota(i32, (CH, CH), 1)
    for a in range(HALF):
        col = jnp.broadcast_to(qid_ref[a], (CH, CH)).T
        bias[a] = jnp.where(lane <= col, 0.0, LOW).astype(bf16)
        seen = (lane < col) | (lane == col + NBLK)
        bias[a + HALF] = jnp.where(seen, 0.0, LOW).astype(bf16)


def both_heads(qo, base):
    return jnp.concatenate([qo[:, base : base + HD], qo[:, base + HD : base + 2 * HD]], axis=0)


def scores(k, q2, hot, bias):
    return nt(
        jnp.concatenate([k, hot], axis=1),
        jnp.concatenate([q2, jnp.concatenate([bias, bias], axis=0)], axis=1),
    )


def for_rest(mm, body):
    def visit(n, carry):
        a = n // HALF
        b = n % HALF

        @pl.when((b > a) & (mm[2, b] <= mm[1, a]))
        def _():
            body((a,), b)

        @pl.when((mm[2, b] <= mm[1, a]) & (mm[3, b] >= mm[0, a]))
        def _():
            body((a + HALF,), b + HALF)

        return carry

    lax.fori_loop(0, HALF * HALF, visit, 0)


def stats_kernel(ids, mm, qid_ref, kid_ref, *refs):
    q_pieces, k_own, k_other = refs[:NZ], refs[NZ], refs[NZ + 1]
    out_ref, qs, kvs, hot, bias, top, total, dot, sem = refs[NZ + 2 :]
    copies = load_all(ids, q_pieces, k_own, k_other, qs, kvs, sem)
    masks(qid_ref, kid_ref, hot, bias)
    for c in copies:
        c.wait()
    top[...] = jnp.full(top.shape, LOW, f32)
    total[...] = jnp.zeros(total.shape, f32)
    dot[...] = jnp.zeros(dot.shape, f32)

    def update(j, s, dp):
        old = top[j]
        new = jnp.maximum(old, jnp.max(s, axis=0, keepdims=True))
        p = jnp.exp2((s - new) * FACTOR)
        f = jnp.exp2((old - new) * FACTOR)
        top[j] = new
        total[j] = total[j] * f + jnp.sum(p, axis=0, keepdims=True)
        dot[j] = dot[j] * f + jnp.sum(p * dp, axis=0, keepdims=True)

    def body(chunks, slot):
        ss = [scores(kvs[slot, :, :HD], both_heads(qs[j], 0), hot[slot], bias[j]) for j in chunks]
        dps = [nt(kvs[slot, :, HD:], both_heads(qs[j], 2 * HD)) for j in chunks]
        for j, s, dp in zip(chunks, ss, dps):
            update(j, s, dp)

    for a in range(HALF):
        keys = kvs[: a + 1].reshape((a + 1) * RUN, 2 * HD)
        blocks = hot[: a + 1].reshape((a + 1) * RUN, CH)
        js = (a, a + HALF)
        ss = [scores(keys[:, :HD], both_heads(qs[j], 0), blocks, bias[j]) for j in js]
        dps = [nt(keys[:, HD:], both_heads(qs[j], 2 * HD)) for j in js]
        for j, s, dp in zip(js, ss, dps):
            update(j, s, dp)

    for_rest(mm, body)
    t = total[...]
    some = t > 0.0
    safe = jnp.where(some, t, 1.0)
    out_ref[:, 0:1, :] = jnp.where(some, top[...] * FACTOR + jnp.log2(safe), LOW)
    out_ref[:, 1:2, :] = dot[...] / safe


def grad_kernel(
    ids,
    mm,
    st_ref,
    qs,
    kvs,
    hot,
    bias,
    dq_ref,
    own_ref,
    other_ref,
    lse,
    delta,
    dq_acc,
    dkv_acc,
):
    parts = st_ref[:, :, 0:1, :]
    high = jnp.max(parts, axis=0)
    shares = jnp.exp2(parts - high[None])
    sums = jnp.sum(shares, axis=0)
    lse[...] = high + jnp.log2(sums)
    delta[...] = jnp.sum(shares * st_ref[:, :, 1:2, :], axis=0) / sums
    dkv_acc[HALF:] = jnp.zeros((HALF, RUN, 2 * HD), f32)

    def visit(js, keys, blocks):
        q2s = [both_heads(qs[j], 0) for j in js]
        o2s = [both_heads(qs[j], 2 * HD) for j in js]
        ss = [scores(keys[:, :HD], q2, blocks, bias[j]) for j, q2 in zip(js, q2s)]
        dps = [nt(keys[:, HD:], o2) for o2 in o2s]
        ps = [jnp.exp2(s * FACTOR - lse[j]) for j, s in zip(js, ss)]
        dss = [
            (p * (dp - delta[j]) * SCALE).astype(bf16) for j, p, dp in zip(js, ps, dps)
        ]
        q2, o2 = jnp.concatenate(q2s, axis=0), jnp.concatenate(o2s, axis=0)
        ds = jnp.concatenate(dss, axis=1)
        p = jnp.concatenate([p.astype(bf16) for p in ps], axis=1)
        dq = lax.dot_general(
            ds, keys[:, :HD], (((0,), (0,)), ((), ())), preferred_element_type=f32
        )
        return dq, nn(ds, q2), nn(p, o2)

    def body(chunks, slot):
        dq, dk, dv = visit(chunks, kvs[slot], hot[slot])
        for i, j in enumerate(chunks):
            dq_acc[j] += dq[2 * CH * i : 2 * CH * (i + 1)]
        dkv_acc[slot, :, :HD] += dk
        dkv_acc[slot, :, HD:] += dv

    for a in reversed(range(HALF)):
        runs = a + 1
        keys = kvs[:runs].reshape(runs * RUN, 2 * HD)
        blocks = hot[:runs].reshape(runs * RUN, CH)
        dq, dk, dv = visit((a, a + HALF), keys, blocks)
        dq_acc[a] = dq[: 2 * CH]
        dq_acc[a + HALF] = dq[2 * CH :]
        dk, dv = dk.reshape(runs, RUN, HD), dv.reshape(runs, RUN, HD)
        if runs == HALF:
            dkv_acc[:runs, :, :HD] = dk
            dkv_acc[:runs, :, HD:] = dv
        else:
            dkv_acc[:runs, :, :HD] += dk
            dkv_acc[:runs, :, HD:] += dv

    for_rest(mm, body)
    for j in range(NZ):
        t = dq_acc[j]
        dq_ref[j] = jnp.concatenate([t[:CH], t[CH:]], axis=1).astype(bf16)
    core = ids[4]
    for slot in range(NRUN):
        for xh in range(NXH):
            y, x = slot // NXL, xh * NXL + slot % NXL
            at = xh * NCORE * CH
            own_at = pl.multiple_of(at + core * CH, CH)
            other_at = pl.multiple_of(at + (1 - core) * CH, CH)
            own_ref[y, x] = dkv_acc[slot, pl.ds(own_at, CH), :].astype(bf16)
            other_ref[y, x] = dkv_acc[slot, pl.ds(other_at, CH), :].astype(bf16)


SMEM = pl.BlockSpec(memory_space=pltpu.SMEM)
VMEM = pl.BlockSpec(memory_space=pltpu.VMEM)
ANY = pl.BlockSpec(memory_space=pl.ANY)
DATA = VMEM
BIG = 44 << 20
LOADS = (
    jax.ShapeDtypeStruct((NZ, CH, 4 * HD), bf16),
    jax.ShapeDtypeStruct((NRUN, RUN, 2 * HD), bf16),
    jax.ShapeDtypeStruct((NRUN, RUN, CH), bf16),
    jax.ShapeDtypeStruct((NZ, CH, CH), bf16),
)
ROW = pltpu.VMEM((NZ, 1, 2 * CH), f32)
SEMS = pltpu.SemaphoreType.DMA((N_COPIES,))


def per_device(queries, key_states, value_states, grad_output, block_ids):
    z, xh, core = (lax.axis_index(n) for n in ROWS)
    y, xl = (lax.axis_index(n) for n in COLS)
    qo, kv = pl.pallas_call(
        pack_kernel,
        out_shape=(
            jax.ShapeDtypeStruct((CH, 4 * HD), bf16),
            jax.ShapeDtypeStruct((NY * NX, CH, 2 * HD), bf16),
        ),
        in_specs=[VMEM] * 4,
        out_specs=(VMEM, VMEM),
    )(queries, grad_output, key_states, value_states)

    def swap(t):
        return lax.ppermute(t, "core", [(0, 1), (1, 0)])

    k_own = lax.all_to_all(kv, ("y",) + XAX, 0, 0)
    pieces = {0: qo}
    for s in range(1, NZ // 2 + 1):
        pieces[s] = shift(pieces[s - 1], "z", NZ, 1)
        if s < NZ // 2:
            pieces[-s] = shift(pieces[1 - s], "z", NZ, -1)
    q_pieces = [pieces[s] for s in Q_SHIFTS]
    k_late, _, _ = lax.optimization_barrier((k_own, pieces[-3], pieces[3]))
    k_other = swap(k_late)

    qid = block_ids.reshape(HALF, NXH * NCORE * NY * NXL, CH)
    place = ((xh * NCORE + core) * NY + y) * NXL + xl
    qid = lax.dynamic_slice_in_dim(qid, place, 1, 1)
    kid = block_ids.reshape(HALF, NZ, RUN)
    kid = lax.dynamic_slice_in_dim(kid, z, 1, 1).reshape(HALF, RUN)
    mm = jnp.stack([qid[:, 0, 0], qid[:, 0, CH - 1], kid[:, 0], kid[:, RUN - 1]])
    ids = jnp.stack([z, y, xh, xl, core]).astype(i32)
    data = (*q_pieces, k_own, k_other)

    stats, *held = stats_call(ids, mm, qid, kid, data)
    stats = jnp.broadcast_to(stats[None], (NZ,) + stats.shape)
    stats = lax.all_to_all(stats, "z", 0, 0)
    dq, own, other = grad_call(ids, mm, stats, held)

    dq = lax.all_to_all(dq, "z", 0, 0)
    pair = (own.astype(f32) + swap(other).astype(f32)).astype(bf16)
    pair = scatter(pair, y, "y", NY)
    pair = scatter(pair, xh * NXL + xl, XAX, NX)
    dq = jnp.sum(dq.astype(f32), axis=0).astype(bf16)
    return dq, pair[:, :HD], pair[:, HD:]


def scatter(t, me, axis, size):
    def part(k):
        return lax.dynamic_index_in_dim(t, (me + k) % size, 0, keepdims=False)

    got = [part(0)] + [shift(part(k), axis, size, k) for k in range(1, size)]
    return sum(g.astype(f32) for g in got).astype(bf16)


def stats_call(ids, mm, qid, kid, data):
    return pl.pallas_call(
        stats_kernel,
        out_shape=(jax.ShapeDtypeStruct((NZ, 2, 2 * CH), f32),) + LOADS,
        in_specs=[SMEM, SMEM, VMEM, VMEM] + [DATA] * len(data),
        out_specs=(VMEM,) * 5,
        scratch_shapes=[ROW, ROW, ROW, SEMS],
        compiler_params=pltpu.CompilerParams(vmem_limit_bytes=BIG),
    )(ids, mm, qid, kid, *data)


def grad_call(ids, mm, stats, held):
    return pl.pallas_call(
        grad_kernel,
        out_shape=(
            jax.ShapeDtypeStruct((NZ, CH, 2 * HD), bf16),
            jax.ShapeDtypeStruct((NY, NX, CH, 2 * HD), bf16),
            jax.ShapeDtypeStruct((NY, NX, CH, 2 * HD), bf16),
        ),
        in_specs=[SMEM, SMEM] + [VMEM] * 5,
        out_specs=(VMEM, VMEM, VMEM),
        scratch_shapes=[
            ROW,
            ROW,
            pltpu.VMEM((NZ, 2 * CH, HD), f32),
            pltpu.VMEM((NRUN, RUN, 2 * HD), f32),
        ],
        compiler_params=pltpu.CompilerParams(vmem_limit_bytes=BIG),
    )(ids, mm, stats, *held)


def solution(mesh):
    fine = Mesh(mesh.devices.reshape(NZ, NXH, NCORE, NY, NXL), ROWS + COLS)
    by_row = P(ROWS + COLS, None)
    by_col = P(COLS + ROWS, None)
    return jax.shard_map(
        per_device,
        mesh=fine,
        in_specs=(by_row, by_col, by_col, by_row, P()),
        out_specs=(by_row, by_col, by_col),
        check_vma=False,
    )
```

time: 117 us -> 107 us (0.915)
  local copies, waits for them, and re-layouts: 11.2 us -> 1.32 us
  waiting for transfers between devices: 24.8 us -> 29.8 us
  Pallas kernels: 29.1 us -> 25.8 us
  starting transfers between devices: 34.5 us -> 32.9 us
    ppermute x19 -> x13, starting transfers between devices: 30.6 us -> 21.9 us  [shift(): return lax.ppermute(x, axis, [(i, (i + by) % size) for i in range(size)])]
    all_to_all x0 -> x1, starting transfers between devices: none -> 7.52 us  [per_device(): k_own = lax.all_to_all(kv, ('y',) + XAX, 0, 0)]
    ppermute x19 -> x13, waiting for transfers between devices: 24.8 us -> 29.8 us  [shift(): return lax.ppermute(x, axis, [(i, (i + by) % size) for i in range(size)])]
    pallas_call x1, Pallas kernels: 17.5 us -> 13.1 us  [grad_call(): pl.pallas_call(grad_kernel, out_shape=(jax.ShapeDtypeStruct((NZ, CH, 2 *...]
    unnamed x41 -> x5, local copies, waits for them, and re-layouts: 4.04 us -> 0.01 us
    concatenate x2 -> x0, local copies, waits for them, and re-layouts: 1.61 us -> none  [the longest x1 0.84 us: per_device(): qo = jnp.concatenate([queries, grad_output], axis=1)]
    dynamic_slice x1, local copies, waits for them, and re-layouts: 1.35 us -> 0.01 us  [per_device(): qid = lax.dynamic_slice_in_dim(qid, place, 1, 1)]
    pallas_call x1 -> x2, Pallas kernels: 11.5 us -> 12.6 us  [the longest x1 10.6 us: stats_call(): pl.pallas_call(stats_kernel, out_shape=(jax.ShapeDtypeStruct((NZ, 2, 2 *...]
  transfers between devices with their start and end apart: 25 -> 17, of which waited for: 10 -> 9; matrix products, arithmetic and copies ran while one was open for 8% -> 3% of each run, Pallas kernels for 0% -> 0%
where the time goes in v3:
time: 107 us; the launch traced here: 106 us
  starting transfers between devices  32.9 us (31%)
  waiting for transfers between devices  29.8 us (28%)
  Pallas kernels  25.8 us (24%)
  blocking collectives  12.9 us (12%)
  other arithmetic  2.42 us (2%)
  local copies, waits for them, and re-layouts  1.32 us (1%)
    ppermute x13, waiting for transfers between devices, shift(): return lax.ppermute(x, axis, [(i, (i + by) % size) for i in range(size)])  29.8 us
    ppermute x13, starting transfers between devices, shift(): return lax.ppermute(x, axis, [(i, (i + by) % size) for i in range(size)])  21.9 us
    pallas_call x1, Pallas kernels, grad_call(): pl.pallas_call(grad_kernel, out_shape=(jax.ShapeDtypeStruct((NZ, CH, 2 *...  13.1 us
    all_to_all x1, blocking collectives, per_device(): stats = lax.all_to_all(stats, 'z', 0, 0)  12.9 us
    pallas_call x1, Pallas kernels, stats_call(): pl.pallas_call(stats_kernel, out_shape=(jax.ShapeDtypeStruct((NZ, 2, 2 *...  10.6 us
    all_to_all x1, starting transfers between devices, per_device(): k_own = lax.all_to_all(kv, ('y',) + XAX, 0, 0)  7.52 us
    all_to_all x1, starting transfers between devices, per_device(): dq = lax.all_to_all(dq, 'z', 0, 0)  3.49 us
  transfers between devices with their start and end apart: 17, of which 9 were waited for; matrix products, arithmetic and copies ran while one was open for 3% of the time, Pallas kernels for 0%

profile of v3, /device:TPU:8, one launch (start us, length us, event | category | flops | bytes accessed | tf_op | source)
XLA Modules:
  0.0 105.9 jit_solution(11090047847125046717)
XLA Ops:
  0.6 0.0 copy-start.1
  0.6 2.0 %shard_map.76 = (bf16[128,512]{1,0:T(8,128)(2,1)}, bf16[16,128,256]{2,1,0:T(8,128)(2,1)}) custom-call(bf16[128,256]{1,0:T(8,128)(2,1)} %q_ref.1, bf16[128,256]{1,0:T(8,128)(2,1)} %o_ref.1, bf16[128,128]{1,0:T(8,128)(2,1)} %k_ref.1, bf16[128,128]{1,0:T(8,128)(2,1)} %v_ref.1), custom_call_target="tpu_custom_call" | custom-call | tf_op jit(solution)/shard_map/pallas_call | solution.py:258
  2.7 0.0 copy-start
  2.7 7.5 %all-to-all-start = ((bf16[16,128,256]{2,1,0:T(8,128)(2,1)}), bf16[16,128,256]{2,1,0:T(8,128)(2,1)S(1)}, u32[]{:S(2)}, u32[]{:S(2)}) async-start(bf16[16,128,256]{2,1,0:T(8,128)(2,1)} %get-tuple-element.15), calls=%async_computation | async-start | bytes 2097152 | tf_op jit(solution)/shard_map/all_to_all | solution.py:271
  10.2 0.0 copy-done
  10.2 2.0 %collective-permute-start = (bf16[128,512]{1,0:T(8,128)(2,1)S(1)}, bf16[128,512]{1,0:T(8,128)(2,1)S(1)}, u32[]{:S(2)}, u32[]{:S(2)}) collective-permute-start(bf16[128,512]{1,0:T(8,128)(2,1)S(1)} %copy-done), channel_id=1, source_target_pairs={{0,32},{32,64},{64,96},{96,128},{128,160},{160,192},{192,224},{224... | collective-permute-start | bytes 393224 | tf_op jit(solution)/shard_map/ppermute | solution.py:32
  12.2 4.0 %collective-permute-start.1 = (bf16[128,512]{1,0:T(8,128)(2,1)S(1)}, bf16[128,512]{1,0:T(8,128)(2,1)S(1)}, u32[]{:S(2)}, u32[]{:S(2)}) collective-permute-start(bf16[128,512]{1,0:T(8,128)(2,1)S(1)} %copy-done), channel_id=1, source_target_pairs={{0,224},{32,0},{64,32},{96,64},{128,96},{160,128},{192,160},{224,1... | collective-permute-start | bytes 393224 | tf_op jit(solution)/shard_map/ppermute | solution.py:32
  16.2 2.9 %collective-permute-done.refs_1_ = bf16[128,512]{1,0:T(8,128)(2,1)S(1)} collective-permute-done((bf16[128,512]{1,0:T(8,128)(2,1)S(1)}, bf16[128,512]{1,0:T(8,128)(2,1)S(1)}, u32[]{:S(2)}, u32[]{:S(2)}) %collective-permute-start) | collective-permute-done | bytes 131104 | tf_op jit(solution)/shard_map/ppermute | solution.py:32
  19.1 0.0 collective-permute-start.2
  19.1 0.0 collective-permute-done.1.refs_2_
  19.1 3.3 %collective-permute-start.3 = (bf16[128,512]{1,0:T(8,128)(2,1)S(1)}, bf16[128,512]{1,0:T(8,128)(2,1)S(1)}, u32[]{:S(2)}, u32[]{:S(2)}) collective-permute-start(bf16[128,512]{1,0:T(8,128)(2,1)S(1)} %collective-permute-done.1.refs_2_), channel_id=1, source_target_pairs={{0,224},{32,0},{64,32},{96,64},{128,96},{160,128},{192,160},{224,1... | collective-permute-start | bytes 393224 | tf_op jit(solution)/shard_map/ppermute | solution.py:32
  22.4 2.9 %collective-permute-done.2.refs_3_ = bf16[128,512]{1,0:T(8,128)(2,1)S(1)} collective-permute-done((bf16[128,512]{1,0:T(8,128)(2,1)S(1)}, bf16[128,512]{1,0:T(8,128)(2,1)S(1)}, u32[]{:S(2)}, u32[]{:S(2)}) %collective-permute-start.2) | collective-permute-done | bytes 131104 | tf_op jit(solution)/shard_map/ppermute | solution.py:32
  25.3 0.0 collective-permute-start.4
  25.3 0.0 collective-permute-done.3.refs_4_
  25.3 3.3 %collective-permute-start.5 = (bf16[128,512]{1,0:T(8,128)(2,1)S(1)}, bf16[128,512]{1,0:T(8,128)(2,1)S(1)}, u32[]{:S(2)}, u32[]{:S(2)}) collective-permute-start(bf16[128,512]{1,0:T(8,128)(2,1)S(1)} %collective-permute-done.3.refs_4_), channel_id=1, source_target_pairs={{0,224},{32,0},{64,32},{96,64},{128,96},{160,128},{192,160},{224,1... | collective-permute-start | bytes 393224 | tf_op jit(solution)/shard_map/ppermute | solution.py:32
  28.6 2.9 %collective-permute-done.4.refs_5_ = bf16[128,512]{1,0:T(8,128)(2,1)S(1)} collective-permute-done((bf16[128,512]{1,0:T(8,128)(2,1)S(1)}, bf16[128,512]{1,0:T(8,128)(2,1)S(1)}, u32[]{:S(2)}, u32[]{:S(2)}) %collective-permute-start.4) | collective-permute-done | bytes 131104 | tf_op jit(solution)/shard_map/ppermute | solution.py:32
  31.4 0.0 collective-permute-done.5.refs_6_
  31.5 0.0 all-to-all-done.refs_8_
  31.5 0.0 collective-permute-start.7
  31.5 0.0 copy-done.1
  31.5 0.2 slice_reduce_fusion.1
  31.7 0.1 collective-permute-start.6
  31.8 0.1 stack.26.ids
  31.9 0.3 fusion.6
  32.2 7.1 %collective-permute-done.6.refs_7_ = bf16[128,512]{1,0:T(8,128)(2,1)S(1)} collective-permute-done((bf16[128,512]{1,0:T(8,128)(2,1)S(1)}, bf16[128,512]{1,0:T(8,128)(2,1)S(1)}, u32[]{:S(2)}, u32[]{:S(2)}) %collective-permute-start.6) | collective-permute-done | bytes 131104 | tf_op jit(solution)/shard_map/ppermute | solution.py:32
  39.3 0.0 collective-permute-done.7.refs_9_
  39.3 10.6 %shard_map.77 = (f32[8,2,256]{2,1,0:T(2,128)S(1)}, bf16[8,128,512]{2,1,0:T(8,128)(2,1)S(1)}, bf16[8,512,256]{2,1,0:T(8,128)(2,1)S(1)}, bf16[8,512,128]{2,1,0:T(8,128)(2,1)S(1)}, bf16[8,128,128]{2,1,0:T(8,128)(2,1)S(1)}) custom-call(s32[5]{0:T(128)S(1)} %stack.26.ids, s32[4,4]{1,0:T(4,128)S(1)} %pad_add_fusion.mm, ...), custom_call_target="tpu_custom_call" | custom-call | tf_op jit(solution)/shard_map/pallas_call | solution.py:312
  49.9 12.9 %all_to_all.15.st_ref = f32[8,8,2,256]{3,2,1,0:T(2,128)S(1)} all-to-all(f32[8,8,2,256]{3,2,1,0:T(2,128)S(1)} %broadcast_in_dim.2), channel_id=1, replica_groups=mesh['z'=8,'xh'=2,'core'=2,'y'=4,'xl'=2] {'z'}, dimensions={0} | all-to-all | bytes 262144 | tf_op jit(solution)/shard_map/all_to_all | solution.py:292
  62.8 13.1 %shard_map.78 = (bf16[8,128,256]{2,1,0:T(8,128)(2,1)}, bf16[4,4,128,256]{3,2,1,0:T(8,128)(2,1)S(1)}, bf16[4,4,128,256]{3,2,1,0:T(8,128)(2,1)S(1)}) custom-call(s32[5]{0:T(128)S(1)} %stack.26.ids, s32[4,4]{1,0:T(4,128)S(1)} %pad_add_fusion.mm, f32[8,8,2,256]{3,2,1,0:T(2,128)S(1)} %all_to_all.15.st_ref, bf16[8,128,512]{2,1,0:T(8,128)(2,1)S(1)} %get-tuple-element.18.qs, ...), custom_call_target="tpu_custom_call" | custom-call | tf_op jit(solution)/shard_map/pallas_call | solution.py:323
  75.9 0.0 collective-permute-start.8
  75.9 3.5 %all-to-all-start.2 = ((bf16[8,128,256]{2,1,0:T(8,128)(2,1)}), bf16[8,128,256]{2,1,0:T(8,128)(2,1)S(1)}, u32[]{:S(2)}, u32[]{:S(2)}) async-start(bf16[8,128,256]{2,1,0:T(8,128)(2,1)} %get-tuple-element.22), calls=%async_computation.2 | async-start | bytes 1048576 | tf_op jit(solution)/shard_map/all_to_all | solution.py:295
  79.4 0.0 collective-permute-done.8
  79.4 1.5 %add_convert_fusion = bf16[4,4,128,256]{3,2,1,0:T(8,128)(2,1)S(1)} fusion(bf16[4,4,128,256]{3,2,1,0:T(8,128)(2,1)} %collective-permute-done.8, bf16[4,4,128,256]{3,2,1,0:T(8,128)(2,1)S(1)} %get-tuple-element.23), kind=kLoop, calls=%fused_computation | loop fusion | flops 2097152 | bytes 3145728 | tf_op jit(solution)/shard_map/convert_element_type | solution.py:296
  80.9 0.1 dynamic-slice_bitcast_fusion.2
  81.0 2.2 %collective-permute-start.10 = (bf16[4,128,256]{2,1,0:T(8,128)(2,1)S(1)}, bf16[4,128,256]{2,1,0:T(8,128)(2,1)S(1)}, u32[]{:S(2)}, u32[]{:S(2)}) collective-permute-start(bf16[4,128,256]{2,1,0:T(8,128)(2,1)S(1)} %get-tuple-element.31), channel_id=1, source_target_pairs={{0,4},{2,6},{4,0},{6,2},{1,5},{3,7},{5,1},{7,3},{8,12},{10,14},{12... | collective-permute-start | bytes 786440 | tf_op jit(solution)/shard_map/ppermute | solution.py:32
  83.2 2.2 %collective-permute-start.11 = (bf16[4,128,256]{2,1,0:T(8,128)(2,1)S(1)}, bf16[4,128,256]{2,1,0:T(8,128)(2,1)S(1)}, u32[]{:S(2)}, u32[]{:S(2)}) collective-permute-start(bf16[4,128,256]{2,1,0:T(8,128)(2,1)S(1)} %get-tuple-element.30), channel_id=1, source_target_pairs={{0,6},{2,0},{4,2},{6,4},{1,7},{3,1},{5,3},{7,5},{8,14},{10,8},{12,... | collective-permute-start | bytes 786440 | tf_op jit(solution)/shard_map/ppermute | solution.py:32
  85.4 0.0 collective-permute-start.9
  85.4 6.4 %collective-permute-done.10 = bf16[4,128,256]{2,1,0:T(8,128)(2,1)S(1)} collective-permute-done((bf16[4,128,256]{2,1,0:T(8,128)(2,1)S(1)}, bf16[4,128,256]{2,1,0:T(8,128)(2,1)S(1)}, u32[]{:S(2)}, u32[]{:S(2)}) %collective-permute-start.10) | collective-permute-done | bytes 262176 | tf_op jit(solution)/shard_map/ppermute | solution.py:32
  91.8 5.2 %collective-permute-done.11 = bf16[4,128,256]{2,1,0:T(8,128)(2,1)S(1)} collective-permute-done((bf16[4,128,256]{2,1,0:T(8,128)(2,1)S(1)}, bf16[4,128,256]{2,1,0:T(8,128)(2,1)S(1)}, u32[]{:S(2)}, u32[]{:S(2)}) %collective-permute-start.11) | collective-permute-done | bytes 262176 | tf_op jit(solution)/shard_map/ppermute | solution.py:32
  96.9 0.8 collective-permute-done.9
  97.7 0.1 fusion.2
  97.9 1.5 %collective-permute-start.12 = (bf16[128,256]{1,0:T(8,128)(2,1)S(1)}, bf16[128,256]{1,0:T(8,128)(2,1)S(1)}, u32[]{:S(2)}, u32[]{:S(2)}) collective-permute-start(bf16[128,256]{1,0:T(8,128)(2,1)S(1)} %get-tuple-element.32), channel_id=1, source_target_pairs={{0,1},{1,16},{16,17},{17,0},{2,3},{3,18},{18,19},{19,2},{4,5},{5,2... | collective-permute-start | bytes 196616 | tf_op jit(solution)/shard_map/ppermute | solution.py:32
  99.4 1.3 %collective-permute-start.13 = (bf16[128,256]{1,0:T(8,128)(2,1)S(1)}, bf16[128,256]{1,0:T(8,128)(2,1)S(1)}, u32[]{:S(2)}, u32[]{:S(2)}) collective-permute-start(bf16[128,256]{1,0:T(8,128)(2,1)S(1)} %get-tuple-element.34), channel_id=1, source_target_pairs={{0,16},{1,17},{16,0},{17,1},{2,18},{3,19},{18,2},{19,3},{4,20},{5,... | collective-permute-start | bytes 196616 | tf_op jit(solution)/shard_map/ppermute | solution.py:32
  100.7 2.0 %collective-permute-start.14 = (bf16[128,256]{1,0:T(8,128)(2,1)S(1)}, bf16[128,256]{1,0:T(8,128)(2,1)S(1)}, u32[]{:S(2)}, u32[]{:S(2)}) collective-permute-start(bf16[128,256]{1,0:T(8,128)(2,1)S(1)} %get-tuple-element.33), channel_id=1, source_target_pairs={{0,17},{1,0},{16,1},{17,16},{2,19},{3,2},{18,3},{19,18},{4,21},{5,... | collective-permute-start | bytes 196616 | tf_op jit(solution)/shard_map/ppermute | solution.py:32
  102.7 0.0 all-to-all-done.2
  102.7 0.7 reduce_sum.12
  103.4 0.8 collective-permute-done.12
  104.1 1.1 collective-permute-done.13
  105.2 0.0 collective-permute-done.14
  105.2 0.6 fusion.8
  (8 shorter events, 0.2 us)
Async XLA Ops:
  0.6 30.9 %copy-start.1 = (s32[16384]{0:T(1024)S(1)}, s32[16384]{0:T(1024)}, u32[]{:S(2)}) copy-start(s32[16384]{0:T(1024)} %param.9) | copy-start | bytes 196612
  2.7 7.5 %copy-start = (bf16[128,512]{1,0:T(8,128)(2,1)S(1)}, bf16[128,512]{1,0:T(8,128)(2,1)}, u32[]{:S(2)}) copy-start(bf16[128,512]{1,0:T(8,128)(2,1)} %get-tuple-element.14.refs_0_) | copy-start | bytes 393220
  2.7 28.8 %all-to-all-start = ((bf16[16,128,256]{2,1,0:T(8,128)(2,1)}), bf16[16,128,256]{2,1,0:T(8,128)(2,1)S(1)}, u32[]{:S(2)}, u32[]{:S(2)}) async-start(bf16[16,128,256]{2,1,0:T(8,128)(2,1)} %get-tuple-element.15), calls=%async_computation | async-start | bytes 2097152 | tf_op jit(solution)/shard_map/all_to_all | solution.py:271
  10.2 8.9 %collective-permute-start = (bf16[128,512]{1,0:T(8,128)(2,1)S(1)}, bf16[128,512]{1,0:T(8,128)(2,1)S(1)}, u32[]{:S(2)}, u32[]{:S(2)}) collective-permute-start(bf16[128,512]{1,0:T(8,128)(2,1)S(1)} %copy-done), channel_id=1, source_target_pairs={{0,32},{32,64},{64,96},{96,128},{128,160},{160,192},{192,224},{224... | collective-permute-start | bytes 393224 | tf_op jit(solution)/shard_map/ppermute | solution.py:32
  12.2 6.9 %collective-permute-start.1 = (bf16[128,512]{1,0:T(8,128)(2,1)S(1)}, bf16[128,512]{1,0:T(8,128)(2,1)S(1)}, u32[]{:S(2)}, u32[]{:S(2)}) collective-permute-start(bf16[128,512]{1,0:T(8,128)(2,1)S(1)} %copy-done), channel_id=1, source_target_pairs={{0,224},{32,0},{64,32},{96,64},{128,96},{160,128},{192,160},{224,1... | collective-permute-start | bytes 393224 | tf_op jit(solution)/shard_map/ppermute | solution.py:32
  19.1 6.2 %collective-permute-start.2 = (bf16[128,512]{1,0:T(8,128)(2,1)S(1)}, bf16[128,512]{1,0:T(8,128)(2,1)S(1)}, u32[]{:S(2)}, u32[]{:S(2)}) collective-permute-start(bf16[128,512]{1,0:T(8,128)(2,1)S(1)} %collective-permute-done.refs_1_), channel_id=1, source_target_pairs={{0,32},{32,64},{64,96},{96,128},{128,160},{160,192},{192,224},{224... | collective-permute-start | bytes 393224 | tf_op jit(solution)/shard_map/ppermute | solution.py:32
  19.1 6.2 %collective-permute-start.3 = (bf16[128,512]{1,0:T(8,128)(2,1)S(1)}, bf16[128,512]{1,0:T(8,128)(2,1)S(1)}, u32[]{:S(2)}, u32[]{:S(2)}) collective-permute-start(bf16[128,512]{1,0:T(8,128)(2,1)S(1)} %collective-permute-done.1.refs_2_), channel_id=1, source_target_pairs={{0,224},{32,0},{64,32},{96,64},{128,96},{160,128},{192,160},{224,1... | collective-permute-start | bytes 393224 | tf_op jit(solution)/shard_map/ppermute | solution.py:32
  25.3 6.2 %collective-permute-start.4 = (bf16[128,512]{1,0:T(8,128)(2,1)S(1)}, bf16[128,512]{1,0:T(8,128)(2,1)S(1)}, u32[]{:S(2)}, u32[]{:S(2)}) collective-permute-start(bf16[128,512]{1,0:T(8,128)(2,1)S(1)} %collective-permute-done.2.refs_3_), channel_id=1, source_target_pairs={{0,32},{32,64},{64,96},{96,128},{128,160},{160,192},{192,224},{224... | collective-permute-start | bytes 393224 | tf_op jit(solution)/shard_map/ppermute | solution.py:32
  25.3 6.2 %collective-permute-start.5 = (bf16[128,512]{1,0:T(8,128)(2,1)S(1)}, bf16[128,512]{1,0:T(8,128)(2,1)S(1)}, u32[]{:S(2)}, u32[]{:S(2)}) collective-permute-start(bf16[128,512]{1,0:T(8,128)(2,1)S(1)} %collective-permute-done.3.refs_4_), channel_id=1, source_target_pairs={{0,224},{32,0},{64,32},{96,64},{128,96},{160,128},{192,160},{224,1... | collective-permute-start | bytes 393224 | tf_op jit(solution)/shard_map/ppermute | solution.py:32
  31.5 7.8 %collective-permute-start.7 = (bf16[16,128,256]{2,1,0:T(8,128)(2,1)S(1)}, bf16[16,128,256]{2,1,0:T(8,128)(2,1)S(1)}, u32[]{:S(2)}, u32[]{:S(2)}) collective-permute-start(bf16[16,128,256]{2,1,0:T(8,128)(2,1)S(1)} %all-to-all-done.refs_8_), channel_id=1, source_target_pairs={{0,8},{8,0},{1,9},{9,1},{2,10},{10,2},{3,11},{11,3},{4,12},{12,4},... | collective-permute-start | bytes 3145736 | tf_op jit(solution)/shard_map/ppermute | solution.py:269
  31.7 7.5 %collective-permute-start.6 = (bf16[128,512]{1,0:T(8,128)(2,1)S(1)}, bf16[128,512]{1,0:T(8,128)(2,1)S(1)}, u32[]{:S(2)}, u32[]{:S(2)}) collective-permute-start(bf16[128,512]{1,0:T(8,128)(2,1)S(1)} %collective-permute-done.4.refs_5_), channel_id=1, source_target_pairs={{0,32},{32,64},{64,96},{96,128},{128,160},{160,192},{192,224},{224... | collective-permute-start | bytes 393224 | tf_op jit(solution)/shard_map/ppermute | solution.py:32
  75.9 3.5 %collective-permute-start.8 = (bf16[4,4,128,256]{3,2,1,0:T(8,128)(2,1)S(1)}, bf16[4,4,128,256]{3,2,1,0:T(8,128)(2,1)}, u32[]{:S(2)}, u32[]{:S(2)}) collective-permute-start(bf16[4,4,128,256]{3,2,1,0:T(8,128)(2,1)S(1)} %get-tuple-element.24), channel_id=1, source_target_pairs={{0,8},{8,0},{1,9},{9,1},{2,10},{10,2},{3,11},{11,3},{4,12},{12,4},... | collective-permute-start | bytes 3145736 | tf_op jit(solution)/shard_map/ppermute | solution.py:269
  75.9 26.8 %all-to-all-start.2 = ((bf16[8,128,256]{2,1,0:T(8,128)(2,1)}), bf16[8,128,256]{2,1,0:T(8,128)(2,1)S(1)}, u32[]{:S(2)}, u32[]{:S(2)}) async-start(bf16[8,128,256]{2,1,0:T(8,128)(2,1)} %get-tuple-element.22), calls=%async_computation.2 | async-start | bytes 1048576 | tf_op jit(solution)/shard_map/all_to_all | solution.py:295
  81.0 10.7 %collective-permute-start.10 = (bf16[4,128,256]{2,1,0:T(8,128)(2,1)S(1)}, bf16[4,128,256]{2,1,0:T(8,128)(2,1)S(1)}, u32[]{:S(2)}, u32[]{:S(2)}) collective-permute-start(bf16[4,128,256]{2,1,0:T(8,128)(2,1)S(1)} %get-tuple-element.31), channel_id=1, source_target_pairs={{0,4},{2,6},{4,0},{6,2},{1,5},{3,7},{5,1},{7,3},{8,12},{10,14},{12... | collective-permute-start | bytes 786440 | tf_op jit(solution)/shard_map/ppermute | solution.py:32
  83.2 13.7 %collective-permute-start.11 = (bf16[4,128,256]{2,1,0:T(8,128)(2,1)S(1)}, bf16[4,128,256]{2,1,0:T(8,128)(2,1)S(1)}, u32[]{:S(2)}, u32[]{:S(2)}) collective-permute-start(bf16[4,128,256]{2,1,0:T(8,128)(2,1)S(1)} %get-tuple-element.30), channel_id=1, source_target_pairs={{0,6},{2,0},{4,2},{6,4},{1,7},{3,1},{5,3},{7,5},{8,14},{10,8},{12,... | collective-permute-start | bytes 786440 | tf_op jit(solution)/shard_map/ppermute | solution.py:32
  85.4 12.4 %collective-permute-start.9 = (bf16[4,128,256]{2,1,0:T(8,128)(2,1)S(1)}, bf16[4,128,256]{2,1,0:T(8,128)(2,1)S(1)}, u32[]{:S(2)}, u32[]{:S(2)}) collective-permute-start(bf16[4,128,256]{2,1,0:T(8,128)(2,1)S(1)} %get-tuple-element.29), channel_id=1, source_target_pairs={{0,2},{2,4},{4,6},{6,0},{1,3},{3,5},{5,7},{7,1},{8,10},{10,12},{12... | collective-permute-start | bytes 786440 | tf_op jit(solution)/shard_map/ppermute | solution.py:32
  97.9 6.3 %collective-permute-start.12 = (bf16[128,256]{1,0:T(8,128)(2,1)S(1)}, bf16[128,256]{1,0:T(8,128)(2,1)S(1)}, u32[]{:S(2)}, u32[]{:S(2)}) collective-permute-start(bf16[128,256]{1,0:T(8,128)(2,1)S(1)} %get-tuple-element.32), channel_id=1, source_target_pairs={{0,1},{1,16},{16,17},{17,0},{2,3},{3,18},{18,19},{19,2},{4,5},{5,2... | collective-permute-start | bytes 196616 | tf_op jit(solution)/shard_map/ppermute | solution.py:32
  99.4 5.8 %collective-permute-start.13 = (bf16[128,256]{1,0:T(8,128)(2,1)S(1)}, bf16[128,256]{1,0:T(8,128)(2,1)S(1)}, u32[]{:S(2)}, u32[]{:S(2)}) collective-permute-start(bf16[128,256]{1,0:T(8,128)(2,1)S(1)} %get-tuple-element.34), channel_id=1, source_target_pairs={{0,16},{1,17},{16,0},{17,1},{2,18},{3,19},{18,2},{19,3},{4,20},{5,... | collective-permute-start | bytes 196616 | tf_op jit(solution)/shard_map/ppermute | solution.py:32
  100.7 4.5 %collective-permute-start.14 = (bf16[128,256]{1,0:T(8,128)(2,1)S(1)}, bf16[128,256]{1,0:T(8,128)(2,1)S(1)}, u32[]{:S(2)}, u32[]{:S(2)}) collective-permute-start(bf16[128,256]{1,0:T(8,128)(2,1)S(1)} %get-tuple-element.33), channel_id=1, source_target_pairs={{0,17},{1,0},{16,1},{17,16},{2,19},{3,2},{18,3},{19,18},{4,21},{5,... | collective-permute-start | bytes 196616 | tf_op jit(solution)/shard_map/ppermute | solution.py:32

commit v4 on v3

--- a/solution.py
+++ b/solution.py
@@ -99,21 +99,25 @@
 
 
 def for_rest(mm, body):
-    def visit(n, carry):
-        a = n // HALF
-        b = n % HALF
-
-        @pl.when((b > a) & (mm[2, b] <= mm[1, a]))
-        def _():
-            body((a,), b)
-
-        @pl.when((mm[2, b] <= mm[1, a]) & (mm[3, b] >= mm[0, a]))
-        def _():
-            body((a + HALF,), b + HALF)
-
-        return carry
-
-    lax.fori_loop(0, HALF * HALF, visit, 0)
+    def shared(a, b):
+        return (mm[2, b] <= mm[1, a]) & (mm[3, b] >= mm[0, a])
+
+    def any_of(flags):
+        return functools.reduce(jnp.logical_or, flags)
+
+    steps = range(HALF - 1)
+
+    @pl.when(any_of([shared(a, a) for a in range(HALF)]))
+    def _():
+        body([(a + HALF, a + HALF) for a in range(HALF)])
+
+    @pl.when(any_of([shared(a, a + 1) for a in steps]))
+    def _():
+        body([(a, a + 1) for a in steps] + [(a + HALF, a + HALF + 1) for a in steps])
+
+    @pl.when(any_of([shared(a + 1, a) for a in steps]))
+    def _():
+        body([(a + HALF + 1, a + HALF) for a in steps])
 
 
 def stats_kernel(ids, mm, qid_ref, kid_ref, *refs):
@@ -136,10 +140,10 @@
         total[j] = total[j] * f + jnp.sum(p, axis=0, keepdims=True)
         dot[j] = dot[j] * f + jnp.sum(p * dp, axis=0, keepdims=True)
 
-    def body(chunks, slot):
-        ss = [scores(kvs[slot, :, :HD], both_heads(qs[j], 0), hot[slot], bias[j]) for j in chunks]
-        dps = [nt(kvs[slot, :, HD:], both_heads(qs[j], 2 * HD)) for j in chunks]
-        for j, s, dp in zip(chunks, ss, dps):
+    def body(pairs):
+        ss = [scores(kvs[b, :, :HD], both_heads(qs[j], 0), hot[b], bias[j]) for j, b in pairs]
+        dps = [nt(kvs[b, :, HD:], both_heads(qs[j], 2 * HD)) for j, b in pairs]
+        for (j, _), s, dp in zip(pairs, ss, dps):
             update(j, s, dp)
 
     for a in range(HALF):
@@ -183,29 +187,32 @@
     delta[...] = jnp.sum(shares * st_ref[:, :, 1:2, :], axis=0) / sums
     dkv_acc[HALF:] = jnp.zeros((HALF, RUN, 2 * HD), f32)
 
-    def visit(js, keys, blocks):
-        q2s = [both_heads(qs[j], 0) for j in js]
-        o2s = [both_heads(qs[j], 2 * HD) for j in js]
-        ss = [scores(keys[:, :HD], q2, blocks, bias[j]) for j, q2 in zip(js, q2s)]
-        dps = [nt(keys[:, HD:], o2) for o2 in o2s]
-        ps = [jnp.exp2(s * FACTOR - lse[j]) for j, s in zip(js, ss)]
-        dss = [
-            (p * (dp - delta[j]) * SCALE).astype(bf16) for j, p, dp in zip(js, ps, dps)
-        ]
-        q2, o2 = jnp.concatenate(q2s, axis=0), jnp.concatenate(o2s, axis=0)
-        ds = jnp.concatenate(dss, axis=1)
-        p = jnp.concatenate([p.astype(bf16) for p in ps], axis=1)
-        dq = lax.dot_general(
+    def start(j, keys, blocks):
+        q2 = both_heads(qs[j], 0)
+        o2 = both_heads(qs[j], 2 * HD)
+        s = scores(keys[:, :HD], q2, blocks, bias[j])
+        dp = nt(keys[:, HD:], o2)
+        p = jnp.exp2(s * FACTOR - lse[j])
+        ds = (p * (dp - delta[j]) * SCALE).astype(bf16)
+        return q2, o2, ds, p.astype(bf16)
+
+    def query_grad(ds, keys):
+        return lax.dot_general(
             ds, keys[:, :HD], (((0,), (0,)), ((), ())), preferred_element_type=f32
         )
-        return dq, nn(ds, q2), nn(p, o2)
-
-    def body(chunks, slot):
-        dq, dk, dv = visit(chunks, kvs[slot], hot[slot])
-        for i, j in enumerate(chunks):
-            dq_acc[j] += dq[2 * CH * i : 2 * CH * (i + 1)]
-        dkv_acc[slot, :, :HD] += dk
-        dkv_acc[slot, :, HD:] += dv
+
+    def visit(js, keys, blocks):
+        parts = [start(j, keys, blocks) for j in js]
+        q2, o2 = (jnp.concatenate([t[n] for t in parts], axis=0) for n in (0, 1))
+        ds, p = (jnp.concatenate([t[n] for t in parts], axis=1) for n in (2, 3))
+        return query_grad(ds, keys), nn(ds, q2), nn(p, o2)
+
+    def body(pairs):
+        parts = [start(j, kvs[b], hot[b]) for j, b in pairs]
+        for (j, b), (q2, o2, ds, p) in zip(pairs, parts):
+            dq_acc[j] += query_grad(ds, kvs[b])
+            dkv_acc[b, :, :HD] += nn(ds, q2)
+            dkv_acc[b, :, HD:] += nn(p, o2)
 
     for a in reversed(range(HALF)):
         runs = a + 1

time: 107 us -> 104 us (0.972); the launches traced: 106 us -> 104 us
  Pallas kernels: 25.8 us -> 22.8 us
  blocking collectives: 12.9 us -> 14.7 us
    all_to_all x1, blocking collectives: 12.9 us -> 14.7 us  [per_device(): stats = lax.all_to_all(stats, 'z', 0, 0)]
    pallas_call x1, Pallas kernels: 13.1 us -> 11.5 us  [grad_call(): pl.pallas_call(grad_kernel, out_shape=(jax.ShapeDtypeStruct((NZ, CH, 2 *...]
    pallas_call x1, Pallas kernels: 10.6 us -> 9.27 us  [stats_call(): pl.pallas_call(stats_kernel, out_shape=(jax.ShapeDtypeStruct((NZ, 2, 2 *...]
  transfers between devices with their start and end apart: 17 -> 17, of which waited for: 9 -> 8; matrix products, arithmetic and copies ran while one was open for 3% -> 3% of each run, Pallas kernels for 0% -> 0%
where the time goes in v4:
time: 104 us
  starting transfers between devices  32.3 us (31%)
  waiting for transfers between devices  29.7 us (29%)
  Pallas kernels  22.8 us (22%)
  blocking collectives  14.7 us (14%)
  other arithmetic  2.42 us (2%)
  local copies, waits for them, and re-layouts  1.32 us (1%)
    ppermute x13, waiting for transfers between devices, shift(): return lax.ppermute(x, axis, [(i, (i + by) % size) for i in range(size)])  29.7 us
    ppermute x13, starting transfers between devices, shift(): return lax.ppermute(x, axis, [(i, (i + by) % size) for i in range(size)])  21.2 us
    all_to_all x1, blocking collectives, per_device(): stats = lax.all_to_all(stats, 'z', 0, 0)  14.7 us
    pallas_call x1, Pallas kernels, grad_call(): pl.pallas_call(grad_kernel, out_shape=(jax.ShapeDtypeStruct((NZ, CH, 2 *...  11.5 us
    pallas_call x1, Pallas kernels, stats_call(): pl.pallas_call(stats_kernel, out_shape=(jax.ShapeDtypeStruct((NZ, 2, 2 *...  9.27 us
    all_to_all x1, starting transfers between devices, per_device(): k_own = lax.all_to_all(kv, ('y',) + XAX, 0, 0)  7.52 us
    all_to_all x1, starting transfers between devices, per_device(): dq = lax.all_to_all(dq, 'z', 0, 0)  3.49 us
  transfers between devices with their start and end apart: 17, of which 8 were waited for; matrix products, arithmetic and copies ran while one was open for 3% of the time, Pallas kernels for 0%

profile of v4, /device:TPU:8, one launch (start us, length us, event | category | flops | bytes accessed | tf_op | source)
XLA Modules:
  0.0 104.1 jit_solution(14574906957515314126)
XLA Ops:
  0.6 0.0 copy-start.1
  0.6 2.0 %shard_map.76 = (bf16[128,512]{1,0:T(8,128)(2,1)}, bf16[16,128,256]{2,1,0:T(8,128)(2,1)}) custom-call(bf16[128,256]{1,0:T(8,128)(2,1)} %q_ref.1, bf16[128,256]{1,0:T(8,128)(2,1)} %o_ref.1, bf16[128,128]{1,0:T(8,128)(2,1)} %k_ref.1, bf16[128,128]{1,0:T(8,128)(2,1)} %v_ref.1), custom_call_target="tpu_custom_call" | custom-call | tf_op jit(solution)/shard_map/pallas_call | solution.py:265
  2.7 0.0 copy-start
  2.7 7.5 %all-to-all-start = ((bf16[16,128,256]{2,1,0:T(8,128)(2,1)}), bf16[16,128,256]{2,1,0:T(8,128)(2,1)S(1)}, u32[]{:S(2)}, u32[]{:S(2)}) async-start(bf16[16,128,256]{2,1,0:T(8,128)(2,1)} %get-tuple-element.15), calls=%async_computation | async-start | bytes 2097152 | tf_op jit(solution)/shard_map/all_to_all | solution.py:278
  10.2 0.0 copy-done
  10.2 2.0 %collective-permute-start = (bf16[128,512]{1,0:T(8,128)(2,1)S(1)}, bf16[128,512]{1,0:T(8,128)(2,1)S(1)}, u32[]{:S(2)}, u32[]{:S(2)}) collective-permute-start(bf16[128,512]{1,0:T(8,128)(2,1)S(1)} %copy-done), channel_id=1, source_target_pairs={{0,32},{32,64},{64,96},{96,128},{128,160},{160,192},{192,224},{224... | collective-permute-start | bytes 393224 | tf_op jit(solution)/shard_map/ppermute | solution.py:32
  12.2 4.0 %collective-permute-start.1 = (bf16[128,512]{1,0:T(8,128)(2,1)S(1)}, bf16[128,512]{1,0:T(8,128)(2,1)S(1)}, u32[]{:S(2)}, u32[]{:S(2)}) collective-permute-start(bf16[128,512]{1,0:T(8,128)(2,1)S(1)} %copy-done), channel_id=1, source_target_pairs={{0,224},{32,0},{64,32},{96,64},{128,96},{160,128},{192,160},{224,1... | collective-permute-start | bytes 393224 | tf_op jit(solution)/shard_map/ppermute | solution.py:32
  16.2 2.9 %collective-permute-done.refs_1_ = bf16[128,512]{1,0:T(8,128)(2,1)S(1)} collective-permute-done((bf16[128,512]{1,0:T(8,128)(2,1)S(1)}, bf16[128,512]{1,0:T(8,128)(2,1)S(1)}, u32[]{:S(2)}, u32[]{:S(2)}) %collective-permute-start) | collective-permute-done | bytes 131104 | tf_op jit(solution)/shard_map/ppermute | solution.py:32
  19.1 0.0 collective-permute-start.2
  19.1 0.0 collective-permute-done.1.refs_2_
  19.1 3.3 %collective-permute-start.3 = (bf16[128,512]{1,0:T(8,128)(2,1)S(1)}, bf16[128,512]{1,0:T(8,128)(2,1)S(1)}, u32[]{:S(2)}, u32[]{:S(2)}) collective-permute-start(bf16[128,512]{1,0:T(8,128)(2,1)S(1)} %collective-permute-done.1.refs_2_), channel_id=1, source_target_pairs={{0,224},{32,0},{64,32},{96,64},{128,96},{160,128},{192,160},{224,1... | collective-permute-start | bytes 393224 | tf_op jit(solution)/shard_map/ppermute | solution.py:32
  22.4 2.9 %collective-permute-done.2.refs_3_ = bf16[128,512]{1,0:T(8,128)(2,1)S(1)} collective-permute-done((bf16[128,512]{1,0:T(8,128)(2,1)S(1)}, bf16[128,512]{1,0:T(8,128)(2,1)S(1)}, u32[]{:S(2)}, u32[]{:S(2)}) %collective-permute-start.2) | collective-permute-done | bytes 131104 | tf_op jit(solution)/shard_map/ppermute | solution.py:32
  25.3 0.0 collective-permute-start.4
  25.3 0.0 collective-permute-done.3.refs_4_
  25.3 3.3 %collective-permute-start.5 = (bf16[128,512]{1,0:T(8,128)(2,1)S(1)}, bf16[128,512]{1,0:T(8,128)(2,1)S(1)}, u32[]{:S(2)}, u32[]{:S(2)}) collective-permute-start(bf16[128,512]{1,0:T(8,128)(2,1)S(1)} %collective-permute-done.3.refs_4_), channel_id=1, source_target_pairs={{0,224},{32,0},{64,32},{96,64},{128,96},{160,128},{192,160},{224,1... | collective-permute-start | bytes 393224 | tf_op jit(solution)/shard_map/ppermute | solution.py:32
  28.6 2.9 %collective-permute-done.4.refs_5_ = bf16[128,512]{1,0:T(8,128)(2,1)S(1)} collective-permute-done((bf16[128,512]{1,0:T(8,128)(2,1)S(1)}, bf16[128,512]{1,0:T(8,128)(2,1)S(1)}, u32[]{:S(2)}, u32[]{:S(2)}) %collective-permute-start.4) | collective-permute-done | bytes 131104 | tf_op jit(solution)/shard_map/ppermute | solution.py:32
  31.4 0.0 collective-permute-done.5.refs_6_
  31.5 0.0 all-to-all-done.refs_8_
  31.5 0.0 collective-permute-start.7
  31.5 0.0 copy-done.1
  31.5 0.2 slice_reduce_fusion.1
  31.7 0.1 collective-permute-start.6
  31.8 0.1 stack.26.ids
  31.9 0.3 fusion.6
  32.2 7.1 %collective-permute-done.6.refs_7_ = bf16[128,512]{1,0:T(8,128)(2,1)S(1)} collective-permute-done((bf16[128,512]{1,0:T(8,128)(2,1)S(1)}, bf16[128,512]{1,0:T(8,128)(2,1)S(1)}, u32[]{:S(2)}, u32[]{:S(2)}) %collective-permute-start.6) | collective-permute-done | bytes 131104 | tf_op jit(solution)/shard_map/ppermute | solution.py:32
  39.3 0.0 collective-permute-done.7.refs_9_
  39.3 9.3 %shard_map.77 = (f32[8,2,256]{2,1,0:T(2,128)S(1)}, bf16[8,128,512]{2,1,0:T(8,128)(2,1)S(1)}, bf16[8,512,256]{2,1,0:T(8,128)(2,1)S(1)}, bf16[8,512,128]{2,1,0:T(8,128)(2,1)S(1)}, bf16[8,128,128]{2,1,0:T(8,128)(2,1)S(1)}) custom-call(s32[5]{0:T(128)S(1)} %stack.26.ids, s32[4,4]{1,0:T(4,128)S(1)} %pad_add_fusion.mm, ...), custom_call_target="tpu_custom_call" | custom-call | tf_op jit(solution)/shard_map/pallas_call | solution.py:319
  48.6 14.7 %all_to_all.15.st_ref = f32[8,8,2,256]{3,2,1,0:T(2,128)S(1)} all-to-all(f32[8,8,2,256]{3,2,1,0:T(2,128)S(1)} %broadcast_in_dim.2), channel_id=1, replica_groups=mesh['z'=8,'xh'=2,'core'=2,'y'=4,'xl'=2] {'z'}, dimensions={0} | all-to-all | bytes 262144 | tf_op jit(solution)/shard_map/all_to_all | solution.py:299
  63.3 11.5 %shard_map.78 = (bf16[8,128,256]{2,1,0:T(8,128)(2,1)}, bf16[4,4,128,256]{3,2,1,0:T(8,128)(2,1)S(1)}, bf16[4,4,128,256]{3,2,1,0:T(8,128)(2,1)S(1)}) custom-call(s32[5]{0:T(128)S(1)} %stack.26.ids, s32[4,4]{1,0:T(4,128)S(1)} %pad_add_fusion.mm, f32[8,8,2,256]{3,2,1,0:T(2,128)S(1)} %all_to_all.15.st_ref, bf16[8,128,512]{2,1,0:T(8,128)(2,1)S(1)} %get-tuple-element.18.qs, ...), custom_call_target="tpu_custom_call" | custom-call | tf_op jit(solution)/shard_map/pallas_call | solution.py:330
  74.8 0.0 collective-permute-start.8
  74.8 3.5 %all-to-all-start.2 = ((bf16[8,128,256]{2,1,0:T(8,128)(2,1)}), bf16[8,128,256]{2,1,0:T(8,128)(2,1)S(1)}, u32[]{:S(2)}, u32[]{:S(2)}) async-start(bf16[8,128,256]{2,1,0:T(8,128)(2,1)} %get-tuple-element.22), calls=%async_computation.2 | async-start | bytes 1048576 | tf_op jit(solution)/shard_map/all_to_all | solution.py:302
  78.3 0.0 collective-permute-done.8
  78.3 1.5 %add_convert_fusion = bf16[4,4,128,256]{3,2,1,0:T(8,128)(2,1)S(1)} fusion(bf16[4,4,128,256]{3,2,1,0:T(8,128)(2,1)} %collective-permute-done.8, bf16[4,4,128,256]{3,2,1,0:T(8,128)(2,1)S(1)} %get-tuple-element.23), kind=kLoop, calls=%fused_computation | loop fusion | flops 2097152 | bytes 3145728 | tf_op jit(solution)/shard_map/convert_element_type | solution.py:303
  79.9 0.1 dynamic-slice_bitcast_fusion.2
  79.9 2.2 %collective-permute-start.10 = (bf16[4,128,256]{2,1,0:T(8,128)(2,1)S(1)}, bf16[4,128,256]{2,1,0:T(8,128)(2,1)S(1)}, u32[]{:S(2)}, u32[]{:S(2)}) collective-permute-start(bf16[4,128,256]{2,1,0:T(8,128)(2,1)S(1)} %get-tuple-element.31), channel_id=1, source_target_pairs={{0,4},{2,6},{4,0},{6,2},{1,5},{3,7},{5,1},{7,3},{8,12},{10,14},{12... | collective-permute-start | bytes 786440 | tf_op jit(solution)/shard_map/ppermute | solution.py:32
  82.1 1.5 %collective-permute-start.11 = (bf16[4,128,256]{2,1,0:T(8,128)(2,1)S(1)}, bf16[4,128,256]{2,1,0:T(8,128)(2,1)S(1)}, u32[]{:S(2)}, u32[]{:S(2)}) collective-permute-start(bf16[4,128,256]{2,1,0:T(8,128)(2,1)S(1)} %get-tuple-element.30), channel_id=1, source_target_pairs={{0,6},{2,0},{4,2},{6,4},{1,7},{3,1},{5,3},{7,5},{8,14},{10,8},{12,... | collective-permute-start | bytes 786440 | tf_op jit(solution)/shard_map/ppermute | solution.py:32
  83.5 0.6 collective-permute-start.9
  84.1 6.5 %collective-permute-done.10 = bf16[4,128,256]{2,1,0:T(8,128)(2,1)S(1)} collective-permute-done((bf16[4,128,256]{2,1,0:T(8,128)(2,1)S(1)}, bf16[4,128,256]{2,1,0:T(8,128)(2,1)S(1)}, u32[]{:S(2)}, u32[]{:S(2)}) %collective-permute-start.10) | collective-permute-done | bytes 262176 | tf_op jit(solution)/shard_map/ppermute | solution.py:32
  90.7 5.2 %collective-permute-done.11 = bf16[4,128,256]{2,1,0:T(8,128)(2,1)S(1)} collective-permute-done((bf16[4,128,256]{2,1,0:T(8,128)(2,1)S(1)}, bf16[4,128,256]{2,1,0:T(8,128)(2,1)S(1)}, u32[]{:S(2)}, u32[]{:S(2)}) %collective-permute-start.11) | collective-permute-done | bytes 262176 | tf_op jit(solution)/shard_map/ppermute | solution.py:32
  95.8 0.0 collective-permute-done.9
  95.9 0.1 fusion.2
  96.1 1.5 %collective-permute-start.12 = (bf16[128,256]{1,0:T(8,128)(2,1)S(1)}, bf16[128,256]{1,0:T(8,128)(2,1)S(1)}, u32[]{:S(2)}, u32[]{:S(2)}) collective-permute-start(bf16[128,256]{1,0:T(8,128)(2,1)S(1)} %get-tuple-element.32), channel_id=1, source_target_pairs={{0,1},{1,16},{16,17},{17,0},{2,3},{3,18},{18,19},{19,2},{4,5},{5,2... | collective-permute-start | bytes 196616 | tf_op jit(solution)/shard_map/ppermute | solution.py:32
  97.6 1.0 collective-permute-start.13
  98.6 1.8 %collective-permute-start.14 = (bf16[128,256]{1,0:T(8,128)(2,1)S(1)}, bf16[128,256]{1,0:T(8,128)(2,1)S(1)}, u32[]{:S(2)}, u32[]{:S(2)}) collective-permute-start(bf16[128,256]{1,0:T(8,128)(2,1)S(1)} %get-tuple-element.33), channel_id=1, source_target_pairs={{0,17},{1,0},{16,1},{17,16},{2,19},{3,2},{18,3},{19,18},{4,21},{5,... | collective-permute-start | bytes 196616 | tf_op jit(solution)/shard_map/ppermute | solution.py:32
  100.4 0.0 all-to-all-done.2
  100.4 0.7 reduce_sum.12
  101.1 1.2 %collective-permute-done.12 = bf16[128,256]{1,0:T(8,128)(2,1)S(1)} collective-permute-done((bf16[128,256]{1,0:T(8,128)(2,1)S(1)}, bf16[128,256]{1,0:T(8,128)(2,1)S(1)}, u32[]{:S(2)}, u32[]{:S(2)}) %collective-permute-start.12) | collective-permute-done | bytes 65568 | tf_op jit(solution)/shard_map/ppermute | solution.py:32
  102.3 1.1 %collective-permute-done.13 = bf16[128,256]{1,0:T(8,128)(2,1)S(1)} collective-permute-done((bf16[128,256]{1,0:T(8,128)(2,1)S(1)}, bf16[128,256]{1,0:T(8,128)(2,1)S(1)}, u32[]{:S(2)}, u32[]{:S(2)}) %collective-permute-start.13) | collective-permute-done | bytes 65568 | tf_op jit(solution)/shard_map/ppermute | solution.py:32
  103.4 0.0 collective-permute-done.14
  103.4 0.6 fusion.8
  (8 shorter events, 0.2 us)
Async XLA Ops:
  0.6 30.9 %copy-start.1 = (s32[16384]{0:T(1024)S(1)}, s32[16384]{0:T(1024)}, u32[]{:S(2)}) copy-start(s32[16384]{0:T(1024)} %param.9) | copy-start | bytes 196612
  2.7 7.5 %copy-start = (bf16[128,512]{1,0:T(8,128)(2,1)S(1)}, bf16[128,512]{1,0:T(8,128)(2,1)}, u32[]{:S(2)}) copy-start(bf16[128,512]{1,0:T(8,128)(2,1)} %get-tuple-element.14.refs_0_) | copy-start | bytes 393220
  2.7 28.8 %all-to-all-start = ((bf16[16,128,256]{2,1,0:T(8,128)(2,1)}), bf16[16,128,256]{2,1,0:T(8,128)(2,1)S(1)}, u32[]{:S(2)}, u32[]{:S(2)}) async-start(bf16[16,128,256]{2,1,0:T(8,128)(2,1)} %get-tuple-element.15), calls=%async_computation | async-start | bytes 2097152 | tf_op jit(solution)/shard_map/all_to_all | solution.py:278
  10.2 8.9 %collective-permute-start = (bf16[128,512]{1,0:T(8,128)(2,1)S(1)}, bf16[128,512]{1,0:T(8,128)(2,1)S(1)}, u32[]{:S(2)}, u32[]{:S(2)}) collective-permute-start(bf16[128,512]{1,0:T(8,128)(2,1)S(1)} %copy-done), channel_id=1, source_target_pairs={{0,32},{32,64},{64,96},{96,128},{128,160},{160,192},{192,224},{224... | collective-permute-start | bytes 393224 | tf_op jit(solution)/shard_map/ppermute | solution.py:32
  12.2 6.9 %collective-permute-start.1 = (bf16[128,512]{1,0:T(8,128)(2,1)S(1)}, bf16[128,512]{1,0:T(8,128)(2,1)S(1)}, u32[]{:S(2)}, u32[]{:S(2)}) collective-permute-start(bf16[128,512]{1,0:T(8,128)(2,1)S(1)} %copy-done), channel_id=1, source_target_pairs={{0,224},{32,0},{64,32},{96,64},{128,96},{160,128},{192,160},{224,1... | collective-permute-start | bytes 393224 | tf_op jit(solution)/shard_map/ppermute | solution.py:32
  19.1 6.2 %collective-permute-start.2 = (bf16[128,512]{1,0:T(8,128)(2,1)S(1)}, bf16[128,512]{1,0:T(8,128)(2,1)S(1)}, u32[]{:S(2)}, u32[]{:S(2)}) collective-permute-start(bf16[128,512]{1,0:T(8,128)(2,1)S(1)} %collective-permute-done.refs_1_), channel_id=1, source_target_pairs={{0,32},{32,64},{64,96},{96,128},{128,160},{160,192},{192,224},{224... | collective-permute-start | bytes 393224 | tf_op jit(solution)/shard_map/ppermute | solution.py:32
  19.1 6.2 %collective-permute-start.3 = (bf16[128,512]{1,0:T(8,128)(2,1)S(1)}, bf16[128,512]{1,0:T(8,128)(2,1)S(1)}, u32[]{:S(2)}, u32[]{:S(2)}) collective-permute-start(bf16[128,512]{1,0:T(8,128)(2,1)S(1)} %collective-permute-done.1.refs_2_), channel_id=1, source_target_pairs={{0,224},{32,0},{64,32},{96,64},{128,96},{160,128},{192,160},{224,1... | collective-permute-start | bytes 393224 | tf_op jit(solution)/shard_map/ppermute | solution.py:32
  25.3 6.2 %collective-permute-start.4 = (bf16[128,512]{1,0:T(8,128)(2,1)S(1)}, bf16[128,512]{1,0:T(8,128)(2,1)S(1)}, u32[]{:S(2)}, u32[]{:S(2)}) collective-permute-start(bf16[128,512]{1,0:T(8,128)(2,1)S(1)} %collective-permute-done.2.refs_3_), channel_id=1, source_target_pairs={{0,32},{32,64},{64,96},{96,128},{128,160},{160,192},{192,224},{224... | collective-permute-start | bytes 393224 | tf_op jit(solution)/shard_map/ppermute | solution.py:32
  25.3 6.2 %collective-permute-start.5 = (bf16[128,512]{1,0:T(8,128)(2,1)S(1)}, bf16[128,512]{1,0:T(8,128)(2,1)S(1)}, u32[]{:S(2)}, u32[]{:S(2)}) collective-permute-start(bf16[128,512]{1,0:T(8,128)(2,1)S(1)} %collective-permute-done.3.refs_4_), channel_id=1, source_target_pairs={{0,224},{32,0},{64,32},{96,64},{128,96},{160,128},{192,160},{224,1... | collective-permute-start | bytes 393224 | tf_op jit(solution)/shard_map/ppermute | solution.py:32
  31.5 7.8 %collective-permute-start.7 = (bf16[16,128,256]{2,1,0:T(8,128)(2,1)S(1)}, bf16[16,128,256]{2,1,0:T(8,128)(2,1)S(1)}, u32[]{:S(2)}, u32[]{:S(2)}) collective-permute-start(bf16[16,128,256]{2,1,0:T(8,128)(2,1)S(1)} %all-to-all-done.refs_8_), channel_id=1, source_target_pairs={{0,8},{8,0},{1,9},{9,1},{2,10},{10,2},{3,11},{11,3},{4,12},{12,4},... | collective-permute-start | bytes 3145736 | tf_op jit(solution)/shard_map/ppermute | solution.py:276
  31.7 7.5 %collective-permute-start.6 = (bf16[128,512]{1,0:T(8,128)(2,1)S(1)}, bf16[128,512]{1,0:T(8,128)(2,1)S(1)}, u32[]{:S(2)}, u32[]{:S(2)}) collective-permute-start(bf16[128,512]{1,0:T(8,128)(2,1)S(1)} %collective-permute-done.4.refs_5_), channel_id=1, source_target_pairs={{0,32},{32,64},{64,96},{96,128},{128,160},{160,192},{192,224},{224... | collective-permute-start | bytes 393224 | tf_op jit(solution)/shard_map/ppermute | solution.py:32
  74.8 3.5 %collective-permute-start.8 = (bf16[4,4,128,256]{3,2,1,0:T(8,128)(2,1)S(1)}, bf16[4,4,128,256]{3,2,1,0:T(8,128)(2,1)}, u32[]{:S(2)}, u32[]{:S(2)}) collective-permute-start(bf16[4,4,128,256]{3,2,1,0:T(8,128)(2,1)S(1)} %get-tuple-element.24), channel_id=1, source_target_pairs={{0,8},{8,0},{1,9},{9,1},{2,10},{10,2},{3,11},{11,3},{4,12},{12,4},... | collective-permute-start | bytes 3145736 | tf_op jit(solution)/shard_map/ppermute | solution.py:276
  74.8 25.6 %all-to-all-start.2 = ((bf16[8,128,256]{2,1,0:T(8,128)(2,1)}), bf16[8,128,256]{2,1,0:T(8,128)(2,1)S(1)}, u32[]{:S(2)}, u32[]{:S(2)}) async-start(bf16[8,128,256]{2,1,0:T(8,128)(2,1)} %get-tuple-element.22), calls=%async_computation.2 | async-start | bytes 1048576 | tf_op jit(solution)/shard_map/all_to_all | solution.py:302
  79.9 10.7 %collective-permute-start.10 = (bf16[4,128,256]{2,1,0:T(8,128)(2,1)S(1)}, bf16[4,128,256]{2,1,0:T(8,128)(2,1)S(1)}, u32[]{:S(2)}, u32[]{:S(2)}) collective-permute-start(bf16[4,128,256]{2,1,0:T(8,128)(2,1)S(1)} %get-tuple-element.31), channel_id=1, source_target_pairs={{0,4},{2,6},{4,0},{6,2},{1,5},{3,7},{5,1},{7,3},{8,12},{10,14},{12... | collective-permute-start | bytes 786440 | tf_op jit(solution)/shard_map/ppermute | solution.py:32
  82.1 13.8 %collective-permute-start.11 = (bf16[4,128,256]{2,1,0:T(8,128)(2,1)S(1)}, bf16[4,128,256]{2,1,0:T(8,128)(2,1)S(1)}, u32[]{:S(2)}, u32[]{:S(2)}) collective-permute-start(bf16[4,128,256]{2,1,0:T(8,128)(2,1)S(1)} %get-tuple-element.30), channel_id=1, source_target_pairs={{0,6},{2,0},{4,2},{6,4},{1,7},{3,1},{5,3},{7,5},{8,14},{10,8},{12,... | collective-permute-start | bytes 786440 | tf_op jit(solution)/shard_map/ppermute | solution.py:32
  83.5 12.4 %collective-permute-start.9 = (bf16[4,128,256]{2,1,0:T(8,128)(2,1)S(1)}, bf16[4,128,256]{2,1,0:T(8,128)(2,1)S(1)}, u32[]{:S(2)}, u32[]{:S(2)}) collective-permute-start(bf16[4,128,256]{2,1,0:T(8,128)(2,1)S(1)} %get-tuple-element.29), channel_id=1, source_target_pairs={{0,2},{2,4},{4,6},{6,0},{1,3},{3,5},{5,7},{7,1},{8,10},{10,12},{12... | collective-permute-start | bytes 786440 | tf_op jit(solution)/shard_map/ppermute | solution.py:32
  96.1 6.3 %collective-permute-start.12 = (bf16[128,256]{1,0:T(8,128)(2,1)S(1)}, bf16[128,256]{1,0:T(8,128)(2,1)S(1)}, u32[]{:S(2)}, u32[]{:S(2)}) collective-permute-start(bf16[128,256]{1,0:T(8,128)(2,1)S(1)} %get-tuple-element.32), channel_id=1, source_target_pairs={{0,1},{1,16},{16,17},{17,0},{2,3},{3,18},{18,19},{19,2},{4,5},{5,2... | collective-permute-start | bytes 196616 | tf_op jit(solution)/shard_map/ppermute | solution.py:32
  97.6 5.8 %collective-permute-start.13 = (bf16[128,256]{1,0:T(8,128)(2,1)S(1)}, bf16[128,256]{1,0:T(8,128)(2,1)S(1)}, u32[]{:S(2)}, u32[]{:S(2)}) collective-permute-start(bf16[128,256]{1,0:T(8,128)(2,1)S(1)} %get-tuple-element.34), channel_id=1, source_target_pairs={{0,16},{1,17},{16,0},{17,1},{2,18},{3,19},{18,2},{19,3},{4,20},{5,... | collective-permute-start | bytes 196616 | tf_op jit(solution)/shard_map/ppermute | solution.py:32
  98.6 4.8 %collective-permute-start.14 = (bf16[128,256]{1,0:T(8,128)(2,1)S(1)}, bf16[128,256]{1,0:T(8,128)(2,1)S(1)}, u32[]{:S(2)}, u32[]{:S(2)}) collective-permute-start(bf16[128,256]{1,0:T(8,128)(2,1)S(1)} %get-tuple-element.33), channel_id=1, source_target_pairs={{0,17},{1,0},{16,1},{17,16},{2,19},{3,2},{18,3},{19,18},{4,21},{5,... | collective-permute-start | bytes 196616 | tf_op jit(solution)/shard_map/ppermute | solution.py:32

commit v5 on v4

--- a/solution.py
+++ b/solution.py
@@ -40,29 +40,21 @@
     return lax.dot_general(a, b, (((1,), (0,)), ((), ())), preferred_element_type=f32)
 
 
-def load_all(ids, q_pieces, k_own, k_other, qs, kvs, sem):
-    z, core = ids[0], ids[4]
-    copies = []
-    for r, by in enumerate(Q_SHIFTS):
-        copies.append((q_pieces[r], qs.at[(z - by) % NZ]))
-    for y in range(NY):
-        for xh in range(NXH):
-            for ref, pc in ((k_own, core), (k_other, 1 - core)):
-                at = pl.multiple_of(xh * (NCORE * CH) + pc * CH, CH)
-                copies.append(
-                    (
-                        ref.at[pl.ds(y * NX + xh * NXL, NXL)],
-                        kvs.at[pl.ds(y * NXL, NXL), pl.ds(at, CH)],
-                    )
-                )
-    copies = [pltpu.make_async_copy(a, b, sem.at[n]) for n, (a, b) in enumerate(copies)]
-    for c in copies:
-        c.start()
-    return copies
+def load_queries(ids, q_pieces, qs):
+    for by, piece in zip(Q_SHIFTS, q_pieces):
+        qs[(ids[0] - by) % NZ] = piece[...]
+
+
+def run_of(own_ref, other_ref, slot):
+    at = slot // NXL * NX + slot % NXL
+    return [ref[at + xh * NXL] for ref in (own_ref, other_ref) for xh in range(NXH)]
+
+
+def runs_of(own_ref, other_ref, slots):
+    return jnp.concatenate([t for n in slots for t in run_of(own_ref, other_ref, n)], axis=0)
 
 
 Q_SHIFTS = (0, 1, -1, 2, -2, 3, -3, 4)
-N_COPIES = NZ + NCORE * NY * NXH
 
 
 def pack_kernel(q_ref, o_ref, k_ref, v_ref, qo_ref, kv_ref):
@@ -73,7 +65,7 @@
         kv_ref[i, :, HD:] = v_ref[...]
 
 
-def masks(qid_ref, kid_ref, hot, bias):
+def make_masks(qid_ref, kid_ref, hot, bias):
     lane = lax.broadcasted_iota(i32, (RUN, CH), 1)
     for b in range(HALF):
         col = jnp.broadcast_to(kid_ref[b : b + 1, :], (CH, RUN)).T
@@ -120,13 +112,10 @@
         body([(a + HALF + 1, a + HALF) for a in steps])
 
 
-def stats_kernel(ids, mm, qid_ref, kid_ref, *refs):
-    q_pieces, k_own, k_other = refs[:NZ], refs[NZ], refs[NZ + 1]
-    out_ref, qs, kvs, hot, bias, top, total, dot, sem = refs[NZ + 2 :]
-    copies = load_all(ids, q_pieces, k_own, k_other, qs, kvs, sem)
-    masks(qid_ref, kid_ref, hot, bias)
-    for c in copies:
-        c.wait()
+def stats_kernel(ids, mm, qid_ref, kid_ref, k_own, k_other, *refs):
+    q_pieces, (out_ref, qs, hot, bias, top, total, dot) = refs[:NZ], refs[NZ:]
+    load_queries(ids, q_pieces, qs)
+    make_masks(qid_ref, kid_ref, hot, bias)
     top[...] = jnp.full(top.shape, LOW, f32)
     total[...] = jnp.zeros(total.shape, f32)
     dot[...] = jnp.zeros(dot.shape, f32)
@@ -141,13 +130,16 @@
         dot[j] = dot[j] * f + jnp.sum(p * dp, axis=0, keepdims=True)
 
     def body(pairs):
-        ss = [scores(kvs[b, :, :HD], both_heads(qs[j], 0), hot[b], bias[j]) for j, b in pairs]
-        dps = [nt(kvs[b, :, HD:], both_heads(qs[j], 2 * HD)) for j, b in pairs]
+        ss, dps = [], []
+        for j, b in pairs:
+            keys = runs_of(k_own, k_other, [b])
+            ss.append(scores(keys[:, :HD], both_heads(qs[j], 0), hot[b], bias[j]))
+            dps.append(nt(keys[:, HD:], both_heads(qs[j], 2 * HD)))
         for (j, _), s, dp in zip(pairs, ss, dps):
             update(j, s, dp)
 
     for a in range(HALF):
-        keys = kvs[: a + 1].reshape((a + 1) * RUN, 2 * HD)
+        keys = runs_of(k_own, k_other, range(a + 1))
         blocks = hot[: a + 1].reshape((a + 1) * RUN, CH)
         js = (a, a + HALF)
         ss = [scores(keys[:, :HD], both_heads(qs[j], 0), blocks, bias[j]) for j in js]
@@ -163,22 +155,8 @@
     out_ref[:, 1:2, :] = dot[...] / safe
 
 
-def grad_kernel(
-    ids,
-    mm,
-    st_ref,
-    qs,
-    kvs,
-    hot,
-    bias,
-    dq_ref,
-    own_ref,
-    other_ref,
-    lse,
-    delta,
-    dq_acc,
-    dkv_acc,
-):
+def grad_kernel(ids, mm, hot, bias, k_own, k_other, *refs):
+    st_ref, qs, dq_ref, own_ref, other_ref, lse, delta, dq_acc, dkv_acc = refs
     parts = st_ref[:, :, 0:1, :]
     high = jnp.max(parts, axis=0)
     shares = jnp.exp2(parts - high[None])
@@ -208,15 +186,16 @@
         return query_grad(ds, keys), nn(ds, q2), nn(p, o2)
 
     def body(pairs):
-        parts = [start(j, kvs[b], hot[b]) for j, b in pairs]
-        for (j, b), (q2, o2, ds, p) in zip(pairs, parts):
-            dq_acc[j] += query_grad(ds, kvs[b])
+        keys = [runs_of(k_own, k_other, [b]) for _, b in pairs]
+        parts = [start(j, k, hot[b]) for (j, b), k in zip(pairs, keys)]
+        for (j, b), k, (q2, o2, ds, p) in zip(pairs, keys, parts):
+            dq_acc[j] += query_grad(ds, k)
             dkv_acc[b, :, :HD] += nn(ds, q2)
             dkv_acc[b, :, HD:] += nn(p, o2)
 
     for a in reversed(range(HALF)):
         runs = a + 1
-        keys = kvs[:runs].reshape(runs * RUN, 2 * HD)
+        keys = runs_of(k_own, k_other, range(runs))
         blocks = hot[:runs].reshape(runs * RUN, CH)
         dq, dk, dv = visit((a, a + HALF), keys, blocks)
         dq_acc[a] = dq[: 2 * CH]
@@ -233,30 +212,24 @@
     for j in range(NZ):
         t = dq_acc[j]
         dq_ref[j] = jnp.concatenate([t[:CH], t[CH:]], axis=1).astype(bf16)
-    core = ids[4]
     for slot in range(NRUN):
         for xh in range(NXH):
             y, x = slot // NXL, xh * NXL + slot % NXL
-            at = xh * NCORE * CH
-            own_at = pl.multiple_of(at + core * CH, CH)
-            other_at = pl.multiple_of(at + (1 - core) * CH, CH)
-            own_ref[y, x] = dkv_acc[slot, pl.ds(own_at, CH), :].astype(bf16)
-            other_ref[y, x] = dkv_acc[slot, pl.ds(other_at, CH), :].astype(bf16)
+            for n, ref in enumerate((own_ref, other_ref)):
+                at = (n * NXH + xh) * CH
+                ref[y, x] = dkv_acc[slot, at : at + CH, :].astype(bf16)
 
 
 SMEM = pl.BlockSpec(memory_space=pltpu.SMEM)
 VMEM = pl.BlockSpec(memory_space=pltpu.VMEM)
-ANY = pl.BlockSpec(memory_space=pl.ANY)
 DATA = VMEM
 BIG = 44 << 20
-LOADS = (
-    jax.ShapeDtypeStruct((NZ, CH, 4 * HD), bf16),
-    jax.ShapeDtypeStruct((NRUN, RUN, 2 * HD), bf16),
+QUERIES = jax.ShapeDtypeStruct((NZ, CH, 4 * HD), bf16)
+MASKS = (
     jax.ShapeDtypeStruct((NRUN, RUN, CH), bf16),
     jax.ShapeDtypeStruct((NZ, CH, CH), bf16),
 )
 ROW = pltpu.VMEM((NZ, 1, 2 * CH), f32)
-SEMS = pltpu.SemaphoreType.DMA((N_COPIES,))
 
 
 def per_device(queries, key_states, value_states, grad_output, block_ids):
@@ -291,13 +264,14 @@
     kid = block_ids.reshape(HALF, NZ, RUN)
     kid = lax.dynamic_slice_in_dim(kid, z, 1, 1).reshape(HALF, RUN)
     mm = jnp.stack([qid[:, 0, 0], qid[:, 0, CH - 1], kid[:, 0], kid[:, RUN - 1]])
+    kid = kid.reshape(HALF, NXH, NCORE, CH)
+    kid = jnp.where(core == 0, kid, kid[:, :, ::-1]).swapaxes(1, 2).reshape(HALF, RUN)
     ids = jnp.stack([z, y, xh, xl, core]).astype(i32)
-    data = (*q_pieces, k_own, k_other)
-
-    stats, *held = stats_call(ids, mm, qid, kid, data)
+    stats, queries, hot, bias = stats_call((ids, mm, qid, kid, k_own, k_other), q_pieces)
+    keys = (ids, mm, hot, bias, k_own, k_other)
     stats = jnp.broadcast_to(stats[None], (NZ,) + stats.shape)
     stats = lax.all_to_all(stats, "z", 0, 0)
-    dq, own, other = grad_call(ids, mm, stats, held)
+    dq, own, other = grad_call(keys, stats, queries)
 
     dq = lax.all_to_all(dq, "z", 0, 0)
     pair = (own.astype(f32) + swap(other).astype(f32)).astype(bf16)
@@ -315,18 +289,21 @@
     return sum(g.astype(f32) for g in got).astype(bf16)
 
 
-def stats_call(ids, mm, qid, kid, data):
+KEY_SPECS = [SMEM, SMEM] + [VMEM] * 4
+
+
+def stats_call(keys, q_pieces):
     return pl.pallas_call(
         stats_kernel,
-        out_shape=(jax.ShapeDtypeStruct((NZ, 2, 2 * CH), f32),) + LOADS,
-        in_specs=[SMEM, SMEM, VMEM, VMEM] + [DATA] * len(data),
-        out_specs=(VMEM,) * 5,
-        scratch_shapes=[ROW, ROW, ROW, SEMS],
+        out_shape=(jax.ShapeDtypeStruct((NZ, 2, 2 * CH), f32), QUERIES) + MASKS,
+        in_specs=KEY_SPECS + [VMEM] * NZ,
+        out_specs=(VMEM,) * 4,
+        scratch_shapes=[ROW, ROW, ROW],
         compiler_params=pltpu.CompilerParams(vmem_limit_bytes=BIG),
-    )(ids, mm, qid, kid, *data)
-
-
-def grad_call(ids, mm, stats, held):
+    )(*keys, *q_pieces)
+
+
+def grad_call(keys, stats, queries):
     return pl.pallas_call(
         grad_kernel,
         out_shape=(
@@ -334,8 +311,8 @@
             jax.ShapeDtypeStruct((NY, NX, CH, 2 * HD), bf16),
             jax.ShapeDtypeStruct((NY, NX, CH, 2 * HD), bf16),
         ),
-        in_specs=[SMEM, SMEM] + [VMEM] * 5,
-        out_specs=(VMEM, VMEM, VMEM),
+        in_specs=KEY_SPECS + [VMEM] * 2,
+        out_specs=(VMEM,) * 3,
         scratch_shapes=[
             ROW,
             ROW,
@@ -343,7 +320,7 @@
             pltpu.VMEM((NRUN, RUN, 2 * HD), f32),
         ],
         compiler_params=pltpu.CompilerParams(vmem_limit_bytes=BIG),
-    )(ids, mm, stats, *held)
+    )(*keys, stats, queries)
 
 
 def solution(mesh):

time: 104 us -> 101 us (0.971)
  Pallas kernels: 22.8 us -> 19 us
    pallas_call x1, Pallas kernels: 9.27 us -> 5.7 us  [stats_call(): pl.pallas_call(stats_kernel, out_shape=(jax.ShapeDtypeStruct((NZ, 2, 2 *...]
where the time goes in v5:
time: 101 us
  starting transfers between devices  32.3 us (32%)
  waiting for transfers between devices  29.7 us (29%)
  Pallas kernels  19 us (19%)
  blocking collectives  14.7 us (15%)
  other arithmetic  2.43 us (2%)
  local copies, waits for them, and re-layouts  2.15 us (2%)
    ppermute x13, waiting for transfers between devices, shift(): return lax.ppermute(x, axis, [(i, (i + by) % size) for i in range(size)])  29.7 us
    ppermute x13, starting transfers between devices, shift(): return lax.ppermute(x, axis, [(i, (i + by) % size) for i in range(size)])  21.2 us
    all_to_all x1, blocking collectives, per_device(): stats = lax.all_to_all(stats, 'z', 0, 0)  14.7 us
    pallas_call x1, Pallas kernels, grad_call(): pl.pallas_call(grad_kernel, out_shape=(jax.ShapeDtypeStruct((NZ, CH, 2 *...  11.3 us
    all_to_all x1, starting transfers between devices, per_device(): k_own = lax.all_to_all(kv, ('y',) + XAX, 0, 0)  7.52 us
    pallas_call x1, Pallas kernels, stats_call(): pl.pallas_call(stats_kernel, out_shape=(jax.ShapeDtypeStruct((NZ, 2, 2 *...  5.7 us
    all_to_all x1, starting transfers between devices, per_device(): dq = lax.all_to_all(dq, 'z', 0, 0)  3.49 us
  transfers between devices with their start and end apart: 17, of which 8 were waited for; matrix products, arithmetic and copies ran while one was open for 3% of the time, Pallas kernels for 0%

profile of v5, /device:TPU:8, one launch (start us, length us, event | category | flops | bytes accessed | tf_op | source)
XLA Modules:
  0.0 101.1 jit_solution(3241013278935058014)
XLA Ops:
  0.6 2.0 %shard_map.76 = (bf16[128,512]{1,0:T(8,128)(2,1)}, bf16[16,128,256]{2,1,0:T(8,128)(2,1)}) custom-call(bf16[128,256]{1,0:T(8,128)(2,1)} %q_ref.1, bf16[128,256]{1,0:T(8,128)(2,1)} %o_ref.1, bf16[128,128]{1,0:T(8,128)(2,1)} %k_ref.1, bf16[128,128]{1,0:T(8,128)(2,1)} %v_ref.1), custom_call_target="tpu_custom_call" | custom-call | tf_op jit(solution)/shard_map/pallas_call | solution.py:238
  2.6 0.0 copy-start.1
  2.6 0.0 copy-start.2
  2.6 7.5 %all-to-all-start = ((bf16[16,128,256]{2,1,0:T(8,128)(2,1)}), bf16[16,128,256]{2,1,0:T(8,128)(2,1)S(1)}, u32[]{:S(2)}, u32[]{:S(2)}) async-start(bf16[16,128,256]{2,1,0:T(8,128)(2,1)} %get-tuple-element.13), calls=%async_computation | async-start | bytes 2097152 | tf_op jit(solution)/shard_map/all_to_all | solution.py:251
  10.2 0.0 copy-done.1
  10.2 2.0 %collective-permute-start.3 = (bf16[128,512]{1,0:T(8,128)(2,1)S(1)}, bf16[128,512]{1,0:T(8,128)(2,1)S(1)}, u32[]{:S(2)}, u32[]{:S(2)}) collective-permute-start(bf16[128,512]{1,0:T(8,128)(2,1)S(1)} %copy-done.1), channel_id=1, source_target_pairs={{0,32},{32,64},{64,96},{96,128},{128,160},{160,192},{192,224},{224... | collective-permute-start | bytes 393224 | tf_op jit(solution)/shard_map/ppermute | solution.py:32
  12.2 4.0 %collective-permute-start = (bf16[128,512]{1,0:T(8,128)(2,1)S(1)}, bf16[128,512]{1,0:T(8,128)(2,1)S(1)}, u32[]{:S(2)}, u32[]{:S(2)}) collective-permute-start(bf16[128,512]{1,0:T(8,128)(2,1)S(1)} %copy-done.1), channel_id=1, source_target_pairs={{0,224},{32,0},{64,32},{96,64},{128,96},{160,128},{192,160},{224,1... | collective-permute-start | bytes 393224 | tf_op jit(solution)/shard_map/ppermute | solution.py:32
  16.2 2.9 %collective-permute-done.3.refs_1_ = bf16[128,512]{1,0:T(8,128)(2,1)S(1)} collective-permute-done((bf16[128,512]{1,0:T(8,128)(2,1)S(1)}, bf16[128,512]{1,0:T(8,128)(2,1)S(1)}, u32[]{:S(2)}, u32[]{:S(2)}) %collective-permute-start.3) | collective-permute-done | bytes 131104 | tf_op jit(solution)/shard_map/ppermute | solution.py:32
  19.0 0.0 collective-permute-start.4
  19.1 0.0 collective-permute-done.refs_2_
  19.1 3.3 %collective-permute-start.1 = (bf16[128,512]{1,0:T(8,128)(2,1)S(1)}, bf16[128,512]{1,0:T(8,128)(2,1)S(1)}, u32[]{:S(2)}, u32[]{:S(2)}) collective-permute-start(bf16[128,512]{1,0:T(8,128)(2,1)S(1)} %collective-permute-done.refs_2_), channel_id=1, source_target_pairs={{0,224},{32,0},{64,32},{96,64},{128,96},{160,128},{192,160},{224,1... | collective-permute-start | bytes 393224 | tf_op jit(solution)/shard_map/ppermute | solution.py:32
  22.4 2.9 %collective-permute-done.4.refs_3_ = bf16[128,512]{1,0:T(8,128)(2,1)S(1)} collective-permute-done((bf16[128,512]{1,0:T(8,128)(2,1)S(1)}, bf16[128,512]{1,0:T(8,128)(2,1)S(1)}, u32[]{:S(2)}, u32[]{:S(2)}) %collective-permute-start.4) | collective-permute-done | bytes 131104 | tf_op jit(solution)/shard_map/ppermute | solution.py:32
  25.2 0.0 collective-permute-start.5
  25.2 0.0 collective-permute-done.1.refs_4_
  25.2 3.3 %collective-permute-start.2 = (bf16[128,512]{1,0:T(8,128)(2,1)S(1)}, bf16[128,512]{1,0:T(8,128)(2,1)S(1)}, u32[]{:S(2)}, u32[]{:S(2)}) collective-permute-start(bf16[128,512]{1,0:T(8,128)(2,1)S(1)} %collective-permute-done.1.refs_4_), channel_id=1, source_target_pairs={{0,224},{32,0},{64,32},{96,64},{128,96},{160,128},{192,160},{224,1... | collective-permute-start | bytes 393224 | tf_op jit(solution)/shard_map/ppermute | solution.py:32
  28.5 2.9 %collective-permute-done.5.refs_5_ = bf16[128,512]{1,0:T(8,128)(2,1)S(1)} collective-permute-done((bf16[128,512]{1,0:T(8,128)(2,1)S(1)}, bf16[128,512]{1,0:T(8,128)(2,1)S(1)}, u32[]{:S(2)}, u32[]{:S(2)}) %collective-permute-start.5) | collective-permute-done | bytes 131104 | tf_op jit(solution)/shard_map/ppermute | solution.py:32
  31.4 0.0 collective-permute-done.2.refs_6_
  31.4 0.0 all-to-all-done.k_own
  31.4 0.0 collective-permute-start.6
  31.4 0.0 copy-done.2
  31.5 0.2 slice_reduce_fusion.1
  31.7 0.1 collective-permute-start.7
  31.8 0.1 stack.26.ids
  31.9 0.3 fusion.7
  32.2 7.0 %collective-permute-done.7.refs_7_ = bf16[128,512]{1,0:T(8,128)(2,1)S(1)} collective-permute-done((bf16[128,512]{1,0:T(8,128)(2,1)S(1)}, bf16[128,512]{1,0:T(8,128)(2,1)S(1)}, u32[]{:S(2)}, u32[]{:S(2)}) %collective-permute-start.7) | collective-permute-done | bytes 131104 | tf_op jit(solution)/shard_map/ppermute | solution.py:32
  39.2 0.0 collective-permute-done.6.k_other
  39.2 5.7 %shard_map.77 = (f32[8,2,256]{2,1,0:T(2,128)S(1)}, bf16[8,128,512]{2,1,0:T(8,128)(2,1)S(1)}, bf16[8,512,128]{2,1,0:T(8,128)(2,1)S(1)}, bf16[8,128,128]{2,1,0:T(8,128)(2,1)S(1)}) custom-call(s32[5]{0:T(128)S(1)} %stack.26.ids, s32[4,4]{1,0:T(4,128)S(1)} %pad_add_fusion.mm, s32[4,1,128]{2,1,0:T(1,128)S(1)} %constant_dynamic-slice_fusion.3.qid_ref, ...), custom_call_target="tpu_custom_call" | custom-call | tf_op jit(solution)/shard_map/pallas_call | solution.py:296
  45.0 14.7 %all_to_all.15.refs_0_ = f32[8,8,2,256]{3,2,1,0:T(2,128)S(1)} all-to-all(f32[8,8,2,256]{3,2,1,0:T(2,128)S(1)} %broadcast_in_dim.2), channel_id=1, replica_groups=mesh['z'=8,'xh'=2,'core'=2,'y'=4,'xl'=2] {'z'}, dimensions={0} | all-to-all | bytes 262144 | tf_op jit(solution)/shard_map/all_to_all | solution.py:273
  59.7 11.3 %shard_map.78 = (bf16[8,128,256]{2,1,0:T(8,128)(2,1)S(1)}, bf16[4,4,128,256]{3,2,1,0:T(8,128)(2,1)S(1)}, bf16[4,4,128,256]{3,2,1,0:T(8,128)(2,1)}) custom-call(s32[5]{0:T(128)S(1)} %stack.26.ids, s32[4,4]{1,0:T(4,128)S(1)} %pad_add_fusion.mm, bf16[8,512,128]{2,1,0:T(8,128)(2,1)S(1)} %get-tuple-element.16.hot, ...), custom_call_target="tpu_custom_call" | custom-call | tf_op jit(solution)/shard_map/pallas_call | solution.py:307
  71.0 0.0 copy-start
  71.0 0.8 copy-done
  71.8 0.0 collective-permute-start.8
  71.8 3.5 %all-to-all-start.2 = ((bf16[8,128,256]{2,1,0:T(8,128)(2,1)}), bf16[8,128,256]{2,1,0:T(8,128)(2,1)S(1)}, u32[]{:S(2)}, u32[]{:S(2)}) async-start(bf16[8,128,256]{2,1,0:T(8,128)(2,1)} %copy-done), calls=%async_computation.2 | async-start | bytes 1048576 | tf_op jit(solution)/shard_map/all_to_all | solution.py:276
  75.3 0.0 collective-permute-done.8
  75.3 1.5 %add_convert_fusion = bf16[4,4,128,256]{3,2,1,0:T(8,128)(2,1)S(1)} fusion(bf16[4,4,128,256]{3,2,1,0:T(8,128)(2,1)} %collective-permute-done.8, bf16[4,4,128,256]{3,2,1,0:T(8,128)(2,1)S(1)} %get-tuple-element.21), kind=kLoop, calls=%fused_computation | loop fusion | flops 2097152 | bytes 3145728 | tf_op jit(solution)/shard_map/convert_element_type | solution.py:277
  76.9 0.1 dynamic-slice_bitcast_fusion.2
  76.9 2.2 %collective-permute-start.10 = (bf16[4,128,256]{2,1,0:T(8,128)(2,1)S(1)}, bf16[4,128,256]{2,1,0:T(8,128)(2,1)S(1)}, u32[]{:S(2)}, u32[]{:S(2)}) collective-permute-start(bf16[4,128,256]{2,1,0:T(8,128)(2,1)S(1)} %get-tuple-element.29), channel_id=1, source_target_pairs={{0,4},{2,6},{4,0},{6,2},{1,5},{3,7},{5,1},{7,3},{8,12},{10,14},{12... | collective-permute-start | bytes 786440 | tf_op jit(solution)/shard_map/ppermute | solution.py:32
  79.1 1.5 %collective-permute-start.11 = (bf16[4,128,256]{2,1,0:T(8,128)(2,1)S(1)}, bf16[4,128,256]{2,1,0:T(8,128)(2,1)S(1)}, u32[]{:S(2)}, u32[]{:S(2)}) collective-permute-start(bf16[4,128,256]{2,1,0:T(8,128)(2,1)S(1)} %get-tuple-element.28), channel_id=1, source_target_pairs={{0,6},{2,0},{4,2},{6,4},{1,7},{3,1},{5,3},{7,5},{8,14},{10,8},{12,... | collective-permute-start | bytes 786440 | tf_op jit(solution)/shard_map/ppermute | solution.py:32
  80.6 0.6 collective-permute-start.9
  81.1 6.6 %collective-permute-done.10 = bf16[4,128,256]{2,1,0:T(8,128)(2,1)S(1)} collective-permute-done((bf16[4,128,256]{2,1,0:T(8,128)(2,1)S(1)}, bf16[4,128,256]{2,1,0:T(8,128)(2,1)S(1)}, u32[]{:S(2)}, u32[]{:S(2)}) %collective-permute-start.10) | collective-permute-done | bytes 262176 | tf_op jit(solution)/shard_map/ppermute | solution.py:32
  87.7 5.2 %collective-permute-done.11 = bf16[4,128,256]{2,1,0:T(8,128)(2,1)S(1)} collective-permute-done((bf16[4,128,256]{2,1,0:T(8,128)(2,1)S(1)}, bf16[4,128,256]{2,1,0:T(8,128)(2,1)S(1)}, u32[]{:S(2)}, u32[]{:S(2)}) %collective-permute-start.11) | collective-permute-done | bytes 262176 | tf_op jit(solution)/shard_map/ppermute | solution.py:32
  92.9 0.0 collective-permute-done.9
  92.9 0.1 fusion.2
  93.1 1.5 %collective-permute-start.12 = (bf16[128,256]{1,0:T(8,128)(2,1)S(1)}, bf16[128,256]{1,0:T(8,128)(2,1)S(1)}, u32[]{:S(2)}, u32[]{:S(2)}) collective-permute-start(bf16[128,256]{1,0:T(8,128)(2,1)S(1)} %get-tuple-element.30), channel_id=1, source_target_pairs={{0,1},{1,16},{16,17},{17,0},{2,3},{3,18},{18,19},{19,2},{4,5},{5,2... | collective-permute-start | bytes 196616 | tf_op jit(solution)/shard_map/ppermute | solution.py:32
  94.6 1.0 %collective-permute-start.13 = (bf16[128,256]{1,0:T(8,128)(2,1)S(1)}, bf16[128,256]{1,0:T(8,128)(2,1)S(1)}, u32[]{:S(2)}, u32[]{:S(2)}) collective-permute-start(bf16[128,256]{1,0:T(8,128)(2,1)S(1)} %get-tuple-element.32), channel_id=1, source_target_pairs={{0,16},{1,17},{16,0},{17,1},{2,18},{3,19},{18,2},{19,3},{4,20},{5,... | collective-permute-start | bytes 196616 | tf_op jit(solution)/shard_map/ppermute | solution.py:32
  95.6 1.8 %collective-permute-start.14 = (bf16[128,256]{1,0:T(8,128)(2,1)S(1)}, bf16[128,256]{1,0:T(8,128)(2,1)S(1)}, u32[]{:S(2)}, u32[]{:S(2)}) collective-permute-start(bf16[128,256]{1,0:T(8,128)(2,1)S(1)} %get-tuple-element.31), channel_id=1, source_target_pairs={{0,17},{1,0},{16,1},{17,16},{2,19},{3,2},{18,3},{19,18},{4,21},{5,... | collective-permute-start | bytes 196616 | tf_op jit(solution)/shard_map/ppermute | solution.py:32
  97.4 0.0 all-to-all-done.2
  97.4 0.7 reduce_sum.12
  98.1 1.2 %collective-permute-done.12 = bf16[128,256]{1,0:T(8,128)(2,1)S(1)} collective-permute-done((bf16[128,256]{1,0:T(8,128)(2,1)S(1)}, bf16[128,256]{1,0:T(8,128)(2,1)S(1)}, u32[]{:S(2)}, u32[]{:S(2)}) %collective-permute-start.12) | collective-permute-done | bytes 65568 | tf_op jit(solution)/shard_map/ppermute | solution.py:32
  99.3 1.1 %collective-permute-done.13 = bf16[128,256]{1,0:T(8,128)(2,1)S(1)} collective-permute-done((bf16[128,256]{1,0:T(8,128)(2,1)S(1)}, bf16[128,256]{1,0:T(8,128)(2,1)S(1)}, u32[]{:S(2)}, u32[]{:S(2)}) %collective-permute-start.13) | collective-permute-done | bytes 65568 | tf_op jit(solution)/shard_map/ppermute | solution.py:32
  100.4 0.0 collective-permute-done.14
  100.4 0.6 fusion.9
  (11 shorter events, 0.2 us)
Async XLA Ops:
  2.6 7.5 %copy-start.1 = (bf16[128,512]{1,0:T(8,128)(2,1)S(1)}, bf16[128,512]{1,0:T(8,128)(2,1)}, u32[]{:S(2)}) copy-start(bf16[128,512]{1,0:T(8,128)(2,1)} %get-tuple-element.14.refs_0_) | copy-start | bytes 393220
  2.6 28.8 %copy-start.2 = (s32[16384]{0:T(1024)S(1)}, s32[16384]{0:T(1024)}, u32[]{:S(2)}) copy-start(s32[16384]{0:T(1024)} %param.9) | copy-start | bytes 196612
  2.6 28.8 %all-to-all-start = ((bf16[16,128,256]{2,1,0:T(8,128)(2,1)}), bf16[16,128,256]{2,1,0:T(8,128)(2,1)S(1)}, u32[]{:S(2)}, u32[]{:S(2)}) async-start(bf16[16,128,256]{2,1,0:T(8,128)(2,1)} %get-tuple-element.13), calls=%async_computation | async-start | bytes 2097152 | tf_op jit(solution)/shard_map/all_to_all | solution.py:251
  10.2 8.9 %collective-permute-start.3 = (bf16[128,512]{1,0:T(8,128)(2,1)S(1)}, bf16[128,512]{1,0:T(8,128)(2,1)S(1)}, u32[]{:S(2)}, u32[]{:S(2)}) collective-permute-start(bf16[128,512]{1,0:T(8,128)(2,1)S(1)} %copy-done.1), channel_id=1, source_target_pairs={{0,32},{32,64},{64,96},{96,128},{128,160},{160,192},{192,224},{224... | collective-permute-start | bytes 393224 | tf_op jit(solution)/shard_map/ppermute | solution.py:32
  12.2 6.9 %collective-permute-start = (bf16[128,512]{1,0:T(8,128)(2,1)S(1)}, bf16[128,512]{1,0:T(8,128)(2,1)S(1)}, u32[]{:S(2)}, u32[]{:S(2)}) collective-permute-start(bf16[128,512]{1,0:T(8,128)(2,1)S(1)} %copy-done.1), channel_id=1, source_target_pairs={{0,224},{32,0},{64,32},{96,64},{128,96},{160,128},{192,160},{224,1... | collective-permute-start | bytes 393224 | tf_op jit(solution)/shard_map/ppermute | solution.py:32
  19.0 6.2 %collective-permute-start.4 = (bf16[128,512]{1,0:T(8,128)(2,1)S(1)}, bf16[128,512]{1,0:T(8,128)(2,1)S(1)}, u32[]{:S(2)}, u32[]{:S(2)}) collective-permute-start(bf16[128,512]{1,0:T(8,128)(2,1)S(1)} %collective-permute-done.3.refs_1_), channel_id=1, source_target_pairs={{0,32},{32,64},{64,96},{96,128},{128,160},{160,192},{192,224},{224... | collective-permute-start | bytes 393224 | tf_op jit(solution)/shard_map/ppermute | solution.py:32
  19.1 6.2 %collective-permute-start.1 = (bf16[128,512]{1,0:T(8,128)(2,1)S(1)}, bf16[128,512]{1,0:T(8,128)(2,1)S(1)}, u32[]{:S(2)}, u32[]{:S(2)}) collective-permute-start(bf16[128,512]{1,0:T(8,128)(2,1)S(1)} %collective-permute-done.refs_2_), channel_id=1, source_target_pairs={{0,224},{32,0},{64,32},{96,64},{128,96},{160,128},{192,160},{224,1... | collective-permute-start | bytes 393224 | tf_op jit(solution)/shard_map/ppermute | solution.py:32
  25.2 6.2 %collective-permute-start.5 = (bf16[128,512]{1,0:T(8,128)(2,1)S(1)}, bf16[128,512]{1,0:T(8,128)(2,1)S(1)}, u32[]{:S(2)}, u32[]{:S(2)}) collective-permute-start(bf16[128,512]{1,0:T(8,128)(2,1)S(1)} %collective-permute-done.4.refs_3_), channel_id=1, source_target_pairs={{0,32},{32,64},{64,96},{96,128},{128,160},{160,192},{192,224},{224... | collective-permute-start | bytes 393224 | tf_op jit(solution)/shard_map/ppermute | solution.py:32
  25.2 6.2 %collective-permute-start.2 = (bf16[128,512]{1,0:T(8,128)(2,1)S(1)}, bf16[128,512]{1,0:T(8,128)(2,1)S(1)}, u32[]{:S(2)}, u32[]{:S(2)}) collective-permute-start(bf16[128,512]{1,0:T(8,128)(2,1)S(1)} %collective-permute-done.1.refs_4_), channel_id=1, source_target_pairs={{0,224},{32,0},{64,32},{96,64},{128,96},{160,128},{192,160},{224,1... | collective-permute-start | bytes 393224 | tf_op jit(solution)/shard_map/ppermute | solution.py:32
  31.4 7.8 %collective-permute-start.6 = (bf16[16,128,256]{2,1,0:T(8,128)(2,1)S(1)}, bf16[16,128,256]{2,1,0:T(8,128)(2,1)S(1)}, u32[]{:S(2)}, u32[]{:S(2)}) collective-permute-start(bf16[16,128,256]{2,1,0:T(8,128)(2,1)S(1)} %all-to-all-done.k_own), channel_id=1, source_target_pairs={{0,8},{8,0},{1,9},{9,1},{2,10},{10,2},{3,11},{11,3},{4,12},{12,4},... | collective-permute-start | bytes 3145736 | tf_op jit(solution)/shard_map/ppermute | solution.py:249
  31.7 7.5 %collective-permute-start.7 = (bf16[128,512]{1,0:T(8,128)(2,1)S(1)}, bf16[128,512]{1,0:T(8,128)(2,1)S(1)}, u32[]{:S(2)}, u32[]{:S(2)}) collective-permute-start(bf16[128,512]{1,0:T(8,128)(2,1)S(1)} %collective-permute-done.5.refs_5_), channel_id=1, source_target_pairs={{0,32},{32,64},{64,96},{96,128},{128,160},{160,192},{192,224},{224... | collective-permute-start | bytes 393224 | tf_op jit(solution)/shard_map/ppermute | solution.py:32
  71.0 0.8 copy-start
  71.8 3.5 %collective-permute-start.8 = (bf16[4,4,128,256]{3,2,1,0:T(8,128)(2,1)}, bf16[4,4,128,256]{3,2,1,0:T(8,128)(2,1)}, u32[]{:S(2)}, u32[]{:S(2)}) collective-permute-start(bf16[4,4,128,256]{3,2,1,0:T(8,128)(2,1)} %get-tuple-element.22), channel_id=1, source_target_pairs={{0,8},{8,0},{1,9},{9,1},{2,10},{10,2},{3,11},{11,3},{4,12},{12,4},... | collective-permute-start | bytes 3145736 | tf_op jit(solution)/shard_map/ppermute | solution.py:249
  71.8 25.6 %all-to-all-start.2 = ((bf16[8,128,256]{2,1,0:T(8,128)(2,1)}), bf16[8,128,256]{2,1,0:T(8,128)(2,1)S(1)}, u32[]{:S(2)}, u32[]{:S(2)}) async-start(bf16[8,128,256]{2,1,0:T(8,128)(2,1)} %copy-done), calls=%async_computation.2 | async-start | bytes 1048576 | tf_op jit(solution)/shard_map/all_to_all | solution.py:276
  76.9 10.7 %collective-permute-start.10 = (bf16[4,128,256]{2,1,0:T(8,128)(2,1)S(1)}, bf16[4,128,256]{2,1,0:T(8,128)(2,1)S(1)}, u32[]{:S(2)}, u32[]{:S(2)}) collective-permute-start(bf16[4,128,256]{2,1,0:T(8,128)(2,1)S(1)} %get-tuple-element.29), channel_id=1, source_target_pairs={{0,4},{2,6},{4,0},{6,2},{1,5},{3,7},{5,1},{7,3},{8,12},{10,14},{12... | collective-permute-start | bytes 786440 | tf_op jit(solution)/shard_map/ppermute | solution.py:32
  79.1 13.8 %collective-permute-start.11 = (bf16[4,128,256]{2,1,0:T(8,128)(2,1)S(1)}, bf16[4,128,256]{2,1,0:T(8,128)(2,1)S(1)}, u32[]{:S(2)}, u32[]{:S(2)}) collective-permute-start(bf16[4,128,256]{2,1,0:T(8,128)(2,1)S(1)} %get-tuple-element.28), channel_id=1, source_target_pairs={{0,6},{2,0},{4,2},{6,4},{1,7},{3,1},{5,3},{7,5},{8,14},{10,8},{12,... | collective-permute-start | bytes 786440 | tf_op jit(solution)/shard_map/ppermute | solution.py:32
  80.6 12.4 %collective-permute-start.9 = (bf16[4,128,256]{2,1,0:T(8,128)(2,1)S(1)}, bf16[4,128,256]{2,1,0:T(8,128)(2,1)S(1)}, u32[]{:S(2)}, u32[]{:S(2)}) collective-permute-start(bf16[4,128,256]{2,1,0:T(8,128)(2,1)S(1)} %get-tuple-element.27), channel_id=1, source_target_pairs={{0,2},{2,4},{4,6},{6,0},{1,3},{3,5},{5,7},{7,1},{8,10},{10,12},{12... | collective-permute-start | bytes 786440 | tf_op jit(solution)/shard_map/ppermute | solution.py:32
  93.1 6.3 %collective-permute-start.12 = (bf16[128,256]{1,0:T(8,128)(2,1)S(1)}, bf16[128,256]{1,0:T(8,128)(2,1)S(1)}, u32[]{:S(2)}, u32[]{:S(2)}) collective-permute-start(bf16[128,256]{1,0:T(8,128)(2,1)S(1)} %get-tuple-element.30), channel_id=1, source_target_pairs={{0,1},{1,16},{16,17},{17,0},{2,3},{3,18},{18,19},{19,2},{4,5},{5,2... | collective-permute-start | bytes 196616 | tf_op jit(solution)/shard_map/ppermute | solution.py:32
  94.6 5.8 %collective-permute-start.13 = (bf16[128,256]{1,0:T(8,128)(2,1)S(1)}, bf16[128,256]{1,0:T(8,128)(2,1)S(1)}, u32[]{:S(2)}, u32[]{:S(2)}) collective-permute-start(bf16[128,256]{1,0:T(8,128)(2,1)S(1)} %get-tuple-element.32), channel_id=1, source_target_pairs={{0,16},{1,17},{16,0},{17,1},{2,18},{3,19},{18,2},{19,3},{4,20},{5,... | collective-permute-start | bytes 196616 | tf_op jit(solution)/shard_map/ppermute | solution.py:32
  95.6 4.8 %collective-permute-start.14 = (bf16[128,256]{1,0:T(8,128)(2,1)S(1)}, bf16[128,256]{1,0:T(8,128)(2,1)S(1)}, u32[]{:S(2)}, u32[]{:S(2)}) collective-permute-start(bf16[128,256]{1,0:T(8,128)(2,1)S(1)} %get-tuple-element.31), channel_id=1, source_target_pairs={{0,17},{1,0},{16,1},{17,16},{2,19},{3,2},{18,3},{19,18},{4,21},{5,... | collective-permute-start | bytes 196616 | tf_op jit(solution)/shard_map/ppermute | solution.py:32

commit v6 on v5

--- a/solution.py
+++ b/solution.py
@@ -156,7 +156,7 @@
 
 
 def grad_kernel(ids, mm, hot, bias, k_own, k_other, *refs):
-    st_ref, qs, dq_ref, own_ref, other_ref, lse, delta, dq_acc, dkv_acc = refs
+    st_ref, qs, other_ref, own_ref, dq_ref, lse, delta, dq_acc, dkv_acc = refs
     parts = st_ref[:, :, 0:1, :]
     high = jnp.max(parts, axis=0)
     shares = jnp.exp2(parts - high[None])
@@ -220,6 +220,12 @@
                 ref[y, x] = dkv_acc[slot, at : at + CH, :].astype(bf16)
 
 
+def add_kernel(ids, own_ref, other_ref, *outs):
+    for k, out in enumerate(outs):
+        at = (ids[1] + k) % NY
+        out[...] = (own_ref[at].astype(f32) + other_ref[at].astype(f32)).astype(bf16)
+
+
 SMEM = pl.BlockSpec(memory_space=pltpu.SMEM)
 VMEM = pl.BlockSpec(memory_space=pltpu.VMEM)
 DATA = VMEM
@@ -271,11 +277,12 @@
     keys = (ids, mm, hot, bias, k_own, k_other)
     stats = jnp.broadcast_to(stats[None], (NZ,) + stats.shape)
     stats = lax.all_to_all(stats, "z", 0, 0)
-    dq, own, other = grad_call(keys, stats, queries)
+    other, own, dq = grad_call(keys, stats, queries)
 
     dq = lax.all_to_all(dq, "z", 0, 0)
-    pair = (own.astype(f32) + swap(other).astype(f32)).astype(bf16)
-    pair = scatter(pair, y, "y", NY)
+    parts = add_call(ids, own, swap(other))
+    got = [parts[0]] + [shift(t, "y", NY, k) for k, t in enumerate(parts) if k]
+    pair = sum(g.astype(f32) for g in got).astype(bf16)
     pair = scatter(pair, xh * NXL + xl, XAX, NX)
     dq = jnp.sum(dq.astype(f32), axis=0).astype(bf16)
     return dq, pair[:, :HD], pair[:, HD:]
@@ -307,9 +314,9 @@
     return pl.pallas_call(
         grad_kernel,
         out_shape=(
-            jax.ShapeDtypeStruct((NZ, CH, 2 * HD), bf16),
             jax.ShapeDtypeStruct((NY, NX, CH, 2 * HD), bf16),
             jax.ShapeDtypeStruct((NY, NX, CH, 2 * HD), bf16),
+            jax.ShapeDtypeStruct((NZ, CH, 2 * HD), bf16),
         ),
         in_specs=KEY_SPECS + [VMEM] * 2,
         out_specs=(VMEM,) * 3,
@@ -323,6 +330,16 @@
     )(*keys, stats, queries)
 
 
+def add_call(ids, own, other):
+    return pl.pallas_call(
+        add_kernel,
+        out_shape=[jax.ShapeDtypeStruct((NX, CH, 2 * HD), bf16)] * NY,
+        in_specs=[SMEM] + [VMEM] * 2,
+        out_specs=[VMEM] * NY,
+        compiler_params=pltpu.CompilerParams(vmem_limit_bytes=BIG),
+    )(ids, own, other)
+
+
 def solution(mesh):
     fine = Mesh(mesh.devices.reshape(NZ, NXH, NCORE, NY, NXL), ROWS + COLS)
     by_row = P(ROWS + COLS, None)

time: 101 us -> 101 us (level)
    convert_element_type x1, other arithmetic: 1.53 us -> 0.13 us  [per_device(): pair = sum((g.astype(f32) for g in got)).astype(bf16)]
    reduce_sum x1, other arithmetic: 0.7 us -> 1.76 us  [per_device(): dq = jnp.sum(dq.astype(f32), axis=0).astype(bf16)]
    pallas_call x1 -> x2, Pallas kernels: 11.3 us -> 12.1 us  [the longest x1 11.3 us: grad_call(): pl.pallas_call(grad_kernel, out_shape=(jax.ShapeDtypeStruct((NY, NX, CH,...]
  transfers between devices with their start and end apart: 17 -> 17, of which waited for: 8 -> 8; matrix products, arithmetic and copies ran while one was open for 3% -> 2% of each run, Pallas kernels for 0% -> 1%
where the time goes in v6:
time: 101 us
  starting transfers between devices  32.9 us (33%)
  waiting for transfers between devices  28.7 us (28%)
  Pallas kernels  19.8 us (20%)
  blocking collectives  14.7 us (15%)
  local copies, waits for them, and re-layouts  2.09 us (2%)
  other arithmetic  1.95 us (2%)
    ppermute x13, waiting for transfers between devices, shift(): return lax.ppermute(x, axis, [(i, (i + by) % size) for i in range(size)])  28.7 us
    ppermute x13, starting transfers between devices, shift(): return lax.ppermute(x, axis, [(i, (i + by) % size) for i in range(size)])  21.2 us
    all_to_all x1, blocking collectives, per_device(): stats = lax.all_to_all(stats, 'z', 0, 0)  14.7 us
    pallas_call x1, Pallas kernels, grad_call(): pl.pallas_call(grad_kernel, out_shape=(jax.ShapeDtypeStruct((NY, NX, CH,...  11.3 us
    all_to_all x1, starting transfers between devices, per_device(): k_own = lax.all_to_all(kv, ('y',) + XAX, 0, 0)  7.52 us
    pallas_call x1, Pallas kernels, stats_call(): pl.pallas_call(stats_kernel, out_shape=(jax.ShapeDtypeStruct((NZ, 2, 2 *...  5.7 us
    all_to_all x1, starting transfers between devices, per_device(): dq = lax.all_to_all(dq, 'z', 0, 0)  4.13 us
  transfers between devices with their start and end apart: 17, of which 8 were waited for; matrix products, arithmetic and copies ran while one was open for 2% of the time, Pallas kernels for 1%

profile of v6, /device:TPU:8, one launch (start us, length us, event | category | flops | bytes accessed | tf_op | source)
XLA Modules:
  0.0 101.0 jit_solution(4651145053598940002)
XLA Ops:
  0.6 2.0 %shard_map.76 = (bf16[128,512]{1,0:T(8,128)(2,1)}, bf16[16,128,256]{2,1,0:T(8,128)(2,1)}) custom-call(bf16[128,256]{1,0:T(8,128)(2,1)} %q_ref.1, bf16[128,256]{1,0:T(8,128)(2,1)} %o_ref.1, bf16[128,128]{1,0:T(8,128)(2,1)} %k_ref.1, bf16[128,128]{1,0:T(8,128)(2,1)} %v_ref.1), custom_call_target="tpu_custom_call" | custom-call | tf_op jit(solution)/shard_map/pallas_call | solution.py:244
  2.6 0.0 copy-start.1
  2.6 0.0 copy-start.2
  2.6 7.5 %all-to-all-start = ((bf16[16,128,256]{2,1,0:T(8,128)(2,1)}), bf16[16,128,256]{2,1,0:T(8,128)(2,1)S(1)}, u32[]{:S(2)}, u32[]{:S(2)}) async-start(bf16[16,128,256]{2,1,0:T(8,128)(2,1)} %get-tuple-element.17), calls=%async_computation | async-start | bytes 2097152 | tf_op jit(solution)/shard_map/all_to_all | solution.py:257
  10.2 0.0 copy-done.1
  10.2 2.0 %collective-permute-start.3 = (bf16[128,512]{1,0:T(8,128)(2,1)S(1)}, bf16[128,512]{1,0:T(8,128)(2,1)S(1)}, u32[]{:S(2)}, u32[]{:S(2)}) collective-permute-start(bf16[128,512]{1,0:T(8,128)(2,1)S(1)} %copy-done.1), channel_id=1, source_target_pairs={{0,32},{32,64},{64,96},{96,128},{128,160},{160,192},{192,224},{224... | collective-permute-start | bytes 393224 | tf_op jit(solution)/shard_map/ppermute | solution.py:32
  12.2 4.0 %collective-permute-start = (bf16[128,512]{1,0:T(8,128)(2,1)S(1)}, bf16[128,512]{1,0:T(8,128)(2,1)S(1)}, u32[]{:S(2)}, u32[]{:S(2)}) collective-permute-start(bf16[128,512]{1,0:T(8,128)(2,1)S(1)} %copy-done.1), channel_id=1, source_target_pairs={{0,224},{32,0},{64,32},{96,64},{128,96},{160,128},{192,160},{224,1... | collective-permute-start | bytes 393224 | tf_op jit(solution)/shard_map/ppermute | solution.py:32
  16.2 2.9 %collective-permute-done.3.refs_1_ = bf16[128,512]{1,0:T(8,128)(2,1)S(1)} collective-permute-done((bf16[128,512]{1,0:T(8,128)(2,1)S(1)}, bf16[128,512]{1,0:T(8,128)(2,1)S(1)}, u32[]{:S(2)}, u32[]{:S(2)}) %collective-permute-start.3) | collective-permute-done | bytes 131104 | tf_op jit(solution)/shard_map/ppermute | solution.py:32
  19.0 0.0 collective-permute-start.4
  19.1 0.0 collective-permute-done.refs_2_
  19.1 3.3 %collective-permute-start.1 = (bf16[128,512]{1,0:T(8,128)(2,1)S(1)}, bf16[128,512]{1,0:T(8,128)(2,1)S(1)}, u32[]{:S(2)}, u32[]{:S(2)}) collective-permute-start(bf16[128,512]{1,0:T(8,128)(2,1)S(1)} %collective-permute-done.refs_2_), channel_id=1, source_target_pairs={{0,224},{32,0},{64,32},{96,64},{128,96},{160,128},{192,160},{224,1... | collective-permute-start | bytes 393224 | tf_op jit(solution)/shard_map/ppermute | solution.py:32
  22.4 2.9 %collective-permute-done.4.refs_3_ = bf16[128,512]{1,0:T(8,128)(2,1)S(1)} collective-permute-done((bf16[128,512]{1,0:T(8,128)(2,1)S(1)}, bf16[128,512]{1,0:T(8,128)(2,1)S(1)}, u32[]{:S(2)}, u32[]{:S(2)}) %collective-permute-start.4) | collective-permute-done | bytes 131104 | tf_op jit(solution)/shard_map/ppermute | solution.py:32
  25.2 0.0 collective-permute-start.5
  25.2 0.0 collective-permute-done.1.refs_4_
  25.2 3.3 %collective-permute-start.2 = (bf16[128,512]{1,0:T(8,128)(2,1)S(1)}, bf16[128,512]{1,0:T(8,128)(2,1)S(1)}, u32[]{:S(2)}, u32[]{:S(2)}) collective-permute-start(bf16[128,512]{1,0:T(8,128)(2,1)S(1)} %collective-permute-done.1.refs_4_), channel_id=1, source_target_pairs={{0,224},{32,0},{64,32},{96,64},{128,96},{160,128},{192,160},{224,1... | collective-permute-start | bytes 393224 | tf_op jit(solution)/shard_map/ppermute | solution.py:32
  28.5 2.9 %collective-permute-done.5.refs_5_ = bf16[128,512]{1,0:T(8,128)(2,1)S(1)} collective-permute-done((bf16[128,512]{1,0:T(8,128)(2,1)S(1)}, bf16[128,512]{1,0:T(8,128)(2,1)S(1)}, u32[]{:S(2)}, u32[]{:S(2)}) %collective-permute-start.5) | collective-permute-done | bytes 131104 | tf_op jit(solution)/shard_map/ppermute | solution.py:32
  31.4 0.0 collective-permute-done.2.refs_6_
  31.4 0.0 all-to-all-done.k_own
  31.4 0.0 collective-permute-start.6
  31.4 0.0 copy-done.2
  31.5 0.2 slice_reduce_fusion.1
  31.7 0.1 collective-permute-start.7
  31.8 0.1 stack.26.ids
  31.9 0.3 dynamic-slice_reduce_fusion.1
  32.2 7.0 %collective-permute-done.7.refs_7_ = bf16[128,512]{1,0:T(8,128)(2,1)S(1)} collective-permute-done((bf16[128,512]{1,0:T(8,128)(2,1)S(1)}, bf16[128,512]{1,0:T(8,128)(2,1)S(1)}, u32[]{:S(2)}, u32[]{:S(2)}) %collective-permute-start.7) | collective-permute-done | bytes 131104 | tf_op jit(solution)/shard_map/ppermute | solution.py:32
  39.2 0.0 collective-permute-done.6.k_other
  39.2 5.7 %shard_map.77 = (f32[8,2,256]{2,1,0:T(2,128)S(1)}, bf16[8,128,512]{2,1,0:T(8,128)(2,1)S(1)}, bf16[8,512,128]{2,1,0:T(8,128)(2,1)S(1)}, bf16[8,128,128]{2,1,0:T(8,128)(2,1)S(1)}) custom-call(s32[5]{0:T(128)S(1)} %stack.26.ids, s32[4,4]{1,0:T(4,128)S(1)} %pad_add_fusion.mm, s32[4,1,128]{2,1,0:T(1,128)S(1)} %constant_dynamic-slice_fusion.1.qid_ref, ...), custom_call_target="tpu_custom_call" | custom-call | tf_op jit(solution)/shard_map/pallas_call | solution.py:303
  45.0 14.7 %all_to_all.15.refs_0_ = f32[8,8,2,256]{3,2,1,0:T(2,128)S(1)} all-to-all(f32[8,8,2,256]{3,2,1,0:T(2,128)S(1)} %broadcast_in_dim.2), channel_id=1, replica_groups=mesh['z'=8,'xh'=2,'core'=2,'y'=4,'xl'=2] {'z'}, dimensions={0} | all-to-all | bytes 262144 | tf_op jit(solution)/shard_map/all_to_all | solution.py:279
  59.7 11.3 %shard_map.78 = (bf16[4,4,128,256]{3,2,1,0:T(8,128)(2,1)}, bf16[4,4,128,256]{3,2,1,0:T(8,128)(2,1)S(1)}, bf16[8,128,256]{2,1,0:T(8,128)(2,1)S(1)}) custom-call(s32[5]{0:T(128)S(1)} %stack.26.ids, s32[4,4]{1,0:T(4,128)S(1)} %pad_add_fusion.mm, bf16[8,512,128]{2,1,0:T(8,128)(2,1)S(1)} %get-tuple-element.20.hot, ...), custom_call_target="tpu_custom_call" | custom-call | tf_op jit(solution)/shard_map/pallas_call | solution.py:314
  71.0 0.0 copy-start
  71.0 0.8 copy-done
  71.8 0.1 collective-permute-start.8
  71.9 4.1 %all-to-all-start.2 = ((bf16[8,128,256]{2,1,0:T(8,128)(2,1)}), bf16[8,128,256]{2,1,0:T(8,128)(2,1)}, u32[]{:S(2)}, u32[]{:S(2)}) async-start(bf16[8,128,256]{2,1,0:T(8,128)(2,1)} %copy-done), calls=%async_computation.2 | async-start | bytes 1048576 | tf_op jit(solution)/shard_map/all_to_all | solution.py:282
  76.0 0.0 collective-permute-done.8.other_ref
  76.0 0.8 shard_map.79
  76.8 2.1 %collective-permute-start.10 = (bf16[4,128,256]{2,1,0:T(8,128)(2,1)S(1)}, bf16[4,128,256]{2,1,0:T(8,128)(2,1)S(1)}, u32[]{:S(2)}, u32[]{:S(2)}) collective-permute-start(bf16[4,128,256]{2,1,0:T(8,128)(2,1)S(1)} %get-tuple-element.29), channel_id=1, source_target_pairs={{0,4},{2,6},{4,0},{6,2},{1,5},{3,7},{5,1},{7,3},{8,12},{10,14},{12... | collective-permute-start | bytes 786440 | tf_op jit(solution)/shard_map/ppermute | solution.py:32
  78.9 1.5 %collective-permute-start.11 = (bf16[4,128,256]{2,1,0:T(8,128)(2,1)S(1)}, bf16[4,128,256]{2,1,0:T(8,128)(2,1)S(1)}, u32[]{:S(2)}, u32[]{:S(2)}) collective-permute-start(bf16[4,128,256]{2,1,0:T(8,128)(2,1)S(1)} %get-tuple-element.30), channel_id=1, source_target_pairs={{0,6},{2,0},{4,2},{6,4},{1,7},{3,1},{5,3},{7,5},{8,14},{10,8},{12,... | collective-permute-start | bytes 786440 | tf_op jit(solution)/shard_map/ppermute | solution.py:32
  80.4 0.6 collective-permute-start.9
  80.9 6.6 %collective-permute-done.10 = bf16[4,128,256]{2,1,0:T(8,128)(2,1)S(1)} collective-permute-done((bf16[4,128,256]{2,1,0:T(8,128)(2,1)S(1)}, bf16[4,128,256]{2,1,0:T(8,128)(2,1)S(1)}, u32[]{:S(2)}, u32[]{:S(2)}) %collective-permute-start.10) | collective-permute-done | bytes 262176 | tf_op jit(solution)/shard_map/ppermute | solution.py:32
  87.6 5.1 %collective-permute-done.11 = bf16[4,128,256]{2,1,0:T(8,128)(2,1)S(1)} collective-permute-done((bf16[4,128,256]{2,1,0:T(8,128)(2,1)S(1)}, bf16[4,128,256]{2,1,0:T(8,128)(2,1)S(1)}, u32[]{:S(2)}, u32[]{:S(2)}) %collective-permute-start.11) | collective-permute-done | bytes 262176 | tf_op jit(solution)/shard_map/ppermute | solution.py:32
  92.7 0.0 collective-permute-done.9
  92.7 0.1 add_convert_fusion
  92.9 1.5 %collective-permute-start.12 = (bf16[128,256]{1,0:T(8,128)(2,1)S(1)}, bf16[128,256]{1,0:T(8,128)(2,1)S(1)}, u32[]{:S(2)}, u32[]{:S(2)}) collective-permute-start(bf16[128,256]{1,0:T(8,128)(2,1)S(1)} %get-tuple-element.35), channel_id=1, source_target_pairs={{0,1},{1,16},{16,17},{17,0},{2,3},{3,18},{18,19},{19,2},{4,5},{5,2... | collective-permute-start | bytes 196616 | tf_op jit(solution)/shard_map/ppermute | solution.py:32
  94.4 1.1 %collective-permute-start.13 = (bf16[128,256]{1,0:T(8,128)(2,1)S(1)}, bf16[128,256]{1,0:T(8,128)(2,1)S(1)}, u32[]{:S(2)}, u32[]{:S(2)}) collective-permute-start(bf16[128,256]{1,0:T(8,128)(2,1)S(1)} %get-tuple-element.37), channel_id=1, source_target_pairs={{0,16},{1,17},{16,0},{17,1},{2,18},{3,19},{18,2},{19,3},{4,20},{5,... | collective-permute-start | bytes 196616 | tf_op jit(solution)/shard_map/ppermute | solution.py:32
  95.5 1.7 %collective-permute-start.14 = (bf16[128,256]{1,0:T(8,128)(2,1)S(1)}, bf16[128,256]{1,0:T(8,128)(2,1)S(1)}, u32[]{:S(2)}, u32[]{:S(2)}) collective-permute-start(bf16[128,256]{1,0:T(8,128)(2,1)S(1)} %get-tuple-element.36), channel_id=1, source_target_pairs={{0,17},{1,0},{16,1},{17,16},{2,19},{3,2},{18,3},{19,18},{4,21},{5,... | collective-permute-start | bytes 196616 | tf_op jit(solution)/shard_map/ppermute | solution.py:32
  97.2 0.0 all-to-all-done.2
  97.2 1.8 %reduce_sum.12 = bf16[128,256]{1,0:T(8,128)(2,1)} reduce(bf16[8,128,256]{2,1,0:T(8,128)(2,1)} %all-to-all-done.2, bf16[]{:T(256)} %constant.65.clone.1), dimensions={0}, to_apply=%region_0.1 | reduce | flops 229376 | bytes 589826 | tf_op jit(solution)/shard_map/reduce_sum | solution.py:287
  99.0 0.0 collective-permute-done.12
  99.0 1.2 %collective-permute-done.13 = bf16[128,256]{1,0:T(8,128)(2,1)S(1)} collective-permute-done((bf16[128,256]{1,0:T(8,128)(2,1)S(1)}, bf16[128,256]{1,0:T(8,128)(2,1)S(1)}, u32[]{:S(2)}, u32[]{:S(2)}) %collective-permute-start.13) | collective-permute-done | bytes 65568 | tf_op jit(solution)/shard_map/ppermute | solution.py:32
  100.2 0.1 collective-permute-done.14
  100.3 0.6 fusion.4
  (11 shorter events, 0.2 us)
Async XLA Ops:
  2.6 7.5 %copy-start.1 = (bf16[128,512]{1,0:T(8,128)(2,1)S(1)}, bf16[128,512]{1,0:T(8,128)(2,1)}, u32[]{:S(2)}) copy-start(bf16[128,512]{1,0:T(8,128)(2,1)} %get-tuple-element.18.refs_0_) | copy-start | bytes 393220
  2.6 28.8 %copy-start.2 = (s32[16384]{0:T(1024)S(1)}, s32[16384]{0:T(1024)}, u32[]{:S(2)}) copy-start(s32[16384]{0:T(1024)} %param.9) | copy-start | bytes 196612
  2.6 28.8 %all-to-all-start = ((bf16[16,128,256]{2,1,0:T(8,128)(2,1)}), bf16[16,128,256]{2,1,0:T(8,128)(2,1)S(1)}, u32[]{:S(2)}, u32[]{:S(2)}) async-start(bf16[16,128,256]{2,1,0:T(8,128)(2,1)} %get-tuple-element.17), calls=%async_computation | async-start | bytes 2097152 | tf_op jit(solution)/shard_map/all_to_all | solution.py:257
  10.2 8.9 %collective-permute-start.3 = (bf16[128,512]{1,0:T(8,128)(2,1)S(1)}, bf16[128,512]{1,0:T(8,128)(2,1)S(1)}, u32[]{:S(2)}, u32[]{:S(2)}) collective-permute-start(bf16[128,512]{1,0:T(8,128)(2,1)S(1)} %copy-done.1), channel_id=1, source_target_pairs={{0,32},{32,64},{64,96},{96,128},{128,160},{160,192},{192,224},{224... | collective-permute-start | bytes 393224 | tf_op jit(solution)/shard_map/ppermute | solution.py:32
  12.2 6.9 %collective-permute-start = (bf16[128,512]{1,0:T(8,128)(2,1)S(1)}, bf16[128,512]{1,0:T(8,128)(2,1)S(1)}, u32[]{:S(2)}, u32[]{:S(2)}) collective-permute-start(bf16[128,512]{1,0:T(8,128)(2,1)S(1)} %copy-done.1), channel_id=1, source_target_pairs={{0,224},{32,0},{64,32},{96,64},{128,96},{160,128},{192,160},{224,1... | collective-permute-start | bytes 393224 | tf_op jit(solution)/shard_map/ppermute | solution.py:32
  19.0 6.2 %collective-permute-start.4 = (bf16[128,512]{1,0:T(8,128)(2,1)S(1)}, bf16[128,512]{1,0:T(8,128)(2,1)S(1)}, u32[]{:S(2)}, u32[]{:S(2)}) collective-permute-start(bf16[128,512]{1,0:T(8,128)(2,1)S(1)} %collective-permute-done.3.refs_1_), channel_id=1, source_target_pairs={{0,32},{32,64},{64,96},{96,128},{128,160},{160,192},{192,224},{224... | collective-permute-start | bytes 393224 | tf_op jit(solution)/shard_map/ppermute | solution.py:32
  19.1 6.2 %collective-permute-start.1 = (bf16[128,512]{1,0:T(8,128)(2,1)S(1)}, bf16[128,512]{1,0:T(8,128)(2,1)S(1)}, u32[]{:S(2)}, u32[]{:S(2)}) collective-permute-start(bf16[128,512]{1,0:T(8,128)(2,1)S(1)} %collective-permute-done.refs_2_), channel_id=1, source_target_pairs={{0,224},{32,0},{64,32},{96,64},{128,96},{160,128},{192,160},{224,1... | collective-permute-start | bytes 393224 | tf_op jit(solution)/shard_map/ppermute | solution.py:32
  25.2 6.2 %collective-permute-start.5 = (bf16[128,512]{1,0:T(8,128)(2,1)S(1)}, bf16[128,512]{1,0:T(8,128)(2,1)S(1)}, u32[]{:S(2)}, u32[]{:S(2)}) collective-permute-start(bf16[128,512]{1,0:T(8,128)(2,1)S(1)} %collective-permute-done.4.refs_3_), channel_id=1, source_target_pairs={{0,32},{32,64},{64,96},{96,128},{128,160},{160,192},{192,224},{224... | collective-permute-start | bytes 393224 | tf_op jit(solution)/shard_map/ppermute | solution.py:32
  25.2 6.2 %collective-permute-start.2 = (bf16[128,512]{1,0:T(8,128)(2,1)S(1)}, bf16[128,512]{1,0:T(8,128)(2,1)S(1)}, u32[]{:S(2)}, u32[]{:S(2)}) collective-permute-start(bf16[128,512]{1,0:T(8,128)(2,1)S(1)} %collective-permute-done.1.refs_4_), channel_id=1, source_target_pairs={{0,224},{32,0},{64,32},{96,64},{128,96},{160,128},{192,160},{224,1... | collective-permute-start | bytes 393224 | tf_op jit(solution)/shard_map/ppermute | solution.py:32
  31.4 7.8 %collective-permute-start.6 = (bf16[16,128,256]{2,1,0:T(8,128)(2,1)S(1)}, bf16[16,128,256]{2,1,0:T(8,128)(2,1)S(1)}, u32[]{:S(2)}, u32[]{:S(2)}) collective-permute-start(bf16[16,128,256]{2,1,0:T(8,128)(2,1)S(1)} %all-to-all-done.k_own), channel_id=1, source_target_pairs={{0,8},{8,0},{1,9},{9,1},{2,10},{10,2},{3,11},{11,3},{4,12},{12,4},... | collective-permute-start | bytes 3145736 | tf_op jit(solution)/shard_map/ppermute | solution.py:255
  31.7 7.5 %collective-permute-start.7 = (bf16[128,512]{1,0:T(8,128)(2,1)S(1)}, bf16[128,512]{1,0:T(8,128)(2,1)S(1)}, u32[]{:S(2)}, u32[]{:S(2)}) collective-permute-start(bf16[128,512]{1,0:T(8,128)(2,1)S(1)} %collective-permute-done.5.refs_5_), channel_id=1, source_target_pairs={{0,32},{32,64},{64,96},{96,128},{128,160},{160,192},{192,224},{224... | collective-permute-start | bytes 393224 | tf_op jit(solution)/shard_map/ppermute | solution.py:32
  71.0 0.8 copy-start
  71.8 4.2 %collective-permute-start.8 = (bf16[4,4,128,256]{3,2,1,0:T(8,128)(2,1)}, bf16[4,4,128,256]{3,2,1,0:T(8,128)(2,1)S(1)}, u32[]{:S(2)}, u32[]{:S(2)}) collective-permute-start(bf16[4,4,128,256]{3,2,1,0:T(8,128)(2,1)} %get-tuple-element.26), channel_id=1, source_target_pairs={{0,8},{8,0},{1,9},{9,1},{2,10},{10,2},{3,11},{11,3},{4,12},{12,4},... | collective-permute-start | bytes 3145736 | tf_op jit(solution)/shard_map/ppermute | solution.py:255
  71.9 25.4 %all-to-all-start.2 = ((bf16[8,128,256]{2,1,0:T(8,128)(2,1)}), bf16[8,128,256]{2,1,0:T(8,128)(2,1)}, u32[]{:S(2)}, u32[]{:S(2)}) async-start(bf16[8,128,256]{2,1,0:T(8,128)(2,1)} %copy-done), calls=%async_computation.2 | async-start | bytes 1048576 | tf_op jit(solution)/shard_map/all_to_all | solution.py:282
  76.8 10.7 %collective-permute-start.10 = (bf16[4,128,256]{2,1,0:T(8,128)(2,1)S(1)}, bf16[4,128,256]{2,1,0:T(8,128)(2,1)S(1)}, u32[]{:S(2)}, u32[]{:S(2)}) collective-permute-start(bf16[4,128,256]{2,1,0:T(8,128)(2,1)S(1)} %get-tuple-element.29), channel_id=1, source_target_pairs={{0,4},{2,6},{4,0},{6,2},{1,5},{3,7},{5,1},{7,3},{8,12},{10,14},{12... | collective-permute-start | bytes 786440 | tf_op jit(solution)/shard_map/ppermute | solution.py:32
  78.9 13.8 %collective-permute-start.11 = (bf16[4,128,256]{2,1,0:T(8,128)(2,1)S(1)}, bf16[4,128,256]{2,1,0:T(8,128)(2,1)S(1)}, u32[]{:S(2)}, u32[]{:S(2)}) collective-permute-start(bf16[4,128,256]{2,1,0:T(8,128)(2,1)S(1)} %get-tuple-element.30), channel_id=1, source_target_pairs={{0,6},{2,0},{4,2},{6,4},{1,7},{3,1},{5,3},{7,5},{8,14},{10,8},{12,... | collective-permute-start | bytes 786440 | tf_op jit(solution)/shard_map/ppermute | solution.py:32
  80.4 12.4 %collective-permute-start.9 = (bf16[4,128,256]{2,1,0:T(8,128)(2,1)S(1)}, bf16[4,128,256]{2,1,0:T(8,128)(2,1)S(1)}, u32[]{:S(2)}, u32[]{:S(2)}) collective-permute-start(bf16[4,128,256]{2,1,0:T(8,128)(2,1)S(1)} %get-tuple-element.28), channel_id=1, source_target_pairs={{0,2},{2,4},{4,6},{6,0},{1,3},{3,5},{5,7},{7,1},{8,10},{10,12},{12... | collective-permute-start | bytes 786440 | tf_op jit(solution)/shard_map/ppermute | solution.py:32
  92.9 6.1 %collective-permute-start.12 = (bf16[128,256]{1,0:T(8,128)(2,1)S(1)}, bf16[128,256]{1,0:T(8,128)(2,1)S(1)}, u32[]{:S(2)}, u32[]{:S(2)}) collective-permute-start(bf16[128,256]{1,0:T(8,128)(2,1)S(1)} %get-tuple-element.35), channel_id=1, source_target_pairs={{0,1},{1,16},{16,17},{17,0},{2,3},{3,18},{18,19},{19,2},{4,5},{5,2... | collective-permute-start | bytes 196616 | tf_op jit(solution)/shard_map/ppermute | solution.py:32
  94.4 5.8 %collective-permute-start.13 = (bf16[128,256]{1,0:T(8,128)(2,1)S(1)}, bf16[128,256]{1,0:T(8,128)(2,1)S(1)}, u32[]{:S(2)}, u32[]{:S(2)}) collective-permute-start(bf16[128,256]{1,0:T(8,128)(2,1)S(1)} %get-tuple-element.37), channel_id=1, source_target_pairs={{0,16},{1,17},{16,0},{17,1},{2,18},{3,19},{18,2},{19,3},{4,20},{5,... | collective-permute-start | bytes 196616 | tf_op jit(solution)/shard_map/ppermute | solution.py:32
  95.5 4.8 %collective-permute-start.14 = (bf16[128,256]{1,0:T(8,128)(2,1)S(1)}, bf16[128,256]{1,0:T(8,128)(2,1)S(1)}, u32[]{:S(2)}, u32[]{:S(2)}) collective-permute-start(bf16[128,256]{1,0:T(8,128)(2,1)S(1)} %get-tuple-element.36), channel_id=1, source_target_pairs={{0,17},{1,0},{16,1},{17,16},{2,19},{3,2},{18,3},{19,18},{4,21},{5,... | collective-permute-start | bytes 196616 | tf_op jit(solution)/shard_map/ppermute | solution.py:32
